TPU v7x, 32 devices: a whole 2x2x4 slice. The times are simulated.
32 devices in a mesh: dp: 4 (over y, x), seq: 8 (over z, core).
Axes of the slice: x: 2, y: 2, z: 4, core: 2. Of those that a mesh axis runs over, the one named last changes fastest.
Arguments:
- inputs: bfloat16 [4, 2048, 1024], P('dp', 'seq'), may hold values from -6 to 6
- encoder_states: bfloat16 [4, 1024, 1024], P('dp', 'seq'), may hold values from -6 to 6
- segment_ids: int32 [4, 2048], P('dp'), may hold values from 0 to 3, never falling along the last dimension, each value on 1 to 1024 neighbouring positions
- encoder_ids: int32 [4, 1024], P('dp'), may hold values from 0 to 3, never falling along the last dimension, each value on 1 to 512 neighbouring positions
- norm_gains: bfloat16 [3, 1024], replicated, may hold values from 0.5 to 1.5
- norm_shifts: bfloat16 [3, 1024], replicated, may hold values from -1 to 1
- attend_weights: bfloat16 [1024, 3072], P('dp', 'seq'), may hold values from -0.1875 to 0.1875
- attend_output: bfloat16 [1024, 1024], P('seq', 'dp'), may hold values from -3 to 3
- attend_biases: bfloat16 [3, 1024], replicated, may hold values from -0.29882812 to 0.29882812
- cross_query: bfloat16 [1024, 1024], P('dp', 'seq'), may hold values from -0.1875 to 0.1875
- cross_memory: bfloat16 [1024, 2048], P('dp', 'seq'), may hold values from -0.1875 to 0.1875
- cross_output: bfloat16 [1024, 1024], P('seq', 'dp'), may hold values from -3 to 3
- cross_biases: bfloat16 [3, 1024], replicated, may hold values from -0.29882812 to 0.29882812
- expand_weight: bfloat16 [1024, 8192], P('dp', 'seq'), may hold values from -0.1875 to 0.1875
- expand_bias: bfloat16 [8192], replicated, may hold values from -3 to 3
- shrink_weight: bfloat16 [8192, 1024], P('seq', 'dp'), may hold values from -0.0625 to 0.0625
- shrink_bias: bfloat16 [1024], replicated, may hold values from -1 to 1
- output_cotangent: bfloat16 [4, 2048, 1024], P('dp', 'seq'), may hold values from -6 to 6
Outputs:
- layer_output: bfloat16 [4, 2048, 1024], P('dp', 'seq')
- input_gradient: bfloat16 [4, 2048, 1024], P('dp', 'seq')
- encoder_gradient: bfloat16 [4, 1024, 1024], P('dp', 'seq')
- norm_gains_grad: float32 [3, 1024], replicated
- norm_shifts_grad: float32 [3, 1024], replicated
- attend_weights_grad: float32 [1024, 3072], P('dp', 'seq')
- attend_output_grad: float32 [1024, 1024], P('seq', 'dp')
- attend_biases_grad: float32 [3, 1024], replicated
- cross_query_grad: float32 [1024, 1024], P('dp', 'seq')
- cross_memory_grad: float32 [1024, 2048], P('dp', 'seq')
- cross_output_grad: float32 [1024, 1024], P('seq', 'dp')
- cross_biases_grad: float32 [3, 1024], replicated
- expand_weight_grad: float32 [1024, 8192], P('dp', 'seq')
- expand_bias_grad: float32 [8192], replicated
- shrink_weight_grad: float32 [8192, 1024], P('seq', 'dp')
- shrink_bias_grad: float32 [1024], replicated
Inputs may be any that keep to these rules, and one draw needn't show every extreme that they name: `segment_ids`: in each pack the document numbers never fall; every document 0 to 3 holds 1 to 1024 tokens, and one holds exactly 1024. `encoder_ids`: in each pack the document numbers never fall; every document 0 to 3 has 1 to 512 encoder states, and one has exactly 512.
All inputs are finite; a program needn't handle non-finite values.
Results may differ from a plain program's by a relative error of at most 0.024.
Values may be sent and summed in bfloat16 or wider, within the bound.
No kernel may reach another device: no remote copies, remote signals or barrier semaphores. Data moves between devices by JAX's collectives and lax.ppermute only.
A program may use at most 256 MiB of HBM per device.

v0:
```python
import math

import jax
import jax.numpy as jnp
from jax import lax
from jax.sharding import PartitionSpec as P

HEADS = 16


epsilon = 1e-05
masked_score = -1e30


def layer_norm(values, gain_row, shift_row):
    center = values - jnp.mean(values, axis=-1, keepdims=True)
    spread = jnp.mean(center * center, axis=-1, keepdims=True)
    return center * lax.rsqrt(spread + epsilon) * gain_row + shift_row


def inner_rows(former, latter):
    return lax.dot_general(
        former, latter, (((0,), (0,)), ((), ())), preferred_element_type=jnp.float32
    )


def against(former, latter):
    return lax.dot_general(
        former, latter, (((1,), (1,)), ((), ())), preferred_element_type=jnp.float32
    )


def block_place(key_count, key_window, block_index, block_rows):
    row_start = block_index * block_rows
    key_start = jnp.clip(row_start + block_rows - key_window, 0, key_count - key_window)
    return (row_start, key_start)


def block_scores(query_part, key_part, query_seg, key_seg, row_start, key_start, causal):
    scaling = 1.0 / math.sqrt(query_part.shape[2])
    scores = (
        jnp.einsum("qhe,khe->hqk", query_part, key_part, preferred_element_type=jnp.float32)
        * scaling
    )
    allowed = query_seg[:, None] == key_seg[None, :]
    if causal:
        query_pos = row_start + jnp.arange(query_part.shape[0], dtype=jnp.int32)
        key_pos = key_start + jnp.arange(key_part.shape[0], dtype=jnp.int32)
        allowed = allowed & (key_pos[None, :] <= query_pos[:, None])
    return jnp.where(allowed[None], scores, masked_score)


def attention_forward(queries, key_rows, values, query_ids, key_ids, causal, key_window):
    row_count = queries.shape[0]
    key_count = key_rows.shape[0]
    block_rows = min(512, row_count)

    def one_block(block_index):
        row_start, key_start = block_place(key_count, key_window, block_index, block_rows)
        query_part = lax.dynamic_slice_in_dim(queries, row_start, block_rows, 0)
        query_seg = lax.dynamic_slice_in_dim(query_ids, row_start, block_rows, 0)
        scores = block_scores(
            query_part, key_rows, query_seg, key_ids, row_start, key_start, causal
        )
        row_max = jnp.max(scores, axis=-1, keepdims=True)
        exponent = jnp.exp(scores - row_max)
        row_total = jnp.sum(exponent, axis=-1, keepdims=True)
        weights = (exponent / row_total).astype(jnp.bfloat16)
        context = jnp.einsum("hqk,khe->qhe", weights, values, preferred_element_type=jnp.float32)
        return (context.astype(jnp.bfloat16), (row_max + jnp.log(row_total))[:, :, 0])

    contexts, log_totals = lax.map(one_block, jnp.arange(row_count // block_rows, dtype=jnp.int32))
    return (contexts.reshape(queries.shape), log_totals)


def attention_backward(
    queries, key_rows, values, context_grad, log_totals, query_ids, key_ids, causal, key_window
):
    row_count = queries.shape[0]
    key_count = key_rows.shape[0]
    block_rows = min(512, row_count)
    scaling = 1.0 / math.sqrt(queries.shape[2])

    def one_block(running, block_index):
        key_sum, value_sum = running
        row_start, key_start = block_place(key_count, key_window, block_index, block_rows)
        query_part = lax.dynamic_slice_in_dim(queries, row_start, block_rows, 0)
        grad_part = lax.dynamic_slice_in_dim(context_grad, row_start, block_rows, 0)
        query_seg = lax.dynamic_slice_in_dim(query_ids, row_start, block_rows, 0)
        scores = block_scores(
            query_part, key_rows, query_seg, key_ids, row_start, key_start, causal
        )
        weights = jnp.exp(scores - log_totals[block_index][:, :, None])
        value_dots = jnp.einsum(
            "qhe,khe->hqk", grad_part, values, preferred_element_type=jnp.float32
        )
        centered = value_dots - jnp.sum(weights * value_dots, axis=-1, keepdims=True)
        dscore = (weights * centered).astype(jnp.bfloat16)
        dquery = (
            jnp.einsum("hqk,khe->qhe", dscore, key_rows, preferred_element_type=jnp.float32)
            * scaling
        )
        d_key = (
            jnp.einsum("hqk,qhe->khe", dscore, query_part, preferred_element_type=jnp.float32)
            * scaling
        )
        dvalue = jnp.einsum(
            "hqk,qhe->khe",
            weights.astype(jnp.bfloat16),
            grad_part,
            preferred_element_type=jnp.float32,
        )
        key_sum = key_sum + d_key
        value_sum = value_sum + dvalue
        return ((key_sum, value_sum), dquery)

    empty_sum = jnp.zeros(key_rows.shape, jnp.float32)
    (key_sum, value_sum), dqueries = lax.scan(
        one_block, (empty_sum, empty_sum), jnp.arange(row_count // block_rows, dtype=jnp.int32)
    )
    return (dqueries.reshape(queries.shape), key_sum, value_sum)


def fetch_pair(inner_part, outer_part):
    inner_part, outer_part = (
        lax.all_gather(inner_part, "dp", axis=0, tiled=True),
        lax.all_gather(outer_part, "dp", axis=1, tiled=True),
    )
    inner_part, outer_part = (
        lax.all_gather(inner_part, "seq", axis=1, tiled=True),
        lax.all_gather(outer_part, "seq", axis=0, tiled=True),
    )
    return (inner_part, outer_part)


def reduce_pair(inner_grad, outer_grad):
    inner_grad, outer_grad = (
        lax.psum_scatter(
            inner_grad.astype(jnp.bfloat16), "seq", scatter_dimension=1, tiled=True
        ).astype(jnp.float32),
        lax.psum_scatter(
            outer_grad.astype(jnp.bfloat16), "seq", scatter_dimension=0, tiled=True
        ).astype(jnp.float32),
    )
    return (
        lax.psum_scatter(
            inner_grad.astype(jnp.bfloat16), "dp", scatter_dimension=0, tiled=True
        ).astype(jnp.float32),
        lax.psum_scatter(
            outer_grad.astype(jnp.bfloat16), "dp", scatter_dimension=1, tiled=True
        ).astype(jnp.float32),
    )


def context_back(context):
    return lax.all_to_all(context, "seq", split_axis=0, concat_axis=1, tiled=True)


def grad_heads(gradient):
    return lax.all_to_all(gradient, "seq", split_axis=1, concat_axis=0, tiled=True)


def split_cross(cross_in, group_width):
    width_rows = cross_in.shape[0]
    held_blocks = cross_in.shape[1] // (3 * group_width)
    grouped = cross_in.reshape(width_rows, held_blocks, 3 * group_width)
    return (
        grouped[:, :, :group_width].reshape(width_rows, held_blocks * group_width),
        grouped[:, :, group_width:].reshape(width_rows, held_blocks * 2 * group_width),
    )


def join_cross(query_grad, memory_grad, group_width):
    width_rows = query_grad.shape[0]
    held_blocks = query_grad.shape[1] // group_width
    joined = jnp.concatenate(
        [
            query_grad.reshape(width_rows, held_blocks, group_width),
            memory_grad.reshape(width_rows, held_blocks, 2 * group_width),
        ],
        axis=2,
    )
    return joined.reshape(width_rows, held_blocks * 3 * group_width)


def shards(
    inputs,
    encoder_states,
    segment_ids,
    encoder_ids,
    norm_gains,
    norm_shifts,
    attend_weights,
    attend_output,
    attend_biases,
    cross_query,
    cross_memory,
    cross_output,
    cross_biases,
    expand_weight,
    expand_bias,
    shrink_weight,
    shrink_bias,
    output_cotangent,
):
    pieces = lax.axis_size("seq")
    tokens = inputs[0].astype(jnp.float32)
    row_count, model_width = tokens.shape
    head_count = HEADS
    head_width = model_width // head_count
    pack_rows = row_count * pieces
    group_width = model_width // pieces
    pack_ids = segment_ids[0]
    memory_ids = encoder_ids[0]
    encoder = encoder_states[0]
    memory_rows = encoder.shape[0]
    gain_rows = norm_gains.astype(jnp.float32)
    shift_rows = norm_shifts.astype(jnp.float32)
    bias_self = attend_biases.astype(jnp.float32)
    bias_cross = cross_biases.astype(jnp.float32)
    bias_expand = expand_bias.astype(jnp.float32)
    bias_shrink = shrink_bias.astype(jnp.float32)
    zero_heads = jnp.zeros((head_count, head_width), jnp.float32)
    self_bias = jnp.stack(
        [
            bias_self[0].reshape(head_count, head_width),
            zero_heads,
            bias_self[1].reshape(head_count, head_width),
        ],
        axis=1,
    )
    memory_bias = jnp.stack([zero_heads, bias_cross[1].reshape(head_count, head_width)], axis=1)
    cross_local = jnp.concatenate([cross_query, cross_memory], axis=1)
    attend_w, attend_o = fetch_pair(attend_weights, attend_output)
    normed1, norm_back1 = jax.vjp(layer_norm, tokens, gain_rows[0], shift_rows[0])
    low_one = normed1.astype(jnp.bfloat16)
    projected = (
        jnp.dot(low_one, attend_w, preferred_element_type=jnp.float32).reshape(
            row_count, head_count, 3, head_width
        )
        + self_bias
    )
    packed = projected.astype(jnp.bfloat16).reshape(row_count, head_count, 3 * head_width)
    head_rows = lax.all_to_all(packed, "seq", split_axis=1, concat_axis=0, tiled=True)
    query1 = head_rows[:, :, :head_width]
    key1 = head_rows[:, :, head_width : 2 * head_width]
    value1 = head_rows[:, :, 2 * head_width :]
    context1, totals1 = attention_forward(query1, key1, value1, pack_ids, pack_ids, True, pack_rows)
    mixed1 = context_back(context1).reshape(row_count, model_width)
    attended = jnp.dot(mixed1, attend_o, preferred_element_type=jnp.float32)
    middle = tokens + attended + bias_self[2]
    cross_in, cross_o = fetch_pair(cross_local, cross_output)
    cross_q, cross_kv = split_cross(cross_in, group_width)
    normed2, norm_back2 = jax.vjp(layer_norm, middle, gain_rows[1], shift_rows[1])
    low_two = normed2.astype(jnp.bfloat16)
    cross_rows = (
        (jnp.dot(low_two, cross_q, preferred_element_type=jnp.float32) + bias_cross[0])
        .astype(jnp.bfloat16)
        .reshape(row_count, head_count, head_width)
    )
    memory_proj = (
        jnp.dot(encoder, cross_kv, preferred_element_type=jnp.float32).reshape(
            memory_rows, head_count, 2, head_width
        )
        + memory_bias
    )
    memory_packed = memory_proj.astype(jnp.bfloat16).reshape(
        memory_rows, head_count, 2 * head_width
    )
    query2, memory2 = (
        lax.all_to_all(cross_rows, "seq", split_axis=1, concat_axis=0, tiled=True),
        lax.all_to_all(memory_packed, "seq", split_axis=1, concat_axis=0, tiled=True),
    )
    key2 = memory2[:, :, :head_width]
    value2 = memory2[:, :, head_width:]
    memory_window = memory2.shape[0]
    context2, totals2 = attention_forward(
        query2, key2, value2, pack_ids, memory_ids, False, memory_window
    )
    mixed2 = context_back(context2).reshape(row_count, model_width)
    crossed = jnp.dot(mixed2, cross_o, preferred_element_type=jnp.float32)
    later = middle + crossed + bias_cross[2]
    expand_w, shrink_w = fetch_pair(expand_weight, shrink_weight)
    normed3, norm_back3 = jax.vjp(layer_norm, later, gain_rows[2], shift_rows[2])
    low_three = normed3.astype(jnp.bfloat16)
    hidden = jnp.dot(low_three, expand_w, preferred_element_type=jnp.float32) + bias_expand
    active, gelu_back = jax.vjp(jax.nn.gelu, hidden)
    low_active = active.astype(jnp.bfloat16)
    expanded = jnp.dot(low_active, shrink_w, preferred_element_type=jnp.float32)
    layer_output = (later + expanded + bias_shrink).astype(jnp.bfloat16)[None]
    upstream = output_cotangent[0]
    expand_w, shrink_w = fetch_pair(expand_weight, shrink_weight)
    shrink_w_grad = inner_rows(low_active, upstream)
    shrink_b_grad = jnp.sum(upstream.astype(jnp.float32), axis=0)
    d_active = against(upstream, shrink_w)
    d_hidden = gelu_back(d_active)[0].astype(jnp.bfloat16)
    expand_w_grad = inner_rows(low_three, d_hidden)
    unit_sums = jnp.sum(d_hidden.astype(jnp.float32), axis=0)
    d_normed3 = against(d_hidden, expand_w)
    back_three = norm_back3(d_normed3)
    d_later = upstream.astype(jnp.float32) + back_three[0]
    expand_sums = reduce_pair(expand_w_grad, shrink_w_grad)
    cross_in, cross_o = fetch_pair(cross_local, cross_output)
    cross_q, cross_kv = split_cross(cross_in, group_width)
    low_later = d_later.astype(jnp.bfloat16)
    cross_out_bias = jnp.sum(low_later.astype(jnp.float32), axis=0)
    d_context2 = grad_heads(
        against(low_later, cross_o).astype(jnp.bfloat16).reshape(row_count, head_count, head_width)
    )
    cross_o_grad = inner_rows(mixed2, low_later)
    d_query2, d_key2, d_value2 = attention_backward(
        query2, key2, value2, d_context2, totals2, pack_ids, memory_ids, False, memory_window
    )
    query_low = d_query2.astype(jnp.bfloat16)
    d_memory2 = jnp.concatenate([d_key2, d_value2], axis=2).astype(jnp.bfloat16)
    query_back, memory_back = (
        lax.all_to_all(query_low, "seq", split_axis=0, concat_axis=1, tiled=True),
        lax.all_to_all(d_memory2, "seq", split_axis=0, concat_axis=1, tiled=True),
    )
    query_flat = query_back.reshape(row_count, model_width)
    memory_flat = memory_back.reshape(memory_rows, 2 * model_width)
    cross_query_bias = jnp.sum(query_flat.astype(jnp.float32), axis=0)
    cross_value_bias = jnp.sum(memory_back[:, :, head_width:].astype(jnp.float32), axis=0).reshape(
        model_width
    )
    d_normed2 = against(query_flat, cross_q)
    encoder_gradient = against(memory_flat, cross_kv).astype(jnp.bfloat16)[None]
    cross_q_grad = inner_rows(low_two, query_flat)
    cross_kv_grad = inner_rows(encoder, memory_flat)
    back_two = norm_back2(d_normed2)
    d_middle = d_later + back_two[0]
    cross_b_grad = jnp.stack([cross_query_bias, cross_value_bias, cross_out_bias])
    cross_sums = reduce_pair(join_cross(cross_q_grad, cross_kv_grad, group_width), cross_o_grad)
    attend_w, attend_o = fetch_pair(attend_weights, attend_output)
    low_middle = d_middle.astype(jnp.bfloat16)
    attend_out_bias = jnp.sum(low_middle.astype(jnp.float32), axis=0)
    d_context1 = grad_heads(
        against(low_middle, attend_o)
        .astype(jnp.bfloat16)
        .reshape(row_count, head_count, head_width)
    )
    attend_o_grad = inner_rows(mixed1, low_middle)
    d_query1, d_key1, d_value1 = attention_backward(
        query1, key1, value1, d_context1, totals1, pack_ids, pack_ids, True, pack_rows
    )
    d_packed = jnp.concatenate([d_query1, d_key1, d_value1], axis=2).astype(jnp.bfloat16)
    token_back = lax.all_to_all(d_packed, "seq", split_axis=0, concat_axis=1, tiled=True)
    token_flat = token_back.reshape(row_count, 3 * model_width)
    head_sums = jnp.sum(token_back.astype(jnp.float32), axis=0)
    attend_query_bias = head_sums[:, :head_width].reshape(model_width)
    attend_value_bias = head_sums[:, 2 * head_width :].reshape(model_width)
    d_normed1 = against(token_flat, attend_w)
    attend_w_grad = inner_rows(low_one, token_flat)
    back_one = norm_back1(d_normed1)
    input_gradient = (d_middle + back_one[0]).astype(jnp.bfloat16)[None]
    attend_b_grad = jnp.stack([attend_query_bias, attend_value_bias, attend_out_bias])
    gain_grads = jnp.stack([back_one[1], back_two[1], back_three[1]])
    shift_grads = jnp.stack([back_one[2], back_two[2], back_three[2]])
    attend_sums = reduce_pair(attend_w_grad, attend_o_grad)
    small_sums = lax.psum(
        (gain_grads, shift_grads, attend_b_grad, cross_b_grad, unit_sums, shrink_b_grad),
        ("dp", "seq"),
    )
    cross_inner = cross_sums[0]
    return (
        layer_output,
        input_gradient,
        encoder_gradient,
        small_sums[0],
        small_sums[1],
        attend_sums[0],
        attend_sums[1],
        small_sums[2],
        cross_inner[:, :group_width],
        cross_inner[:, group_width:],
        cross_sums[1],
        small_sums[3],
        expand_sums[0],
        small_sums[4],
        expand_sums[1],
        small_sums[5],
    )


def solution(mesh):
    in_specs = (
        P("dp", "seq", None),
        P("dp", "seq", None),
        P("dp", None),
        P("dp", None),
        P(),
        P(),
        P("dp", "seq"),
        P("seq", "dp"),
        P(),
        P("dp", "seq"),
        P("dp", "seq"),
        P("seq", "dp"),
        P(),
        P("dp", "seq"),
        P(),
        P("seq", "dp"),
        P(),
        P("dp", "seq", None),
    )
    out_specs = (
        P("dp", "seq", None),
        P("dp", "seq", None),
        P("dp", "seq", None),
        P(),
        P(),
        P("dp", "seq"),
        P("seq", "dp"),
        P(),
        P("dp", "seq"),
        P("dp", "seq"),
        P("seq", "dp"),
        P(),
        P("dp", "seq"),
        P(),
        P("seq", "dp"),
        P(),
    )
    return jax.shard_map(shards, mesh=mesh, in_specs=in_specs, out_specs=out_specs, check_vma=False)
```

profile of v0, /device:TPU:8, one launch (start us, length us, event | category | flops | bytes accessed | tf_op | source)
XLA Modules:
  0.0 1787.8 jit_solution(2541696325762381082)
XLA Ops:
  63.8 50.8 %all-gather.9.cloned.1.call-done = bf16[1024,3072]{1,0:T(8,128)(2,1)} async-done(((bf16[1024,384]{1,0:T(8,128)(2,1)}), bf16[1024,3072]{1,0:T(8,128)(2,1)}) %all-gather.9.cloned.1.call-update) | async-done | bytes 6291472 | tf_op jit(solution)/shard_map/all_gather | solution.py:130
  135.2 16.6 all-gather.21.cloned.1.call-done
  151.9 38.8 %all-to-all-done = bf16[256,16,192]{0,2,1:T(8,128)(2,1)S(1)} async-done(((bf16[256,16,192]{0,2,1:T(8,128)(2,1)}), bf16[256,16,192]{0,2,1:T(8,128)(2,1)S(1)}, u32[]{:S(2)}, u32[]{:S(2)}) %all-to-all-start) | async-done | bytes 1572896 | tf_op jit(solution)/shard_map/all_to_all | solution.py:244
  198.0 37.9 %while.62 = (s32[]{:T(128)}, bf16[4,512,2,64]{1,3,2,0:T(8,128)(2,1)S(1)}, f32[4,2,512]{2,1,0:T(2,128)S(1)}, s32[4]{0:T(128)S(1)}, s32[2048]{0:T(1024)S(1)}, /*in...) while((s32[]{:T(128)}, ...), condition=%wide.region_5.6_spmd, body=%wide.region_2.5_spmd.sunk | while | flops 565249536 | bytes 30738692 | solution.py:72
  274.5 17.9 %all-to-all-done.3 = bf16[128,16,128]{0,2,1:T(8,128)(2,1)S(1)} async-done(((bf16[128,16,128]{0,2,1:T(8,128)(2,1)}), bf16[128,16,128]{0,2,1:T(8,128)(2,1)S(1)}, u32[]{:S(2)}, u32[]{:S(2)}) %all-to-all-start.3) | async-done | bytes 524320 | tf_op jit(solution)/shard_map/all_to_all | solution.py:272
  300.8 19.4 %all-to-all-done.2 = bf16[256,16,64]{0,2,1:T(8,128)(2,1)S(1)} async-done(((bf16[256,16,64]{0,2,1:T(8,128)(2,1)}), bf16[256,16,64]{0,2,1:T(8,128)(2,1)S(1)}, u32[]{:S(2)}, u32[]{:S(2)}) %all-to-all-start.2) | async-done | bytes 524320 | tf_op jit(solution)/shard_map/all_to_all | solution.py:271
  321.1 25.6 %while.63 = (s32[]{:T(128)}, bf16[4,512,2,64]{1,3,2,0:T(8,128)(2,1)S(1)}, f32[4,2,512]{2,1,0:T(2,128)S(1)}, s32[4]{0:T(128)S(1)}, s32[2048]{0:T(1024)S(1)}, /*in...) while((s32[]{:T(128)}, ...), condition=%wide.region_11.12_spmd, body=%wide.region_8.11_spmd.sunk | while | flops 281607168 | bytes 15509711 | solution.py:72
  355.7 26.7 %all-to-all-done.4 = bf16[8,2,16384]{2,1,0:T(2,128)(2,1)S(1)} async-done(((bf16[8,2,16384]{2,1,0:T(2,128)(2,1)}), bf16[8,2,16384]{2,1,0:T(2,128)(2,1)S(1)}, u32[]{:S(2)}, u32[]{:S(2)}) %all-to-all-start.4) | async-done | bytes 524320 | tf_op jit(solution)/shard_map/all_to_all | solution.py:156
  386.5 71.9 %all-gather.19.cloned.1.call-done = bf16[1024,8192]{1,0:T(8,128)(2,1)} async-done(((bf16[1024,1024]{1,0:T(8,128)(2,1)}), bf16[1024,8192]{1,0:T(8,128)(2,1)}) %all-gather.19.cloned.1.call-update) | async-done | bytes 16777232 | tf_op jit(solution)/shard_map/all_gather | solution.py:130
  471.2 140.6 %all-gather.23.cloned.1.call-done = bf16[8192,1024]{1,0:T(8,128)(2,1)} async-done(((bf16[1024,1024]{1,0:T(8,128)(2,1)}), bf16[8192,1024]{1,0:T(8,128)(2,1)}) %all-gather.23.cloned.1.call-update) | async-done | bytes 16777232 | tf_op jit(solution)/shard_map/all_gather | solution.py:131
  611.7 16.0 convert_reduce_fusion
  669.2 86.6 %while.64 = (s32[]{:T(128)}, f32[1024,2,64]{0,2,1:T(8,128)}, f32[1024,2,64]{0,2,1:T(8,128)}, bf16[4,512,2,64]{1,3,2,0:T(8,128)(2,1)}, s32[4]{0:T(128)S(1)}, /*in...) while((s32[]{:T(128)}, f32[1024,2,64]{0,2,1:T(8,128)}, ...), condition=%wide.region_18.19_spmd.clone, body=%wide.region_16.18_spmd.clone.sunk | while | flops 688061440 | bytes 58235256 | solution.py:118
  758.9 20.3 %all_to_all.168 = bf16[8,2,16384]{2,1,0:T(2,128)(2,1)S(1)} all-to-all(bf16[8,2,16384]{2,1,0:T(2,128)(2,1)S(1)} %reshape.586), channel_id=1, replica_groups=mesh['dp'=4,'seq'=8] {'seq'}, dimensions={0} | all-to-all | bytes 1048576 | tf_op jit(solution)/shard_map/all_to_all | solution.py:317
  805.7 14.7 all-to-all-done.9
  842.2 124.5 %while.65 = (s32[]{:T(128)}, f32[2048,2,64]{0,2,1:T(8,128)S(1)}, f32[2048,2,64]{0,2,1:T(8,128)}, bf16[4,512,2,64]{1,3,2,0:T(8,128)(2,1)}, s32[4]{0:T(128)S(1)}, ...) while((s32[]{:T(128)}, f32[2048,2,64]{0,2,1:T(8,128)S(1)}, ...), condition=%wide.region_23.24_spmd.clone, body=%wide.region_21.23_spmd.clone.sunk | while | flops 1378158080 | bytes 128252448 | solution.py:118
  973.0 53.7 %all_to_all.169 = bf16[2048,2,192]{2,1,0:T(2,128)(2,1)S(1)} all-to-all(bf16[2048,2,192]{2,1,0:T(2,128)(2,1)} %copy.212), channel_id=1, replica_groups=mesh['dp'=4,'seq'=8] {'seq'}, dimensions={0} | all-to-all | bytes 3145728 | tf_op jit(solution)/shard_map/all_to_all | solution.py:347
  1075.1 37.8 %reduce-scatter.37.cloned.1.call-done = bf16[384,1024]{1,0:T(8,128)(2,1)} async-done(((bf16[3072,1024]{1,0:T(8,128)(2,1)}), bf16[384,1024]{1,0:T(8,128)(2,1)}) %reduce-scatter.37.cloned.1.call-update) | async-done | bytes 786448
  1115.3 166.6 %reduce-scatter.29.cloned.1.call-done = bf16[1024,1024]{1,0:T(8,128)(2,1)} async-done(((bf16[1024,8192]{1,0:T(8,128)(2,1)}), bf16[1024,1024]{1,0:T(8,128)(2,1)}) %reduce-scatter.29.cloned.1.call-update) | async-done | bytes 2097168 | tf_op jit(solution)/shard_map/reduce_scatter | solution.py:138
  1282.0 168.7 %reduce-scatter.33.cloned.1.call-done = bf16[1024,1024]{1,0:T(8,128)(2,1)} async-done(((bf16[8192,1024]{1,0:T(8,128)(2,1)}), bf16[1024,1024]{1,0:T(8,128)(2,1)}) %reduce-scatter.33.cloned.1.call-update) | async-done | bytes 2097168 | tf_op jit(solution)/shard_map/reduce_scatter | solution.py:141
  1507.1 27.4 %reduce-scatter.23.cloned.1.call-done = bf16[256,384]{1,0:T(8,128)(2,1)} async-done(((bf16[1024,384]{1,0:T(8,128)(2,1)}), bf16[256,384]{1,0:T(8,128)(2,1)}) %reduce-scatter.23.cloned.1.call-update) | async-done | bytes 196624 | tf_op jit(solution)/shard_map/reduce_scatter | solution.py:146
  1537.6 25.7 %reduce-scatter.17.cloned.1.call-done = bf16[256,384]{1,0:T(8,128)(2,1)} async-done(((bf16[1024,384]{1,0:T(8,128)(2,1)}), bf16[256,384]{1,0:T(8,128)(2,1)}) %reduce-scatter.17.cloned.1.call-update) | async-done | bytes 196624 | tf_op jit(solution)/shard_map/reduce_scatter | solution.py:146
  1565.1 36.5 %reduce-scatter.31.cloned.1.call-done = bf16[256,1024]{1,0:T(8,128)(2,1)} async-done(((bf16[1024,1024]{1,0:T(8,128)(2,1)}), bf16[256,1024]{1,0:T(8,128)(2,1)}) %reduce-scatter.31.cloned.1.call-update) | async-done | bytes 524304 | tf_op jit(solution)/shard_map/reduce_scatter | solution.py:146
  1603.7 36.2 %reduce-scatter.35.cloned.1.call-done = bf16[1024,256]{1,0:T(8,128)(2,1)} async-done(((bf16[1024,1024]{1,0:T(8,128)(2,1)}), bf16[1024,256]{1,0:T(8,128)(2,1)}) %reduce-scatter.35.cloned.1.call-update) | async-done | bytes 524304 | tf_op jit(solution)/shard_map/reduce_scatter | solution.py:149
  1641.9 130.7 %all-reduce.4.cloned.1.call-done = (f32[3,1024]{1,0:T(4,128)}, f32[3,1024]{1,0:T(4,128)}, f32[3,1024]{1,0:T(4,128)}, f32[3,1024]{1,0:T(4,128)}, f32[8192]{0:T(1024)}, /*index=5*/f32[1024]{0:T(1024)}) async-done(((f32[3,1024]{1,0:T(4,128)}, f32[3,1024]{1,0:T(4,128)}, f32[3,1024]{1,0:T(4,128)}, f32[3,1024]{1,0:T(4,128)}, f32[8192]{0:T(1024)}, /*index=5*/f32[1024]{0:T(1024)}), (f32[3,1024]{1,0:T(4,128)}, ...) | async-done | bytes 86032 | tf_op jit(solution)/shard_map/psum | solution.py:360
  (607 shorter events, 626.6 us)
Async XLA Ops:
  7.2 53.2 %all-gather.17.cloned.1.call-start = ((), (), s32[]{:S(2)}) async-start(), calls=%async_computation.26 | async-start | bytes 2621440 | tf_op jit(solution)/shard_map/all_gather | solution.py:126
  8.0 106.6 %all-gather.9.cloned.1.call-start = ((), (), s32[]{:S(2)}) async-start(), calls=%async_computation.22 | async-start | bytes 7077888 | tf_op jit(solution)/shard_map/all_gather | solution.py:130
  22.2 129.7 %all-gather.21.cloned.1.call-start = ((), (), s32[]{:S(2)}) async-start(), calls=%async_computation.28 | async-start | bytes 2621440 | tf_op jit(solution)/shard_map/all_gather | solution.py:127
  22.9 226.2 %all-gather.13.cloned.1.call-start = ((), (), s32[]{:S(2)}) async-start(), calls=%async_computation.24 | async-start | bytes 7077888 | tf_op jit(solution)/shard_map/all_gather | solution.py:130
  35.5 234.2 %all-gather.11.cloned.1.call-start = ((), (), s32[]{:S(2)}) async-start(), calls=%async_computation.23 | async-start | bytes 2359296 | tf_op jit(solution)/shard_map/all_gather | solution.py:131
  49.8 334.0 %all-gather.15.cloned.1.call-start = ((), (), s32[]{:S(2)}) async-start(), calls=%async_computation.25 | async-start | bytes 2359296 | tf_op jit(solution)/shard_map/all_gather | solution.py:131
  60.4 398.0 %all-gather.19.cloned.1.call-start = ((), (), s32[]{:S(2)}) async-start(), calls=%async_computation.27 | async-start | bytes 18874368 | tf_op jit(solution)/shard_map/all_gather | solution.py:130
  129.5 61.1 %all-to-all-start = ((bf16[256,16,192]{0,2,1:T(8,128)(2,1)}), bf16[256,16,192]{0,2,1:T(8,128)(2,1)S(1)}, u32[]{:S(2)}, u32[]{:S(2)}) async-start(bf16[256,16,192]{0,2,1:T(8,128)(2,1)} %bitcast.410), calls=%async_computation | async-start | bytes 3145728 | tf_op jit(solution)/shard_map/all_to_all | solution.py:244
  134.9 476.8 %all-gather.23.cloned.1.call-start = ((), (), s32[]{:S(2)}) async-start(), calls=%async_computation.29 | async-start | bytes 18874368 | tf_op jit(solution)/shard_map/all_gather | solution.py:131
  262.0 30.4 %all-to-all-start.3 = ((bf16[128,16,128]{0,2,1:T(8,128)(2,1)}), bf16[128,16,128]{0,2,1:T(8,128)(2,1)S(1)}, u32[]{:S(2)}, u32[]{:S(2)}) async-start(bf16[128,16,128]{0,2,1:T(8,128)(2,1)} %add_convert_fusion.3), calls=%async_computation.3 | async-start | bytes 1048576 | tf_op jit(solution)/shard_map/all_to_all | solution.py:272
  349.0 33.5 %all-to-all-start.4 = ((bf16[8,2,16384]{2,1,0:T(2,128)(2,1)}), bf16[8,2,16384]{2,1,0:T(2,128)(2,1)S(1)}, u32[]{:S(2)}, u32[]{:S(2)}) async-start(bf16[8,2,16384]{2,1,0:T(2,128)(2,1)} %reshape.584), calls=%async_computation.4 | async-start | bytes 1048576 | tf_op jit(solution)/shard_map/all_to_all | solution.py:156
  653.4 418.1 %reduce-scatter.25.cloned.1.call-start = ((), (), s32[]{:S(2)}) async-start(), calls=%async_computation.34 | async-start | bytes 2359296 | tf_op jit(solution)/shard_map/reduce_scatter | solution.py:141
  655.5 416.6 %reduce-scatter.19.cloned.1.call-start = ((), (), s32[]{:S(2)}) async-start(), calls=%async_computation.31 | async-start | bytes 2359296 | tf_op jit(solution)/shard_map/reduce_scatter | solution.py:141
  826.9 245.8 %reduce-scatter.39.cloned.1.call-start = ((), (), s32[]{:S(2)}) async-start(), calls=%async_computation.41 | async-start | bytes 7077888
  835.6 277.4 %reduce-scatter.37.cloned.1.call-start = ((), (), s32[]{:S(2)}) async-start(), calls=%async_computation.40 | async-start | bytes 7077888
  1045.2 236.7 %reduce-scatter.29.cloned.1.call-start = ((), (), s32[]{:S(2)}) async-start(), calls=%async_computation.36 | async-start | bytes 18874368 | tf_op jit(solution)/shard_map/reduce_scatter | solution.py:138
  1058.9 391.9 %reduce-scatter.33.cloned.1.call-start = ((), (), s32[]{:S(2)}) async-start(), calls=%async_computation.38 | async-start | bytes 18874368 | tf_op jit(solution)/shard_map/reduce_scatter | solution.py:141
  1071.5 407.2 %reduce-scatter.27.cloned.1.call-start = ((), (), s32[]{:S(2)}) async-start(), calls=%async_computation.35 | async-start | bytes 327680 | tf_op jit(solution)/shard_map/reduce_scatter | solution.py:149
  1072.1 433.6 %reduce-scatter.21.cloned.1.call-start = ((), (), s32[]{:S(2)}) async-start(), calls=%async_computation.32 | async-start | bytes 327680 | tf_op jit(solution)/shard_map/reduce_scatter | solution.py:149
  1072.6 461.9 %reduce-scatter.23.cloned.1.call-start = ((), (), s32[]{:S(2)}) async-start(), calls=%async_computation.33 | async-start | bytes 983040 | tf_op jit(solution)/shard_map/reduce_scatter | solution.py:146
  1075.0 488.4 %reduce-scatter.17.cloned.1.call-start = ((), (), s32[]{:S(2)}) async-start(), calls=%async_computation.30 | async-start | bytes 983040 | tf_op jit(solution)/shard_map/reduce_scatter | solution.py:146
  1115.3 486.3 %reduce-scatter.31.cloned.1.call-start = ((), (), s32[]{:S(2)}) async-start(), calls=%async_computation.37 | async-start | bytes 2621440 | tf_op jit(solution)/shard_map/reduce_scatter | solution.py:146
  1281.9 357.9 %reduce-scatter.35.cloned.1.call-start = ((), (), s32[]{:S(2)}) async-start(), calls=%async_computation.39 | async-start | bytes 2621440 | tf_op jit(solution)/shard_map/reduce_scatter | solution.py:149
  1450.8 321.8 %all-reduce.4.cloned.1.call-start = ((), (), s32[]{:S(2)}) async-start(), calls=%async_computation.42 | async-start | bytes 204800 | tf_op jit(solution)/shard_map/psum | solution.py:360
  (122 other events, 3707.9 us)
Sparse Core Ops, SparseCore 0:
  9.9 40.0 all-gather.16
  51.6 62.9 all-gather.8
  116.4 35.3 all-gather.20
  153.3 67.4 all-gather.12
  222.3 31.8 all-gather.10
  255.6 39.1 all-gather.14
  296.5 161.9 all-gather.18
  460.0 151.6 all-gather.22
  656.5 33.5 reduce-scatter.24
  787.7 41.4 reduce-scatter.18
  835.7 68.3 reduce-scatter.38
  1045.3 67.5 reduce-scatter.36
  1115.3 166.6 reduce-scatter.28
  1284.1 166.5 reduce-scatter.32
  1453.4 25.2 reduce-scatter.26
  1481.5 24.0 reduce-scatter.20
  1508.4 26.0 reduce-scatter.22
  1537.3 26.0 reduce-scatter.16
  1566.3 35.1 reduce-scatter.30
  1604.6 35.1 reduce-scatter.34
  1647.4 125.1 all-reduce.3
where the time goes:
time: 1800 us; the launch traced here: 1790 us
  waiting for transfers between devices  1060 us (59%)
  matrix products  304 us (17%)
  blocking collectives  124 us (7%)
  local copies, waits for them, and re-layouts  121 us (7%)
  other arithmetic  79.7 us (4%)
  starting transfers between devices  55.3 us (3%)
  loops' own time  28.2 us (2%)
    reduce_scatter x3, waiting for transfers between devices, reduce_pair(): lax.psum_scatter(outer_grad.astype(jnp.bfloat16), 'seq', scatter_dimensio...  169 us
    reduce_scatter x1, waiting for transfers between devices, reduce_pair(): lax.psum_scatter(inner_grad.astype(jnp.bfloat16), 'seq', scatter_dimensio...  167 us
    all_gather x3, waiting for transfers between devices, fetch_pair(): lax.all_gather(outer_part, 'seq', axis=0, tiled=True)  141 us
    psum x1, waiting for transfers between devices, shards(): lax.psum((gain_grads, shift_grads, attend_b_grad, cross_b_grad, unit_sums...  131 us
    all_gather x3, waiting for transfers between devices, fetch_pair(): lax.all_gather(inner_part, 'seq', axis=1, tiled=True)  123 us
    reduce_scatter x3, waiting for transfers between devices, reduce_pair(): lax.psum_scatter(inner_grad.astype(jnp.bfloat16), 'dp', scatter_dimension...  89.6 us
    all_to_all x1, blocking collectives, shards(): lax.all_to_all(d_packed, 'seq', split_axis=0, concat_axis=1, tiled=True)  53.7 us
    dot_general x16, matrix products, block_scores(): jnp.einsum('qhe,khe->hqk', query_part, key_part, preferred_element_type=j...  52.6 us
  transfers between devices with their start and end apart: 29, of which 22 were waited for; matrix products, arithmetic and copies ran while one was open for 25% of the time, Pallas kernels for 0%

commit v1 on v0

v1 whole, which is shorter than its diff:
```python
import functools
import math

import jax
import jax.numpy as jnp
from jax import lax
from jax.experimental import pallas as pl
from jax.experimental.pallas import tpu as pltpu
from jax.sharding import Mesh
from jax.sharding import PartitionSpec as P

HEADS = 16

epsilon = 1e-05
masked_score = -1e30
head_width = 64


def piece_slot(position, own, relative):
    return position ^ own if relative else position


def load_block(ref, core, plane, own, relative):
    parts = [
        ref[piece_slot(piece, own[0], relative), piece_slot(core, own[1], relative), plane]
        for piece in range(ref.shape[0])
    ]
    return jnp.concatenate(parts, axis=0)


def load_rows(ref, own, relative):
    parts = [ref[piece_slot(piece, own[0], relative), 0, 0] for piece in range(ref.shape[0])]
    return jnp.concatenate(parts, axis=0)


def store_rows(ref, block, own, relative):
    piece_rows = ref.shape[3]
    for piece in range(ref.shape[0]):
        ref[piece_slot(piece, own[0], relative), 0, 0] = block[
            piece * piece_rows : (piece + 1) * piece_rows
        ]


def head_columns(transposed, heads):
    if heads == 1:
        return transposed
    feature = lax.broadcasted_iota(jnp.int32, transposed.shape, 0) // head_width
    zero = jnp.zeros_like(transposed)
    return jnp.concatenate([jnp.where(feature == h, transposed, zero) for h in range(heads)], axis=1)


def head_rows(block, heads):
    if heads == 1:
        return block
    feature = lax.broadcasted_iota(jnp.int32, block.shape, 1) // head_width
    zero = jnp.zeros_like(block)
    return jnp.concatenate([jnp.where(feature == h, block, zero) for h in range(heads)], axis=0)


def flip(block):
    return jnp.transpose(block.astype(jnp.float32), (1, 0)).astype(block.dtype)


def repeat_heads(row, heads):
    return row if heads == 1 else jnp.concatenate([row] * heads, axis=1)


def forward_kernel(
    scalars, q_ref, k_ref, v_ref, first_ref, last_ref, ctx_ref, keep_ref, lse_ref, keys, flipped,
    *, heads, q_rel, kv_rel, key_block,
):
    step = pl.program_id(0)
    steps = pl.num_programs(0)
    own = (scalars[0], scalars[1])
    cores, planes = k_ref.shape[1], k_ref.shape[2]
    group = k_ref.shape[0] * k_ref.shape[3]

    @pl.when(step == 0)
    def _():
        for plane in range(planes):
            for core in range(cores):
                start = (plane * cores + core) * group
                keys[start : start + group, :] = load_block(k_ref, core, plane, own, kv_rel)
                values = load_block(v_ref, core, plane, own, kv_rel)
                offset = start % key_block
                flipped[start // key_block, :, offset : offset + group] = flip(values)

    rows = q_ref.shape[0] * q_ref.shape[3]
    query = load_rows(q_ref, own, q_rel) * jnp.asarray(1.0 / math.sqrt(head_width), jnp.bfloat16)
    columns = head_columns(flip(query), heads)
    first = repeat_heads(first_ref[0], heads)
    last = repeat_heads(last_ref[0], heads)

    def one(block, carry):
        peak, total, sums = carry
        start = pl.multiple_of(block * key_block, key_block)
        scores = jnp.dot(keys[pl.ds(start, key_block), :], columns, preferred_element_type=jnp.float32)
        place = start + lax.broadcasted_iota(jnp.int32, scores.shape, 0)
        scores = jnp.where((place >= first) & (place <= last), scores, masked_score)
        newer = jnp.maximum(peak, jnp.max(scores, axis=0, keepdims=True))
        shrink = jnp.exp(peak - newer)
        exponent = jnp.exp(scores - newer)
        total = total * shrink + jnp.sum(exponent, axis=0, keepdims=True)
        low = exponent.astype(jnp.bfloat16)
        turned = flipped[block]
        fresh = []
        for h in range(heads):
            part = jnp.dot(
                turned[h * head_width : (h + 1) * head_width],
                low[:, h * rows : (h + 1) * rows],
                preferred_element_type=jnp.float32,
            )
            fresh.append(sums[h] * shrink[:, h * rows : (h + 1) * rows] + part)
        return (newer, total, tuple(fresh))

    empty = (
        jnp.full((1, heads * rows), masked_score, jnp.float32),
        jnp.zeros((1, heads * rows), jnp.float32),
        tuple(jnp.zeros((head_width, rows), jnp.float32) for _ in range(heads)),
    )
    peak, total, sums = lax.fori_loop(scalars[2 + step], scalars[2 + steps + step] + 1, one, empty)
    context = jnp.concatenate(
        [sums[h] / total[:, h * rows : (h + 1) * rows] for h in range(heads)], axis=0
    )
    keep_ref[0] = context
    lse_ref[0] = peak + jnp.log(total)
    store_rows(ctx_ref, jnp.transpose(context, (1, 0)).astype(jnp.bfloat16), own, False)


def backward_kernel(
    scalars, q_ref, k_ref, v_ref, dc_ref, keep_ref, lse_ref, first_ref, last_ref,
    dq_ref, dkv_ref, keys, values, flipped, dkeys, dvalues,
    *, heads, q_rel, kv_rel, key_block,
):
    step = pl.program_id(0)
    steps = pl.num_programs(0)
    own = (scalars[0], scalars[1])
    pieces, cores, planes, piece_rows = k_ref.shape[:4]
    group = pieces * piece_rows
    width = heads * head_width
    scaling = 1.0 / math.sqrt(head_width)

    @pl.when(step == 0)
    def _():
        for plane in range(planes):
            for core in range(cores):
                start = (plane * cores + core) * group
                block = load_block(k_ref, core, plane, own, kv_rel)
                keys[start : start + group, :] = block
                offset = start % key_block
                flipped[start // key_block, :, offset : offset + group] = flip(block)
                values[start : start + group, :] = load_block(v_ref, core, plane, own, kv_rel)
        dkeys[...] = jnp.zeros_like(dkeys)
        dvalues[...] = jnp.zeros_like(dvalues)

    rows = q_ref.shape[0] * q_ref.shape[3]
    query = load_rows(q_ref, own, q_rel) * jnp.asarray(scaling, jnp.bfloat16)
    grad = load_rows(dc_ref, own, False)
    turned_grad = flip(grad)
    query_columns = head_columns(flip(query), heads)
    grad_columns = head_columns(turned_grad, heads)
    query_rows = head_rows(query, heads)
    grad_rows = head_rows(grad, heads)
    product = turned_grad.astype(jnp.float32) * keep_ref[0]
    center = jnp.concatenate(
        [
            jnp.sum(product[h * head_width : (h + 1) * head_width], axis=0, keepdims=True)
            for h in range(heads)
        ],
        axis=1,
    )
    first = repeat_heads(first_ref[0], heads)
    last = repeat_heads(last_ref[0], heads)
    lse = lse_ref[0]

    def one(block, sums):
        start = pl.multiple_of(block * key_block, key_block)
        here = pl.ds(start, key_block)
        scores = jnp.dot(keys[here, :], query_columns, preferred_element_type=jnp.float32)
        place = start + lax.broadcasted_iota(jnp.int32, scores.shape, 0)
        scores = jnp.where((place >= first) & (place <= last), scores, masked_score)
        weights = jnp.exp(scores - lse)
        dots = jnp.dot(values[here, :], grad_columns, preferred_element_type=jnp.float32)
        dscore = (weights * (dots - center)).astype(jnp.bfloat16)
        dvalues[here, :] += jnp.dot(
            weights.astype(jnp.bfloat16), grad_rows, preferred_element_type=jnp.float32
        )
        dkeys[here, :] += jnp.dot(dscore, query_rows, preferred_element_type=jnp.float32)
        turned = flipped[block]
        return tuple(
            sums[h]
            + jnp.dot(
                turned[h * head_width : (h + 1) * head_width],
                dscore[:, h * rows : (h + 1) * rows],
                preferred_element_type=jnp.float32,
            )
            for h in range(heads)
        )

    empty = tuple(jnp.zeros((head_width, rows), jnp.float32) for _ in range(heads))
    sums = lax.fori_loop(scalars[2 + step], scalars[2 + steps + step] + 1, one, empty)
    dquery = jnp.transpose(jnp.concatenate(sums, axis=0) * scaling, (1, 0)).astype(jnp.bfloat16)
    store_rows(dq_ref, dquery, own, q_rel)

    @pl.when(step == steps - 1)
    def _():
        for plane in range(planes):
            for core in range(cores):
                start = (plane * cores + core) * group
                dk = dkeys[start : start + group, :].astype(jnp.bfloat16)
                dv = dvalues[start : start + group, :].astype(jnp.bfloat16)
                for piece in range(pieces):
                    slot = (piece_slot(piece, own[0], kv_rel), piece_slot(core, own[1], kv_rel), plane)
                    span = slice(piece * piece_rows, (piece + 1) * piece_rows)
                    dkv_ref[slot[0], slot[1], slot[2], :, 0:width] = dk[span]
                    dkv_ref[slot[0], slot[1], slot[2], :, width : 2 * width] = dv[span]


def row_spec(shape, width, relative, column=0):
    pieces, cores, planes, piece_rows = shape[:4]

    def place(step, scalars):
        core = lax.rem(step, cores)
        return (0, core ^ scalars[1] if relative else core, lax.div(step, cores), 0, column)

    return pl.BlockSpec((pieces, 1, 1, piece_rows, width), place)


def whole_spec(shape, column=0):
    return pl.BlockSpec(shape, lambda step, scalars: (0,) * (len(shape) - 1) + (column,))


def step_spec(shape):
    return pl.BlockSpec((1,) + shape[1:], lambda step, scalars: (step, 0, 0))


def pick(array, column, width):
    if width % 128 == 0:
        return (array, column)
    return (array[..., column * width : (column + 1) * width], 0)


def attend(scalars, queries, key_rows, values, first, last, width, q_rel, kv_rel):
    heads = width // head_width
    q_array, q_column = queries
    pieces, cores, planes, q_rows = q_array.shape[:4]
    steps = cores * planes
    rows = pieces * q_rows
    key_shape = key_rows[0].shape[:4]
    key_count = math.prod(key_shape)
    key_block = min(256, key_count)
    out_shape = (
        jax.ShapeDtypeStruct((pieces, cores, planes, q_rows, width), jnp.bfloat16),
        jax.ShapeDtypeStruct((steps, width, rows), jnp.float32),
        jax.ShapeDtypeStruct((steps, 1, heads * rows), jnp.float32),
    )
    return pl.pallas_call(
        functools.partial(
            forward_kernel, heads=heads, q_rel=q_rel, kv_rel=kv_rel, key_block=key_block
        ),
        grid_spec=pltpu.PrefetchScalarGridSpec(
            num_scalar_prefetch=1,
            grid=(steps,),
            in_specs=[
                row_spec(q_array.shape, width, q_rel, q_column),
                whole_spec(key_shape + (width,), key_rows[1]),
                whole_spec(key_shape + (width,), values[1]),
                step_spec(first.shape),
                step_spec(last.shape),
            ],
            out_specs=[
                row_spec(q_array.shape, width, False),
                step_spec(out_shape[1].shape),
                step_spec(out_shape[2].shape),
            ],
            scratch_shapes=[
                pltpu.VMEM((key_count, width), jnp.bfloat16),
                pltpu.VMEM((key_count // key_block, width, key_block), jnp.bfloat16),
            ],
        ),
        out_shape=out_shape,
        compiler_params=pltpu.CompilerParams(vmem_limit_bytes=32 * 2**20),
    )(scalars, q_array, key_rows[0], values[0], first, last)


def attend_back(
    scalars, queries, key_rows, values, grad, kept, lse, first, last, width, q_rel, kv_rel
):
    heads = width // head_width
    q_array, q_column = queries
    pieces, cores, planes, q_rows = q_array.shape[:4]
    steps = cores * planes
    key_shape = key_rows[0].shape[:4]
    key_count = math.prod(key_shape)
    key_block = min(256, key_count)
    out_shape = (
        jax.ShapeDtypeStruct((pieces, cores, planes, q_rows, width), jnp.bfloat16),
        jax.ShapeDtypeStruct(key_shape + (2 * width,), jnp.bfloat16),
    )
    return pl.pallas_call(
        functools.partial(
            backward_kernel, heads=heads, q_rel=q_rel, kv_rel=kv_rel, key_block=key_block
        ),
        grid_spec=pltpu.PrefetchScalarGridSpec(
            num_scalar_prefetch=1,
            grid=(steps,),
            in_specs=[
                row_spec(q_array.shape, width, q_rel, q_column),
                whole_spec(key_shape + (width,), key_rows[1]),
                whole_spec(key_shape + (width,), values[1]),
                row_spec(q_array.shape, width, False),
                step_spec(kept.shape),
                step_spec(lse.shape),
                step_spec(first.shape),
                step_spec(last.shape),
            ],
            out_specs=[
                row_spec(q_array.shape, width, q_rel),
                whole_spec(key_shape + (2 * width,)),
            ],
            scratch_shapes=[
                pltpu.VMEM((key_count, width), jnp.bfloat16),
                pltpu.VMEM((key_count, width), jnp.bfloat16),
                pltpu.VMEM((key_count // key_block, width, key_block), jnp.bfloat16),
                pltpu.VMEM((key_count, width), jnp.float32),
                pltpu.VMEM((key_count, width), jnp.float32),
            ],
        ),
        out_shape=out_shape,
        compiler_params=pltpu.CompilerParams(vmem_limit_bytes=32 * 2**20),
    )(scalars, q_array, key_rows[0], values[0], grad, kept, lse, first, last)


def layer_norm(values, gain_row, shift_row):
    center = values - jnp.mean(values, axis=-1, keepdims=True)
    spread = jnp.mean(center * center, axis=-1, keepdims=True)
    return center * lax.rsqrt(spread + epsilon) * gain_row + shift_row


def inner_rows(former, latter):
    return lax.dot_general(
        former, latter, (((0,), (0,)), ((), ())), preferred_element_type=jnp.float32
    )


def against(former, latter):
    return lax.dot_general(
        former, latter, (((1,), (1,)), ((), ())), preferred_element_type=jnp.float32
    )


def product(former, latter):
    return jnp.dot(former, latter, preferred_element_type=jnp.float32)


def low(values):
    return values.astype(jnp.bfloat16)


def wide(values):
    return values.astype(jnp.float32)


def other(values, axis, shift):
    count = lax.axis_size(axis)
    return lax.ppermute(values, axis, [(i, i ^ shift) for i in range(count)])


def trade(values, axis, split, concat):
    return lax.all_to_all(values, axis, split_axis=split, concat_axis=concat, tiled=True)


PLANE = ("dp", "core")


def swap_in(block):
    return trade(trade(block, "dp", 0, 0), "z", 0, 0)


def swap_out(block):
    return trade(trade(block, "z", 0, 0), "dp", 0, 0)


def plane_gather(block):
    pieces = [block] + [other(block, "dp", m) for m in range(1, lax.axis_size("dp"))]
    return [jnp.stack([piece, other(piece, "core", 1)]) for piece in pieces]


def plane_reduce(parts):
    sums = [part[0] + wide(other(low(part[1]), "core", 1)) for part in parts]
    total = sums[0]
    for m in range(1, len(sums)):
        total = total + wide(other(low(sums[m]), "dp", m))
    return total


def sum_blocks(parts, axis):
    return jnp.sum(wide(trade(low(parts), axis, 0, 0)), axis=0)


def fetch_heads(weight):
    rows = weight.shape[0]
    whole = lax.all_gather(weight, "z", axis=0, tiled=True)
    return trade(whole, "dp", 0, 0)


def return_heads(grad):
    planes = lax.axis_size("z")
    mine = trade(low(grad), "dp", 0, 0)
    return sum_blocks(mine.reshape((planes, mine.shape[0] // planes, mine.shape[1])), "z")


def fetch_square(weights):
    kinds, rows, width = weights.shape
    planes, cores, pieces = lax.axis_size("z"), lax.axis_size("core"), lax.axis_size("dp")
    core, piece = lax.axis_index("core"), lax.axis_index("dp")
    part = lax.all_gather(weights, "z", axis=1, tiled=False)
    pair = jnp.zeros((kinds, planes, cores, rows, width), weights.dtype)
    for shift, block in enumerate((part, other(part, "core", 1))):
        pair = lax.dynamic_update_slice(pair, block[:, :, None], (0, 0, core ^ shift, 0, 0))
    whole = jnp.zeros((kinds, planes, cores, rows, pieces * width), weights.dtype)
    for shift in range(pieces):
        block = pair if shift == 0 else other(pair, "dp", shift)
        whole = lax.dynamic_update_slice(whole, block, (0, 0, 0, 0, (piece ^ shift) * width))
    return whole.reshape(kinds, planes * cores * rows, pieces * width)


def return_square(grads):
    planes, cores, pieces = lax.axis_size("z"), lax.axis_size("core"), lax.axis_size("dp")
    kinds, rows, width = grads.shape
    split = low(grads).reshape(
        kinds, planes, cores, rows // (planes * cores), pieces, width // pieces
    )
    split = split.transpose(2, 4, 1, 0, 3, 5)
    for axis in ("core", "dp", "z"):
        split = sum_blocks(split, axis)
    return split


def fetch_units(expand, shrink):
    width = expand.shape[0] * lax.axis_size("dp")
    former = trade(expand, "dp", 1, 0).T
    latter = trade(shrink, "dp", 0, 1)
    whole = lax.all_gather(
        jnp.concatenate([former, latter], axis=1), "z", axis=0, tiled=True
    )
    return (whole[:, :width], whole[:, width:])


def return_units(expand_grad, shrink_grad):
    width = expand_grad.shape[1]
    both = low(jnp.concatenate([expand_grad, shrink_grad], axis=1))
    mine = lax.psum_scatter(both, "z", scatter_dimension=0, tiled=True)
    former = trade(mine[:, :width].T, "dp", 0, 1)
    latter = trade(mine[:, width:], "dp", 1, 0)
    return (wide(former), wide(latter))


def sum_all(values):
    for axis in ("core", "dp", "z"):
        shift = 1
        while shift < lax.axis_size(axis):
            values = values + other(values, axis, shift)
            shift *= 2
    return values


def document_edges(ids, memory_ids, steps):
    documents = jnp.arange(4, dtype=jnp.int32)
    starts = jnp.sum((memory_ids[None] < documents[:, None]).astype(jnp.int32), axis=1)
    ends = jnp.sum((memory_ids[None] <= documents[:, None]).astype(jnp.int32), axis=1) - 1
    match = ids[None] == documents[:, None]
    first = jnp.sum(jnp.where(match, starts[:, None], 0), axis=0)
    last = jnp.sum(jnp.where(match, ends[:, None], 0), axis=0)
    return (first.reshape(steps, 1, -1), last.reshape(steps, 1, -1))


def shards(
    inputs,
    encoder_states,
    segment_ids,
    encoder_ids,
    norm_gains,
    norm_shifts,
    attend_weights,
    attend_output,
    attend_biases,
    cross_query,
    cross_memory,
    cross_output,
    cross_biases,
    expand_weight,
    expand_bias,
    shrink_weight,
    shrink_bias,
    output_cotangent,
):
    pieces, planes, cores = lax.axis_size("dp"), lax.axis_size("z"), lax.axis_size("core")
    piece, plane, core = lax.axis_index("dp"), lax.axis_index("z"), lax.axis_index("core")
    members = pieces * cores
    member = piece * cores + core
    row_count, model_width = inputs.shape[1:]
    memory_rows = encoder_states.shape[1]
    pack_rows, pack_memory = segment_ids.shape[1], encoder_ids.shape[1]
    heads = HEADS // members
    head_size = model_width // HEADS
    width = heads * head_size
    steps = planes * cores
    unit_count = expand_weight.shape[1]

    swapping = [
        ((d * planes + z) * cores + c, (z * planes + d) * cores + c)
        for d in range(pieces)
        for z in range(planes)
        for c in range(cores)
    ]
    all_ids = lax.ppermute(
        jnp.concatenate([segment_ids[0], encoder_ids[0]]), ("dp", "z", "core"), swapping
    )
    pack_ids, memory_ids = all_ids[:pack_rows], all_ids[pack_rows:]
    raw = swap_in(inputs[0])
    attend_w = fetch_heads(attend_weights)
    attend_w = (
        attend_w.reshape(model_width, heads, 3, head_size)
        .transpose(0, 2, 1, 3)
        .reshape(model_width, 3 * width)
    )
    encoder = swap_in(encoder_states[0])
    cross_kv = fetch_heads(cross_memory)
    cross_kv = (
        cross_kv.reshape(model_width, heads, 2, head_size)
        .transpose(0, 2, 1, 3)
        .reshape(model_width, 2 * width)
    )
    squares = fetch_square(jnp.stack([attend_output, cross_query.T, cross_output]))
    attend_o, cross_qt, cross_o = squares[0], squares[1], squares[2]
    upstream = swap_in(output_cotangent[0])
    expand_t, shrink_w = fetch_units(expand_weight, shrink_weight)

    own = jnp.stack([piece, core]).astype(jnp.int32)
    key_block = min(256, pack_rows)
    self_first, _ = document_edges(pack_ids, pack_ids, steps)
    self_last = jnp.arange(pack_rows, dtype=jnp.int32).reshape(steps, 1, -1)
    self_scalars = jnp.concatenate(
        [own, self_first[:, 0, 0] // key_block, self_last[:, 0, -1] // key_block]
    )
    cross_first, cross_last = document_edges(pack_ids, memory_ids, steps)
    key_block = min(256, pack_memory)
    cross_scalars = jnp.concatenate(
        [own, cross_first[:, 0, 0] // key_block, cross_last[:, 0, -1] // key_block]
    )

    gain_rows, shift_rows = wide(norm_gains), wide(norm_shifts)
    bias_self, bias_cross = wide(attend_biases), wide(cross_biases)

    def of_heads(row):
        return lax.dynamic_slice_in_dim(row, member * width, width, 0)

    zero_heads = jnp.zeros((width,), jnp.float32)
    packed_bias = jnp.concatenate([of_heads(bias_self[0]), zero_heads, of_heads(bias_self[1])])
    memory_bias = jnp.concatenate([zero_heads, of_heads(bias_cross[1])])

    tokens = wide(raw)
    normed1, norm_back1 = jax.vjp(layer_norm, tokens, gain_rows[0], shift_rows[0])
    all_one = jnp.concatenate(plane_gather(low(normed1))).reshape(pack_rows, model_width)
    packed = low(product(all_one, attend_w) + packed_bias)
    packed = packed.reshape(pieces, cores, planes, row_count // planes, 3 * width)
    self_q, self_k, self_v = (pick(packed, i, width) for i in range(3))
    context1, kept1, lse1 = attend(
        self_scalars, self_q, self_k, self_v, self_first, self_last, width, True, True
    )
    mixed1 = trade(context1.reshape(pack_rows, width), PLANE, 0, 1)
    middle = tokens + product(mixed1, attend_o) + bias_self[2]

    all_encoder = jnp.concatenate(plane_gather(encoder)).reshape(pack_memory, model_width)
    memory = low(product(all_encoder, cross_kv) + memory_bias)
    memory = memory.reshape(pieces, cores, planes, memory_rows // planes, 2 * width)
    normed2, norm_back2 = jax.vjp(layer_norm, middle, gain_rows[1], shift_rows[1])
    low_two = low(normed2)
    query2 = trade(low(against(low_two, cross_qt) + bias_cross[0]), PLANE, 1, 0)
    query2 = query2.reshape(pieces, cores, planes, row_count // planes, width)
    cross_q = (query2, 0)
    cross_k, cross_v = (pick(memory, i, width) for i in range(2))
    context2, kept2, lse2 = attend(
        cross_scalars, cross_q, cross_k, cross_v, cross_first, cross_last, width, False, True
    )
    mixed2 = trade(context2.reshape(pack_rows, width), PLANE, 0, 1)
    later = middle + product(mixed2, cross_o) + bias_cross[2]

    bias_units = wide(expand_bias).reshape(planes, cores, pieces, unit_count // pieces)
    bias_units = lax.dynamic_slice(
        bias_units, (0, core, piece, 0), (planes, 1, 1, unit_count // pieces)
    ).reshape(unit_count)
    normed3, norm_back3 = jax.vjp(layer_norm, later, gain_rows[2], shift_rows[2])
    ups = plane_gather(upstream)
    threes = plane_gather(low(normed3))
    d_threes, outs, actives, d_hiddens = [], [], [], []
    for m in range(pieces):
        up_m = ups[m].reshape(cores * row_count, model_width)
        three_m = threes[m].reshape(cores * row_count, model_width)
        d_active = against(up_m, shrink_w)
        hidden = against(three_m, expand_t) + bias_units
        active, gelu_back = jax.vjp(jax.nn.gelu, hidden)
        d_hidden = low(gelu_back(d_active)[0])
        active = low(active)
        d_threes.append(product(d_hidden, expand_t).reshape(cores, row_count, model_width))
        outs.append(product(active, shrink_w).reshape(cores, row_count, model_width))
        actives.append(active)
        d_hiddens.append(d_hidden)
    d_normed3 = plane_reduce(d_threes)
    back_three = norm_back3(d_normed3)
    d_later = wide(upstream) + back_three[0]
    all_up = jnp.concatenate(ups).reshape(pack_rows, model_width)
    all_three = jnp.concatenate(threes).reshape(pack_rows, model_width)
    all_active, all_d_hidden = jnp.concatenate(actives), jnp.concatenate(d_hiddens)
    layer_output = swap_out(low(later + plane_reduce(outs) + wide(shrink_bias)))
    expand_sum, shrink_sum = return_units(
        inner_rows(all_d_hidden, all_three), inner_rows(all_active, all_up)
    )
    unit_sums = jnp.sum(wide(all_d_hidden), axis=0).reshape(planes, 1, 1, unit_count // pieces)
    unit_sums = lax.dynamic_update_slice(
        jnp.zeros((planes, cores, pieces, unit_count // pieces), jnp.float32),
        unit_sums,
        (0, core, piece, 0),
    ).reshape(-1)
    up_sums = jnp.sum(wide(upstream), axis=0)

    def place_heads(row):
        return lax.dynamic_update_slice(
            jnp.zeros((model_width,), jnp.float32), row, (member * width,)
        )

    low_later = low(d_later)
    d_context2 = trade(low(against(low_later, cross_o)), PLANE, 1, 0)
    d_context2 = d_context2.reshape(pieces, cores, planes, row_count // planes, width)
    d_query2, d_memory = attend_back(
        cross_scalars, cross_q, cross_k, cross_v, d_context2, kept2, lse2,
        cross_first, cross_last, width, False, True,
    )
    query_flat = trade(d_query2.reshape(pack_rows, width), PLANE, 0, 1)
    memory_flat = d_memory.reshape(pack_memory, 2 * width)
    d_normed2 = product(query_flat, cross_qt)
    back_two = norm_back2(d_normed2)
    d_middle = d_later + back_two[0]
    d_encoder = against(memory_flat, cross_kv).reshape(pieces, cores, memory_rows, model_width)
    encoder_gradient = swap_out(low(plane_reduce([d_encoder[m] for m in range(pieces)])))
    cross_squares = return_square(
        jnp.stack([inner_rows(query_flat, low_two), inner_rows(mixed2, low_later)])
    )
    cross_kv_grad = (
        inner_rows(all_encoder, memory_flat)
        .reshape(model_width, 2, heads, head_size)
        .transpose(0, 2, 1, 3)
        .reshape(model_width, 2 * width)
    )
    cross_kv_sum = return_heads(cross_kv_grad)
    cross_b_grad = jnp.stack(
        [
            jnp.sum(wide(query_flat), axis=0),
            place_heads(jnp.sum(wide(memory_flat[:, width:]), axis=0)),
            jnp.sum(wide(low_later), axis=0),
        ]
    )

    low_middle = low(d_middle)
    d_context1 = trade(low(against(low_middle, attend_o)), PLANE, 1, 0)
    d_context1 = d_context1.reshape(pieces, cores, planes, row_count // planes, width)
    attend_o_sum = return_square(inner_rows(mixed1, low_middle)[None])
    d_query1, d_memory1 = attend_back(
        self_scalars, self_q, self_k, self_v, d_context1, kept1, lse1,
        self_first, self_last, width, True, True,
    )
    d_packed = jnp.concatenate(
        [d_query1.reshape(pack_rows, width), d_memory1.reshape(pack_rows, 2 * width)], axis=1
    )
    d_ones = against(d_packed, attend_w).reshape(pieces, cores, row_count, model_width)
    d_normed1 = plane_reduce([d_ones[m] for m in range(pieces)])
    back_one = norm_back1(d_normed1)
    input_gradient = swap_out(low(d_middle + back_one[0]))
    attend_w_grad = (
        inner_rows(all_one, d_packed)
        .reshape(model_width, 3, heads, head_size)
        .transpose(0, 2, 1, 3)
        .reshape(model_width, 3 * width)
    )
    attend_w_sum = return_heads(attend_w_grad)

    early = jnp.concatenate(
        [
            back_two[1],
            back_three[1],
            back_two[2],
            back_three[2],
            jnp.sum(wide(low_middle), axis=0),
            cross_b_grad.reshape(-1),
            up_sums,
            unit_sums,
        ]
    )
    early = lax.psum(early.reshape(-1, 128), ("dp", "z", "core")).reshape(-1)
    head_sums = jnp.sum(wide(d_packed), axis=0)
    late = jnp.stack(
        [
            back_one[1],
            back_one[2],
            place_heads(head_sums[:width]),
            place_heads(head_sums[2 * width :]),
        ]
    )
    late = sum_all(late)
    rows = early[: 9 * model_width].reshape(9, model_width)
    gain_grads = jnp.stack([late[0], rows[0], rows[1]])
    shift_grads = jnp.stack([late[1], rows[2], rows[3]])
    attend_b_grad = jnp.stack([late[2], late[3], rows[4]])
    return (
        layer_output[None],
        input_gradient[None],
        encoder_gradient[None],
        gain_grads,
        shift_grads,
        attend_w_sum,
        attend_o_sum[0],
        attend_b_grad,
        cross_squares[0].T,
        cross_kv_sum,
        cross_squares[1],
        rows[5:8],
        expand_sum,
        early[9 * model_width :],
        shrink_sum,
        rows[8],
    )


def solution(mesh):
    pieces, sequence = mesh.devices.shape
    planes = Mesh(mesh.devices.reshape(pieces, sequence // 2, 2), ("dp", "z", "core"))
    seq = ("z", "core")
    in_specs = (
        P("dp", seq, None),
        P("dp", seq, None),
        P("dp", None),
        P("dp", None),
        P(),
        P(),
        P("dp", seq),
        P(seq, "dp"),
        P(),
        P("dp", seq),
        P("dp", seq),
        P(seq, "dp"),
        P(),
        P("dp", seq),
        P(),
        P(seq, "dp"),
        P(),
        P("dp", seq, None),
    )
    out_specs = (
        P("dp", seq, None),
        P("dp", seq, None),
        P("dp", seq, None),
        P(),
        P(),
        P("dp", seq),
        P(seq, "dp"),
        P(),
        P("dp", seq),
        P("dp", seq),
        P(seq, "dp"),
        P(),
        P("dp", seq),
        P(),
        P(seq, "dp"),
        P(),
    )
    return jax.shard_map(
        shards, mesh=planes, in_specs=in_specs, out_specs=out_specs, check_vma=False
    )
```

time: 1800 us -> 969 us (0.54)
  waiting for transfers between devices: 1060 us -> 327 us
  matrix products: 304 us -> 92.1 us
  starting transfers between devices: 55.3 us -> 195 us
  blocking collectives: 124 us -> 80.1 us
  Pallas kernels: 0 us -> 43.6 us
  loops' own time: 28.2 us -> 0 us
    reduce_scatter x10 -> x1, waiting for transfers between devices: 473 us -> 11.5 us  [return_units(): mine = lax.psum_scatter(both, 'z', scatter_dimension=0, tiled=True)]
    all_gather x8 -> x1, waiting for transfers between devices: 280 us -> 0.01 us  [fetch_units(): lax.all_gather(jnp.concatenate([former, latter], axis=1), 'z', axis=0, ti...]
    dot_general x63 -> x13, matrix products: 219 us -> 25 us  [product(): return jnp.dot(former, latter, preferred_element_type=jnp.float32)]
    ppermute x0 -> x66, waiting for transfers between devices: none -> 171 us  [the longest x65 171 us: other(): return lax.ppermute(values, axis, [(i, i ^ shift) for i in range(count)])]
    psum x1, waiting for transfers between devices: 131 us -> 0.02 us  [shards(): early = lax.psum(early.reshape(-1, 128), ('dp', 'z', 'core')).reshape(-1)]
    all_to_all x8 -> x31, starting transfers between devices: 53.8 us -> 151 us  [trade(): lax.all_to_all(values, axis, split_axis=split, concat_axis=concat, tiled=...]
    all_to_all x2 -> x3, blocking collectives: 74 us -> 26.8 us  [trade(): lax.all_to_all(values, axis, split_axis=split, concat_axis=concat, tiled=...]
    ppermute x0 -> x66, starting transfers between devices: none -> 43.6 us  [the longest x65 40.3 us: other(): return lax.ppermute(values, axis, [(i, i ^ shift) for i in range(count)])]
  transfers between devices with their start and end apart: 29 -> 100, of which waited for: 22 -> 37; matrix products, arithmetic and copies ran while one was open for 25% -> 27% of each run, Pallas kernels for 0% -> 3%
where the time goes in v1:
time: 969 us; the launch traced here: 958 us
  waiting for transfers between devices  327 us (34%)
  starting transfers between devices  195 us (20%)
  local copies, waits for them, and re-layouts  135 us (14%)
  matrix products  92.1 us (10%)
  blocking collectives  80.1 us (8%)
  other arithmetic  69.6 us (7%)
  Pallas kernels  43.6 us (4%)
  between operations  16.3 us (2%)
    ppermute x65, waiting for transfers between devices, other(): return lax.ppermute(values, axis, [(i, i ^ shift) for i in range(count)])  171 us
    all_to_all x31, starting transfers between devices, trade(): lax.all_to_all(values, axis, split_axis=split, concat_axis=concat, tiled=...  151 us
    all_to_all x31, waiting for transfers between devices, trade(): lax.all_to_all(values, axis, split_axis=split, concat_axis=concat, tiled=...  144 us
    unnamed x226, local copies, waits for them, and re-layouts  43.8 us
    ppermute x65, starting transfers between devices, other(): return lax.ppermute(values, axis, [(i, i ^ shift) for i in range(count)])  40.3 us
    dot_general x13, matrix products, against(): lax.dot_general(former, latter, (((1,), (1,)), ((), ())), preferred_eleme...  34.6 us
    all_gather x2, blocking collectives, fetch_heads(): whole = lax.all_gather(weight, 'z', axis=0, tiled=True)  33.8 us
    dot_general x7, matrix products, inner_rows(): lax.dot_general(former, latter, (((0,), (0,)), ((), ())), preferred_eleme...  32.4 us
  transfers between devices with their start and end apart: 100, of which 37 were waited for; matrix products, arithmetic and copies ran while one was open for 27% of the time, Pallas kernels for 3%

profile of v1, /device:TPU:8, one launch (start us, length us, event | category | flops | bytes accessed | tf_op | source)
XLA Modules:
  0.0 957.7 jit_solution(16842315281723864681)
XLA Ops:
  13.2 19.5 %all-gather = bf16[3,512,256]{2,1,0:T(8,128)(2,1)} all-gather(bf16[3,128,256]{2,1,0:T(8,128)(2,1)S(1)} %pad_maximum_fusion.14), channel_id=2, replica_groups=mesh['dp'=4,'z'=4,'core'=2] {'z'}, dimensions={1}, use_global_device_ids=true | all-gather | bytes 983040 | tf_op jit(solution)/shard_map/all_gather | solution.py:417
  37.2 16.5 %all_gather.18 = bf16[1024,256]{1,0:T(8,128)(2,1)S(1)} all-gather(bf16[256,256]{1,0:T(8,128)(2,1)S(1)} %copy-done.59), channel_id=1, replica_groups=mesh['dp'=4,'z'=4,'core'=2] {'z'}, dimensions={0}, use_global_device_ids=true | all-gather | bytes 655360 | tf_op jit(solution)/shard_map/all_gather | solution.py:403
  59.9 17.3 %all_gather.15 = bf16[1024,384]{1,0:T(8,128)(2,1)S(1)} all-gather(bf16[256,384]{1,0:T(8,128)(2,1)S(1)} %copy-done.56), channel_id=1, replica_groups=mesh['dp'=4,'z'=4,'core'=2] {'z'}, dimensions={0}, use_global_device_ids=true | all-gather | bytes 983040 | tf_op jit(solution)/shard_map/all_gather | solution.py:403
  153.8 29.9 %all-to-all-done.13 = bf16[4,64,1024]{2,1,0:T(8,128)(2,1)S(1)} async-done(((bf16[4,64,1024]{2,1,0:T(8,128)(2,1)}), bf16[4,64,1024]{2,1,0:T(8,128)(2,1)S(1)}, u32[]{:S(2)}, u32[]{:S(2)}) %all-to-all-start.13) | async-done | bytes 524320 | tf_op jit(solution)/shard_map/all_to_all | solution.py:370
  194.1 14.2 %all-to-all-done.1 = bf16[4,64,1024]{2,1,0:T(8,128)(2,1)S(1)} async-done(((bf16[4,64,1024]{2,1,0:T(8,128)(2,1)}), bf16[4,64,1024]{2,1,0:T(8,128)(2,1)S(1)}, u32[]{:S(2)}, u32[]{:S(2)}) %all-to-all-start.1) | async-done | bytes 524320 | tf_op jit(solution)/shard_map/all_to_all | solution.py:370
  244.8 9.8 %collective-permute-done.6 = bf16[256,1024]{1,0:T(8,128)(2,1)S(1)} collective-permute-done((bf16[256,1024]{1,0:T(8,128)(2,1)}, bf16[256,1024]{1,0:T(8,128)(2,1)S(1)}, u32[]{:S(2)}, u32[]{:S(2)}) %collective-permute-start.6) | collective-permute-done | bytes 524320 | tf_op jit(solution)/shard_map/ppermute | solution.py:366
  262.2 11.5 %shard_map.297 = (bf16[4,2,4,64,128]{4,3,2,1,0:T(8,128)(2,1)S(1)}, f32[8,128,256]{2,1,0:T(8,128)S(1)}, f32[8,1,512]{2,1,0:T(1,128)S(1)}) custom-call(s32[18]{0:T(128)S(1)} %pad_add_fusion.1.scalars, bf16[4,2,4,64,384]{4,3,2,1,0:T(8,128)(2,1)S(1)} %bitcast.363, bf16[4,2,4,64,384]{4,3,2,1,0:T(8,128)(2,1)S(1)} %bitcast.364, ...), custom_call_target="tpu_custom_call" | custom-call | tf_op jit(solution)/shard_map/pallas_call | solution.py:257
  279.9 63.7 %collective-permute-done.39 = bf16[256,1024]{1,0:T(8,128)(2,1)} collective-permute-done((bf16[256,1024]{1,0:T(8,128)(2,1)S(1)}, bf16[256,1024]{1,0:T(8,128)(2,1)}, u32[]{:S(2)}, u32[]{:S(2)}) %collective-permute-start.39) | collective-permute-done | bytes 524320 | tf_op jit(solution)/shard_map/ppermute | solution.py:366
  376.5 9.8 %shard_map.298 = (bf16[4,2,4,64,128]{4,3,2,1,0:T(8,128)(2,1)S(1)}, f32[8,128,256]{2,1,0:T(8,128)S(1)}, f32[8,1,512]{2,1,0:T(1,128)S(1)}) custom-call(s32[18]{0:T(128)S(1)} %pad_add_fusion.3.scalars, bf16[4,2,4,64,128]{4,3,2,1,0:T(8,128)(2,1)S(1)} %bitcast.376, bf16[4,2,4,32,256]{4,3,2,1,0:T(8,128)(2,1)S(1)} %bitcast.372, ...), custom_call_target="tpu_custom_call" | custom-call | tf_op jit(solution)/shard_map/pallas_call | solution.py:257
  420.5 11.1 %collective-permute-done.25 = bf16[256,1024]{1,0:T(8,128)(2,1)S(1)} collective-permute-done((bf16[256,1024]{1,0:T(8,128)(2,1)S(1)}, bf16[256,1024]{1,0:T(8,128)(2,1)S(1)}, u32[]{:S(2)}, u32[]{:S(2)}) %collective-permute-start.25) | collective-permute-done | bytes 524320 | tf_op jit(solution)/shard_map/ppermute | solution.py:366
  470.8 9.4 fusion.36
  486.7 8.8 convolution_convert_fusion
  521.6 11.8 %collective-permute-done.42 = bf16[256,1024]{1,0:T(8,128)(2,1)S(1)} collective-permute-done((bf16[256,1024]{1,0:T(8,128)(2,1)S(1)}, bf16[256,1024]{1,0:T(8,128)(2,1)S(1)}, u32[]{:S(2)}, u32[]{:S(2)}) %collective-permute-start.42) | collective-permute-done | bytes 524320 | tf_op jit(solution)/shard_map/ppermute | solution.py:366
  542.9 12.2 %collective-permute-done.28 = bf16[256,1024]{1,0:T(8,128)(2,1)S(1)} collective-permute-done((bf16[256,1024]{1,0:T(8,128)(2,1)S(1)}, bf16[256,1024]{1,0:T(8,128)(2,1)S(1)}, u32[]{:S(2)}, u32[]{:S(2)}) %collective-permute-start.28) | collective-permute-done | bytes 524320 | tf_op jit(solution)/shard_map/ppermute | solution.py:366
  573.5 10.1 %shard_map.299 = (bf16[4,2,4,64,128]{4,3,2,1,0:T(8,128)(2,1)S(1)}, bf16[4,2,4,32,256]{4,3,2,1,0:T(8,128)(2,1)S(1)}) custom-call(s32[18]{0:T(128)S(1)} %pad_add_fusion.3.scalars, bf16[4,2,4,64,128]{4,3,2,1,0:T(8,128)(2,1)S(1)} %bitcast.377, bf16[4,2,4,32,256]{4,3,2,1,0:T(8,128)(2,1)S(1)} %bitcast.374, bf16[4,2,4,32,256]{4,3,2,1,0:T(8,128)(2,1)S(1)} %bitcast.375, ...), custom_call_target="tpu_custom_call" | custom-call | tf_op jit(solution)/shard_map/pallas_call | solution.py:300
  606.0 9.3 all-to-all-start.11
  645.3 12.0 %all_to_all.335 = bf16[2,4,4,2,128,256]{5,4,1,2,3,0:T(8,128)(2,1)} all-to-all(bf16[2,4,4,2,128,256]{5,4,1,2,3,0:T(8,128)(2,1)} %copy.260), channel_id=1, replica_groups=mesh['dp'=4,'z'=4,'core'=2] {'core'}, dimensions={0} | all-to-all | bytes 8388608 | tf_op jit(solution)/shard_map/all_to_all | solution.py:370
  721.3 12.1 %shard_map.300 = (bf16[4,2,4,64,128]{4,3,2,1,0:T(8,128)(2,1)S(1)}, bf16[4,2,4,64,256]{4,3,2,1,0:T(8,128)(2,1)S(1)}) custom-call(s32[18]{0:T(128)S(1)} %copy-done.12, bf16[4,2,4,64,384]{4,3,2,1,0:T(8,128)(2,1)S(1)} %bitcast.366, bf16[4,2,4,64,384]{4,3,2,1,0:T(8,128)(2,1)S(1)} %bitcast.367, bf16[4,2,4,64,384]{4,3,2,1,0:T(8,128)(2,1)S(1)} %bitcast.368, ...), custom_call_target="tpu_custom_call" | custom-call | tf_op jit(solution)/shard_map/pallas_call | solution.py:300
  796.5 12.6 %all-to-all-done.28 = bf16[4,4,2,128,256]{4,3,1,2,0:T(8,128)(2,1)} async-done(((bf16[4,4,2,128,256]{4,3,1,2,0:T(8,128)(2,1)}), bf16[4,4,2,128,256]{4,3,1,2,0:T(8,128)(2,1)}, u32[]{:S(2)}, u32[]{:S(2)}) %all-to-all-start.28) | async-done | bytes 2097184 | tf_op jit(solution)/shard_map/all_to_all | solution.py:370
  820.3 8.9 collective-permute-done.53
  838.8 12.7 %all-to-all-start.18 = ((bf16[4,64,1024]{2,1,0:T(8,128)(2,1)}), bf16[4,64,1024]{2,1,0:T(8,128)(2,1)}, u32[]{:S(2)}, u32[]{:S(2)}) async-start(bf16[4,64,1024]{2,1,0:T(8,128)(2,1)} %bitcast.113), calls=%async_computation.18 | async-start | bytes 1048576 | tf_op jit(solution)/shard_map/all_to_all | solution.py:370
  857.2 18.1 %all-to-all-done.18 = bf16[4,64,1024]{2,1,0:T(8,128)(2,1)} async-done(((bf16[4,64,1024]{2,1,0:T(8,128)(2,1)}), bf16[4,64,1024]{2,1,0:T(8,128)(2,1)}, u32[]{:S(2)}, u32[]{:S(2)}) %all-to-all-start.18) | async-done | bytes 524320 | tf_op jit(solution)/shard_map/all_to_all | solution.py:370
  888.0 9.4 collective-permute-done.64
  909.2 11.5 %reduce-scatter.2.cloned.1.call-done = bf16[256,2048]{0,1:T(8,128)(2,1)} async-done(((bf16[1024,2048]{0,1:T(8,128)(2,1)}), bf16[256,2048]{0,1:T(8,128)(2,1)}) %reduce-scatter.2.cloned.1.call-update) | async-done | bytes 1048592 | tf_op jit(solution)/shard_map/reduce_scatter | solution.py:453
  (631 shorter events, 579.2 us)
Async XLA Ops:
  8.0 76.0 %collective-permute-start = (s32[3072]{0:T(1024)S(1)}, s32[3072]{0:T(1024)S(1)}, u32[]{:S(2)}, u32[]{:S(2)}) collective-permute-start(s32[3072]{0:T(1024)S(1)} %pad_add_fusion), channel_id=1, source_target_pairs={{0,0},{1,1},{2,8},{3,9},{4,16},{5,17},{6,24},{7,25},{8,2},{9,3},{1... | collective-permute-start | bytes 36872 | tf_op jit(solution)/shard_map/ppermute | solution.py:517
  32.7 104.3 %collective-permute-start.8 = (bf16[3,4,128,256]{3,2,1,0:T(8,128)(2,1)}, bf16[3,4,128,256]{3,2,1,0:T(8,128)(2,1)}, u32[]{:S(2)}, u32[]{:S(2)}) collective-permute-start(bf16[3,4,128,256]{3,2,1,0:T(8,128)(2,1)} %bitcast.32), channel_id=1, source_target_pairs={{0,1},{1,0},{2,3},{3,2},{4,5},{5,4},{6,7},{7,6},{8,9},{9,8},{10,11... | collective-permute-start | bytes 2359304 | tf_op jit(solution)/shard_map/ppermute | solution.py:366
  113.2 329.1 %all-gather.3.cloned.1.call-start = ((), (), s32[]{:S(2)}) async-start(), calls=%async_computation.35 | async-start | bytes 5242880 | tf_op jit(solution)/shard_map/all_gather | solution.py:444
  138.2 205.9 %collective-permute-start.9 = (bf16[3,4,2,128,256]{4,3,2,1,0:T(8,128)(2,1)S(1)}, bf16[3,4,2,128,256]{4,3,2,1,0:T(8,128)(2,1)}, u32[]{:S(2)}, u32[]{:S(2)}) collective-permute-start(bf16[3,4,2,128,256]{4,3,2,1,0:T(8,128)(2,1)S(1)} %bitcast_dynamic-update-slice_fusion), channel_id=1, source_target_pairs={{0,8},{8,0},{16,24},{24,16},{1,9},{9,1},{17,25},{25,17},{2,10},{10... | collective-permute-start | bytes 4718600 | tf_op jit(solution)/shard_map/ppermute | solution.py:366
  144.9 42.8 %collective-permute-start.16 = (bf16[128,1024]{1,0:T(8,128)(2,1)}, bf16[128,1024]{1,0:T(8,128)(2,1)}, u32[]{:S(2)}, u32[]{:S(2)}) collective-permute-start(bf16[128,1024]{1,0:T(8,128)(2,1)} %collective-permute-done.15), channel_id=1, source_target_pairs={{0,1},{1,0},{2,3},{3,2},{4,5},{5,4},{6,7},{7,6},{8,9},{9,8},{10,11... | collective-permute-start | bytes 786440 | tf_op jit(solution)/shard_map/ppermute | solution.py:366
  145.5 44.7 %collective-permute-start.18 = (bf16[128,1024]{1,0:T(8,128)(2,1)S(1)}, bf16[128,1024]{1,0:T(8,128)(2,1)}, u32[]{:S(2)}, u32[]{:S(2)}) collective-permute-start(bf16[128,1024]{1,0:T(8,128)(2,1)S(1)} %collective-permute-done.17), channel_id=1, source_target_pairs={{0,1},{1,0},{2,3},{3,2},{4,5},{5,4},{6,7},{7,6},{8,9},{9,8},{10,11... | collective-permute-start | bytes 786440 | tf_op jit(solution)/shard_map/ppermute | solution.py:366
  236.1 110.9 %collective-permute-start.10 = (bf16[3,4,2,128,256]{4,3,2,1,0:T(8,128)(2,1)S(1)}, bf16[3,4,2,128,256]{4,3,2,1,0:T(8,128)(2,1)}, u32[]{:S(2)}, u32[]{:S(2)}) collective-permute-start(bf16[3,4,2,128,256]{4,3,2,1,0:T(8,128)(2,1)S(1)} %bitcast_dynamic-update-slice_fusion), channel_id=1, source_target_pairs={{0,16},{8,24},{16,0},{24,8},{1,17},{9,25},{17,1},{25,9},{2,18},{10... | collective-permute-start | bytes 4718600 | tf_op jit(solution)/shard_map/ppermute | solution.py:366
  254.7 95.1 %collective-permute-start.11 = (bf16[3,4,2,128,256]{4,3,2,1,0:T(8,128)(2,1)S(1)}, bf16[3,4,2,128,256]{4,3,2,1,0:T(8,128)(2,1)}, u32[]{:S(2)}, u32[]{:S(2)}) collective-permute-start(bf16[3,4,2,128,256]{4,3,2,1,0:T(8,128)(2,1)S(1)} %bitcast_dynamic-update-slice_fusion), channel_id=1, source_target_pairs={{0,24},{8,16},{16,8},{24,0},{1,25},{9,17},{17,9},{25,1},{2,26},{10... | collective-permute-start | bytes 4718600 | tf_op jit(solution)/shard_map/ppermute | solution.py:366
  257.4 86.2 %collective-permute-start.39 = (bf16[256,1024]{1,0:T(8,128)(2,1)S(1)}, bf16[256,1024]{1,0:T(8,128)(2,1)}, u32[]{:S(2)}, u32[]{:S(2)}) collective-permute-start(bf16[256,1024]{1,0:T(8,128)(2,1)S(1)} %bitcast.404), channel_id=1, source_target_pairs={{0,16},{8,24},{16,0},{24,8},{1,17},{9,25},{17,1},{25,9},{2,18},{10... | collective-permute-start | bytes 1572872 | tf_op jit(solution)/shard_map/ppermute | solution.py:366
  259.0 84.6 %collective-permute-start.43 = (bf16[256,1024]{1,0:T(8,128)(2,1)S(1)}, bf16[256,1024]{1,0:T(8,128)(2,1)}, u32[]{:S(2)}, u32[]{:S(2)}) collective-permute-start(bf16[256,1024]{1,0:T(8,128)(2,1)S(1)} %bitcast.405), channel_id=1, source_target_pairs={{0,24},{8,16},{16,8},{24,0},{1,25},{9,17},{17,9},{25,1},{2,26},{10... | collective-permute-start | bytes 1572872 | tf_op jit(solution)/shard_map/ppermute | solution.py:366
  275.7 82.6 %all-to-all-start.3 = ((bf16[8,256,128]{1,2,0:T(8,128)(2,1)}), bf16[8,256,128]{1,2,0:T(8,128)(2,1)}, u32[]{:S(2)}, u32[]{:S(2)}) async-start(bf16[8,256,128]{1,2,0:T(8,128)(2,1)} %copy.238), calls=%async_computation.3 | async-start | bytes 1048576 | tf_op jit(solution)/shard_map/all_to_all | solution.py:370
  344.1 65.1 %collective-permute-start.44 = (bf16[256,1024]{1,0:T(8,128)(2,1)}, bf16[256,1024]{1,0:T(8,128)(2,1)}, u32[]{:S(2)}, u32[]{:S(2)}) collective-permute-start(bf16[256,1024]{1,0:T(8,128)(2,1)} %collective-permute-done.43), channel_id=1, source_target_pairs={{0,1},{1,0},{2,3},{3,2},{4,5},{5,4},{6,7},{7,6},{8,9},{9,8},{10,11... | collective-permute-start | bytes 1572872 | tf_op jit(solution)/shard_map/ppermute | solution.py:366
  456.3 46.2 %collective-permute-start.23 = (bf16[256,1024]{1,0:T(8,128)(2,1)}, bf16[256,1024]{1,0:T(8,128)(2,1)}, u32[]{:S(2)}, u32[]{:S(2)}) collective-permute-start(bf16[256,1024]{1,0:T(8,128)(2,1)} %slice.623), channel_id=1, source_target_pairs={{0,1},{1,0},{2,3},{3,2},{4,5},{5,4},{6,7},{7,6},{8,9},{9,8},{10,11... | collective-permute-start | bytes 1572872 | tf_op jit(solution)/shard_map/ppermute | solution.py:366
  458.5 49.6 %collective-permute-start.27 = (bf16[256,1024]{1,0:T(8,128)(2,1)}, bf16[256,1024]{1,0:T(8,128)(2,1)}, u32[]{:S(2)}, u32[]{:S(2)}) collective-permute-start(bf16[256,1024]{1,0:T(8,128)(2,1)} %slice.622), channel_id=1, source_target_pairs={{0,1},{1,0},{2,3},{3,2},{4,5},{5,4},{6,7},{7,6},{8,9},{9,8},{10,11... | collective-permute-start | bytes 1572872 | tf_op jit(solution)/shard_map/ppermute | solution.py:366
  461.2 49.7 %collective-permute-start.31 = (bf16[256,1024]{1,0:T(8,128)(2,1)}, bf16[256,1024]{1,0:T(8,128)(2,1)}, u32[]{:S(2)}, u32[]{:S(2)}) collective-permute-start(bf16[256,1024]{1,0:T(8,128)(2,1)} %slice.621), channel_id=1, source_target_pairs={{0,1},{1,0},{2,3},{3,2},{4,5},{5,4},{6,7},{7,6},{8,9},{9,8},{10,11... | collective-permute-start | bytes 1572872 | tf_op jit(solution)/shard_map/ppermute | solution.py:366
  465.7 38.6 %collective-permute-start.37 = (bf16[256,1024]{1,0:T(8,128)(2,1)}, bf16[256,1024]{1,0:T(8,128)(2,1)}, u32[]{:S(2)}, u32[]{:S(2)}) collective-permute-start(bf16[256,1024]{1,0:T(8,128)(2,1)} %slice.619), channel_id=1, source_target_pairs={{0,1},{1,0},{2,3},{3,2},{4,5},{5,4},{6,7},{7,6},{8,9},{9,8},{10,11... | collective-permute-start | bytes 1572872 | tf_op jit(solution)/shard_map/ppermute | solution.py:366
  470.8 41.4 %collective-permute-start.34 = (bf16[256,1024]{1,0:T(8,128)(2,1)}, bf16[256,1024]{1,0:T(8,128)(2,1)}, u32[]{:S(2)}, u32[]{:S(2)}) collective-permute-start(bf16[256,1024]{1,0:T(8,128)(2,1)} %slice.620), channel_id=1, source_target_pairs={{0,1},{1,0},{2,3},{3,2},{4,5},{5,4},{6,7},{7,6},{8,9},{9,8},{10,11... | collective-permute-start | bytes 1572872 | tf_op jit(solution)/shard_map/ppermute | solution.py:366
  596.0 85.1 %collective-permute-start.54 = (bf16[128,1024]{1,0:T(8,128)(2,1)}, bf16[128,1024]{1,0:T(8,128)(2,1)S(1)}, u32[]{:S(2)}, u32[]{:S(2)}) collective-permute-start(bf16[128,1024]{1,0:T(8,128)(2,1)} %get-tuple-element.204), channel_id=1, source_target_pairs={{0,1},{1,0},{2,3},{3,2},{4,5},{5,4},{6,7},{7,6},{8,9},{9,8},{10,11... | collective-permute-start | bytes 786440 | tf_op jit(solution)/shard_map/ppermute | solution.py:366
  602.5 78.6 %collective-permute-start.56 = (bf16[128,1024]{1,0:T(8,128)(2,1)}, bf16[128,1024]{1,0:T(8,128)(2,1)}, u32[]{:S(2)}, u32[]{:S(2)}) collective-permute-start(bf16[128,1024]{1,0:T(8,128)(2,1)} %get-tuple-element.197), channel_id=1, source_target_pairs={{0,8},{8,0},{16,24},{24,16},{1,9},{9,1},{17,25},{25,17},{2,10},{10... | collective-permute-start | bytes 786440 | tf_op jit(solution)/shard_map/ppermute | solution.py:366
  604.5 76.6 %collective-permute-start.58 = (bf16[128,1024]{1,0:T(8,128)(2,1)}, bf16[128,1024]{1,0:T(8,128)(2,1)}, u32[]{:S(2)}, u32[]{:S(2)}) collective-permute-start(bf16[128,1024]{1,0:T(8,128)(2,1)} %get-tuple-element.199), channel_id=1, source_target_pairs={{0,16},{8,24},{16,0},{24,8},{1,17},{9,25},{17,1},{25,9},{2,18},{10... | collective-permute-start | bytes 786440 | tf_op jit(solution)/shard_map/ppermute | solution.py:366
  605.9 75.2 %collective-permute-start.60 = (bf16[128,1024]{1,0:T(8,128)(2,1)}, bf16[128,1024]{1,0:T(8,128)(2,1)}, u32[]{:S(2)}, u32[]{:S(2)}) collective-permute-start(bf16[128,1024]{1,0:T(8,128)(2,1)} %get-tuple-element.198), channel_id=1, source_target_pairs={{0,24},{8,16},{16,8},{24,0},{1,25},{9,17},{17,9},{25,1},{2,26},{10... | collective-permute-start | bytes 786440 | tf_op jit(solution)/shard_map/ppermute | solution.py:366
  680.3 172.6 %all-reduce.3.cloned.1.call-start = ((), (), s32[]{:S(2)}) async-start(), calls=%async_computation.36 | async-start | bytes 139264 | tf_op jit(solution)/shard_map/psum | solution.py:700
  695.1 225.7 %reduce-scatter.2.cloned.1.call-start = ((), (), s32[]{:S(2)}) async-start(), calls=%async_computation.37 | async-start | bytes 5242880 | tf_op jit(solution)/shard_map/reduce_scatter | solution.py:453
  838.8 36.5 %all-to-all-start.18 = ((bf16[4,64,1024]{2,1,0:T(8,128)(2,1)}), bf16[4,64,1024]{2,1,0:T(8,128)(2,1)}, u32[]{:S(2)}, u32[]{:S(2)}) async-start(bf16[4,64,1024]{2,1,0:T(8,128)(2,1)} %bitcast.113), calls=%async_computation.18 | async-start | bytes 1048576 | tf_op jit(solution)/shard_map/all_to_all | solution.py:370
  (169 other events, 3065.2 us)
Sparse Core Ops, SparseCore 0:
  124.2 87.8 all-gather.2
  687.3 125.4 all-reduce.2
  815.1 105.5 reduce-scatter.1

commit v2 on v1

v2 whole, which is shorter than its diff:
```python
import functools
import math

import jax
import jax.numpy as jnp
from jax import lax
from jax.experimental import pallas as pl
from jax.experimental.pallas import tpu as pltpu
from jax.sharding import Mesh
from jax.sharding import PartitionSpec as P

HEADS = 16

epsilon = 1e-05
masked_score = -1e30
head_width = 64


def head_columns(transposed, heads):
    if heads == 1:
        return transposed
    feature = lax.broadcasted_iota(jnp.int32, transposed.shape, 0) // head_width
    zero = jnp.zeros_like(transposed)
    return jnp.concatenate([jnp.where(feature == h, transposed, zero) for h in range(heads)], axis=1)


def head_rows(block, heads):
    if heads == 1:
        return block
    feature = lax.broadcasted_iota(jnp.int32, block.shape, 1) // head_width
    zero = jnp.zeros_like(block)
    return jnp.concatenate([jnp.where(feature == h, block, zero) for h in range(heads)], axis=0)


def flip(block):
    return jnp.transpose(block.astype(jnp.float32), (1, 0)).astype(block.dtype)


def repeat_heads(row, heads):
    return row if heads == 1 else jnp.concatenate([row] * heads, axis=1)


def project(scalars, mine_ref, theirs_ref, weight_ref, bias_ref, out_refs, width):
    weight = weight_ref[...]
    bias = bias_ref[...]
    for j, source in enumerate((mine_ref, theirs_ref)):
        for m in range(source.shape[0]):
            rows = bias + lax.dot_general(
                source[m], weight, (((1,), (1,)), ((), ())), preferred_element_type=jnp.float32
            )
            rows = rows.astype(jnp.bfloat16)
            for i, out_ref in enumerate(out_refs):
                out_ref[j, m] = rows[:, i * width : (i + 1) * width]


def natural_blocks(scalars, shape, planes):
    cores, pieces, rows = shape[:3]
    part = rows // planes
    for plane in range(planes):
        for core in range(cores):
            slots = [
                ((core ^ scalars[0], piece ^ scalars[1]), plane * part) for piece in range(pieces)
            ]
            if planes == 1:
                for piece in range(pieces):
                    yield (piece * cores + core) * rows, rows, slots[piece : piece + 1]
            else:
                yield (plane * cores + core) * pieces * part, part, slots


def take_rows(ref, part, slots):
    blocks = [ref[slot[0], slot[1], first : first + part] for slot, first in slots]
    return blocks[0] if len(blocks) == 1 else jnp.concatenate(blocks, axis=0)


def query_rows_of(ref, flip_by=0):
    return jnp.concatenate([ref[0, piece ^ flip_by, 0] for piece in range(ref.shape[1])], axis=0)


def put_query_rows(ref, block, flip_by=0):
    part = ref.shape[3]
    for piece in range(ref.shape[1]):
        ref[0, piece ^ flip_by, 0] = block[piece * part : (piece + 1) * part]


def attend_rows(scalars, query, first_ref, last_ref, keys, flipped, heads, key_block):
    step = pl.program_id(0)
    steps = pl.num_programs(0)
    rows = query.shape[0]
    query = query * jnp.asarray(1.0 / math.sqrt(head_width), jnp.bfloat16)
    columns = head_columns(flip(query), heads)
    first = repeat_heads(first_ref[0], heads)
    last = repeat_heads(last_ref[0], heads)

    def one(block, carry):
        peak, total, sums = carry
        start = pl.multiple_of(block * key_block, key_block)
        scores = jnp.dot(keys[pl.ds(start, key_block), :], columns, preferred_element_type=jnp.float32)
        place = start + lax.broadcasted_iota(jnp.int32, scores.shape, 0)
        scores = jnp.where((place >= first) & (place <= last), scores, masked_score)
        newer = jnp.maximum(peak, jnp.max(scores, axis=0, keepdims=True))
        shrink = jnp.exp(peak - newer)
        exponent = jnp.exp(scores - newer)
        total = total * shrink + jnp.sum(exponent, axis=0, keepdims=True)
        low_part = exponent.astype(jnp.bfloat16)
        turned = flipped[block]
        fresh = []
        for h in range(heads):
            part = jnp.dot(
                turned[h * head_width : (h + 1) * head_width],
                low_part[:, h * rows : (h + 1) * rows],
                preferred_element_type=jnp.float32,
            )
            fresh.append(sums[h] * shrink[:, h * rows : (h + 1) * rows] + part)
        return (newer, total, tuple(fresh))

    empty = (
        jnp.full((1, heads * rows), masked_score, jnp.float32),
        jnp.zeros((1, heads * rows), jnp.float32),
        tuple(jnp.zeros((head_width, rows), jnp.float32) for _ in range(heads)),
    )
    peak, total, sums = lax.fori_loop(scalars[2 + step], scalars[2 + steps + step] + 1, one, empty)
    context = jnp.concatenate(
        [sums[h] / total[:, h * rows : (h + 1) * rows] for h in range(heads)], axis=0
    )
    return context, peak + jnp.log(total)


def prepare(scalars, k_ref, v_ref, keys, flipped, key_block, planes):
    for start, part, slots in natural_blocks(scalars, k_ref.shape, planes):
        rows = part * len(slots)
        keys[start : start + rows, :] = take_rows(k_ref, part, slots)
        offset = start % key_block
        flipped[start // key_block, :, offset : offset + rows] = flip(take_rows(v_ref, part, slots))


def finish_forward(context, lse, ctx_ref, keep_ref, lse_ref):
    keep_ref[0] = context
    lse_ref[0] = lse
    put_query_rows(ctx_ref, jnp.transpose(context, (1, 0)).astype(jnp.bfloat16))


def self_forward_kernel(
    scalars, mine_ref, theirs_ref, weight_ref, bias_ref, first_ref, last_ref,
    q_ref, k_ref, v_ref, ctx_ref, keep_ref, lse_ref, keys, flipped,
    *, heads, key_block, planes,
):
    step = pl.program_id(0)
    cores, pieces, rows = q_ref.shape[:3]
    part = rows // planes

    @pl.when(step == 0)
    def _():
        outs = (q_ref, k_ref, v_ref)
        project(scalars, mine_ref, theirs_ref, weight_ref, bias_ref, outs, heads * head_width)
        prepare(scalars, k_ref, v_ref, keys, flipped, key_block, planes)

    core = lax.rem(step, cores) ^ scalars[0]
    here = pl.ds(pl.multiple_of(lax.div(step, cores) * part, part), part)
    query = jnp.concatenate(
        [q_ref[core, piece ^ scalars[1], here, :] for piece in range(pieces)], axis=0
    )
    context, lse = attend_rows(
        scalars, query, first_ref, last_ref, keys, flipped, heads, key_block
    )
    finish_forward(context, lse, ctx_ref, keep_ref, lse_ref)


def cross_forward_kernel(
    scalars, q_ref, mine_ref, theirs_ref, weight_ref, bias_ref, first_ref, last_ref,
    k_ref, v_ref, ctx_ref, keep_ref, lse_ref, keys, flipped,
    *, heads, key_block,
):
    @pl.when(pl.program_id(0) == 0)
    def _():
        outs = (k_ref, v_ref)
        project(scalars, mine_ref, theirs_ref, weight_ref, bias_ref, outs, heads * head_width)
        prepare(scalars, k_ref, v_ref, keys, flipped, key_block, 1)

    context, lse = attend_rows(
        scalars, query_rows_of(q_ref), first_ref, last_ref, keys, flipped, heads, key_block
    )
    finish_forward(context, lse, ctx_ref, keep_ref, lse_ref)


def backward_kernel(
    scalars, q_ref, k_ref, v_ref, dc_ref, keep_ref, lse_ref, first_ref, last_ref,
    *rest, heads, key_block, planes, near,
):
    if near:
        dq_ref, dqt_ref, dkv_ref, dkvt_ref, keys, values, flipped, dkeys, dvalues = rest
    else:
        dq_ref, dkv_ref, dkvt_ref, keys, values, flipped, dkeys, dvalues = rest
    step = pl.program_id(0)
    steps = pl.num_programs(0)
    width = heads * head_width
    scaling = 1.0 / math.sqrt(head_width)

    @pl.when(step == 0)
    def _():
        prepare(scalars, k_ref, k_ref, keys, flipped, key_block, planes)
        for start, part, slots in natural_blocks(scalars, v_ref.shape, planes):
            values[start : start + part * len(slots), :] = take_rows(v_ref, part, slots)
        dkeys[...] = jnp.zeros_like(dkeys)
        dvalues[...] = jnp.zeros_like(dvalues)

    flip_by = scalars[1] if near else 0
    query = query_rows_of(q_ref, flip_by) * jnp.asarray(scaling, jnp.bfloat16)
    rows = query.shape[0]
    grad = query_rows_of(dc_ref)
    turned_grad = flip(grad)
    query_columns = head_columns(flip(query), heads)
    grad_columns = head_columns(turned_grad, heads)
    query_rows = head_rows(query, heads)
    grad_rows = head_rows(grad, heads)
    dots_kept = turned_grad.astype(jnp.float32) * keep_ref[0]
    center = jnp.concatenate(
        [
            jnp.sum(dots_kept[h * head_width : (h + 1) * head_width], axis=0, keepdims=True)
            for h in range(heads)
        ],
        axis=1,
    )
    first = repeat_heads(first_ref[0], heads)
    last = repeat_heads(last_ref[0], heads)
    lse = lse_ref[0]

    def one(block, sums):
        start = pl.multiple_of(block * key_block, key_block)
        here = pl.ds(start, key_block)
        scores = jnp.dot(keys[here, :], query_columns, preferred_element_type=jnp.float32)
        place = start + lax.broadcasted_iota(jnp.int32, scores.shape, 0)
        scores = jnp.where((place >= first) & (place <= last), scores, masked_score)
        weights = jnp.exp(scores - lse)
        dots = jnp.dot(values[here, :], grad_columns, preferred_element_type=jnp.float32)
        dscore = (weights * (dots - center)).astype(jnp.bfloat16)
        dvalues[here, :] += jnp.dot(
            weights.astype(jnp.bfloat16), grad_rows, preferred_element_type=jnp.float32
        )
        dkeys[here, :] += jnp.dot(dscore, query_rows, preferred_element_type=jnp.float32)
        turned = flipped[block]
        return tuple(
            sums[h]
            + jnp.dot(
                turned[h * head_width : (h + 1) * head_width],
                dscore[:, h * rows : (h + 1) * rows],
                preferred_element_type=jnp.float32,
            )
            for h in range(heads)
        )

    empty = tuple(jnp.zeros((head_width, rows), jnp.float32) for _ in range(heads))
    sums = lax.fori_loop(scalars[2 + step], scalars[2 + steps + step] + 1, one, empty)
    dquery = jnp.concatenate(sums, axis=0) * scaling
    dquery = jnp.transpose(dquery, (1, 0)).astype(jnp.bfloat16)
    if near:
        core = lax.rem(step, dq_ref.shape[0]) ^ scalars[0]
        plane = lax.div(step, dq_ref.shape[0])
        part = dq_ref.shape[3]
        for piece in range(dq_ref.shape[1]):
            dq_ref[core, piece ^ flip_by, plane] = dquery[piece * part : (piece + 1) * part]
    else:
        put_query_rows(dq_ref, dquery)

    @pl.when(step == steps - 1)
    def _():
        cores, pieces, key_rows = k_ref.shape[:3]
        for start, part, slots in natural_blocks(scalars, k_ref.shape, planes):
            for i, (slot, first) in enumerate(slots):
                here = slice(start + i * part, start + (i + 1) * part)
                for column, total in ((0, dkeys), (width, dvalues)):
                    dkv_ref[slot[0], slot[1], first : first + part, column : column + width] = (
                        total[here, :].astype(jnp.bfloat16)
                    )
        for j in range(cores):
            for m in range(pieces):
                place = (j * pieces + m) * key_rows
                dkvt_ref[:, place : place + key_rows] = flip(dkv_ref[j, m])
                if near:
                    block = dq_ref[j, m].reshape(key_rows, width)
                    dqt_ref[:, place : place + key_rows] = flip(block)


def whole_spec(shape, index=None):
    index = (0,) * len(shape) if index is None else index
    return pl.BlockSpec(shape, lambda step, scalars: index)


def step_spec(shape):
    return pl.BlockSpec((1,) + shape[1:], lambda step, scalars: (step, 0, 0))


def member_spec(shape, near):
    cores, pieces = shape[:2]

    def place(step, scalars):
        core = lax.rem(step, cores)
        return (core ^ scalars[0] if near else core, 0, lax.div(step, cores), 0, 0)

    return pl.BlockSpec((1, pieces, 1) + shape[3:], place)


def forward_outputs(shape):
    cores, pieces, planes, rows, width = shape
    steps = cores * planes
    heads = width // head_width
    shapes = [
        jax.ShapeDtypeStruct(shape, jnp.bfloat16),
        jax.ShapeDtypeStruct((steps, width, pieces * rows), jnp.float32),
        jax.ShapeDtypeStruct((steps, 1, heads * pieces * rows), jnp.float32),
    ]
    specs = [member_spec(shape, False), step_spec(shapes[1].shape), step_spec(shapes[2].shape)]
    return shapes, specs


def cost(microseconds):
    return pl.CostEstimate(
        flops=int(microseconds * 1.1e9), bytes_accessed=1 << 20, transcendentals=0
    )


def params():
    return pltpu.CompilerParams(vmem_limit_bytes=36 * 2**20)


def self_forward(scalars, mine, theirs, planes, weight, bias, first, last):
    pieces, rows, model_width = mine.shape
    width = weight.shape[0] // 3
    shape = (2, pieces, rows, width)
    steps = 2 * planes
    key_count = 2 * pieces * rows
    key_block = min(256, key_count)
    shapes, specs = forward_outputs((2, pieces, planes, rows // planes, width))
    full = jax.ShapeDtypeStruct(shape, jnp.bfloat16)
    return pl.pallas_call(
        functools.partial(
            self_forward_kernel, heads=width // head_width, key_block=key_block, planes=planes
        ),
        grid_spec=pltpu.PrefetchScalarGridSpec(
            num_scalar_prefetch=1,
            grid=(steps,),
            in_specs=[
                whole_spec(mine.shape),
                whole_spec(theirs.shape),
                whole_spec(weight.shape),
                whole_spec(bias.shape),
                step_spec(first.shape),
                step_spec(last.shape),
            ],
            out_specs=[whole_spec(shape)] * 3 + specs,
            scratch_shapes=[
                pltpu.VMEM((key_count, width), jnp.bfloat16),
                pltpu.VMEM((key_count // key_block, width, key_block), jnp.bfloat16),
            ],
        ),
        out_shape=[full] * 3 + shapes,
        compiler_params=params(),
        cost_estimate=cost(16),
    )(scalars, mine, theirs, weight, bias, first, last)


def cross_forward(scalars, queries, mine, theirs, weight, bias, first, last):
    cores, pieces, planes, rows, width = queries.shape
    state_rows = mine.shape[1]
    steps = cores * planes
    key_count = cores * pieces * state_rows
    key_block = min(256, key_count)
    shapes, specs = forward_outputs(queries.shape)
    key_shape = (cores, pieces, state_rows, width)
    full = jax.ShapeDtypeStruct(key_shape, jnp.bfloat16)
    return pl.pallas_call(
        functools.partial(cross_forward_kernel, heads=width // head_width, key_block=key_block),
        grid_spec=pltpu.PrefetchScalarGridSpec(
            num_scalar_prefetch=1,
            grid=(steps,),
            in_specs=[
                member_spec(queries.shape, False),
                whole_spec(mine.shape),
                whole_spec(theirs.shape),
                whole_spec(weight.shape),
                whole_spec(bias.shape),
                step_spec(first.shape),
                step_spec(last.shape),
            ],
            out_specs=[whole_spec(key_shape)] * 2 + specs,
            scratch_shapes=[
                pltpu.VMEM((key_count, width), jnp.bfloat16),
                pltpu.VMEM((key_count // key_block, width, key_block), jnp.bfloat16),
            ],
        ),
        out_shape=[full] * 2 + shapes,
        compiler_params=params(),
        cost_estimate=cost(11),
    )(scalars, queries, mine, theirs, weight, bias, first, last)


def attend_back(scalars, queries, key_rows, values, grad, kept, lse, first, last, near):
    cores, pieces, planes, rows, width = queries.shape
    steps = cores * planes
    key_shape = key_rows.shape
    key_count = cores * pieces * key_shape[2]
    key_block = min(256, key_count)
    dq_shape = jax.ShapeDtypeStruct(queries.shape, jnp.bfloat16)
    if near:
        dq_shapes = [dq_shape, jax.ShapeDtypeStruct((width, key_count), jnp.bfloat16)]
        dq_specs = [whole_spec(queries.shape), whole_spec((width, key_count))]
    else:
        dq_shapes, dq_specs = [dq_shape], [member_spec(queries.shape, False)]
    return pl.pallas_call(
        functools.partial(
            backward_kernel,
            heads=width // head_width,
            key_block=key_block,
            planes=planes if near else 1,
            near=near,
        ),
        grid_spec=pltpu.PrefetchScalarGridSpec(
            num_scalar_prefetch=1,
            grid=(steps,),
            in_specs=[
                member_spec(queries.shape, near),
                whole_spec(key_shape),
                whole_spec(key_shape),
                member_spec(grad.shape, False),
                step_spec(kept.shape),
                step_spec(lse.shape),
                step_spec(first.shape),
                step_spec(last.shape),
            ],
            out_specs=dq_specs
            + [whole_spec(key_shape[:3] + (2 * width,)), whole_spec((2 * width, key_count))],
            scratch_shapes=[
                pltpu.VMEM((key_count, width), jnp.bfloat16),
                pltpu.VMEM((key_count, width), jnp.bfloat16),
                pltpu.VMEM((key_count // key_block, width, key_block), jnp.bfloat16),
                pltpu.VMEM((key_count, width), jnp.float32),
                pltpu.VMEM((key_count, width), jnp.float32),
            ],
        ),
        out_shape=dq_shapes
        + [
            jax.ShapeDtypeStruct(key_shape[:3] + (2 * width,), jnp.bfloat16),
            jax.ShapeDtypeStruct((2 * width, key_count), jnp.bfloat16),
        ],
        compiler_params=params(),
        cost_estimate=cost(12),
    )(scalars, queries, key_rows, values, grad, kept, lse, first, last)


def single(kernel, out_shape, in_specs, scratch, *args):
    return pl.pallas_call(
        kernel,
        grid_spec=pltpu.PrefetchScalarGridSpec(
            num_scalar_prefetch=1,
            grid=(1,),
            in_specs=[
                whole_spec(value.shape) if spec is None else spec
                for spec, value in zip(in_specs, args[1:])
            ],
            out_specs=[whole_spec(value.shape) for value in out_shape],
            scratch_shapes=scratch,
        ),
        out_shape=out_shape,
        compiler_params=params(),
        cost_estimate=cost(4),
    )(*args)


def kind_spec(array, kind):
    shape = (array.shape[0], array.shape[1], 1) + array.shape[3:]
    return whole_spec(shape, (0, 0, kind, 0, 0))


def square_block(ref, m):
    block = ref[m, :, 0]
    return block.reshape(block.shape[0] * block.shape[1], block.shape[2])


def heads_of(ref, core):
    return jnp.concatenate([ref[core, piece] for piece in range(ref.shape[1])], axis=1)


def near_span(scalars, m, size):
    return pl.ds(pl.multiple_of((scalars[1] ^ m) * size, size), size)


def heads_to_model(scalars, heads_ref, mine_ref, theirs_ref, sums):
    mine, theirs = heads_of(heads_ref, scalars[0]), heads_of(heads_ref, 1 ^ scalars[0])
    size = mine_ref.shape[4]
    for m in range(mine_ref.shape[0]):
        sums[:, near_span(scalars, m, size)] = jnp.dot(
            mine, square_block(mine_ref, m), preferred_element_type=jnp.float32
        ) + jnp.dot(theirs, square_block(theirs_ref, m), preferred_element_type=jnp.float32)


def model_to_heads(scalars, rows_ref, mine_ref, theirs_ref, heads_ref, bias_ref=None):
    size = mine_ref.shape[4]
    pieces, width = heads_ref.shape[1], heads_ref.shape[3]
    for j, weight_ref in enumerate((mine_ref, theirs_ref)):
        total = 0.0
        for m in range(weight_ref.shape[0]):
            total = total + lax.dot_general(
                rows_ref[:, near_span(scalars, m, size)],
                square_block(weight_ref, m),
                (((1,), (1,)), ((), ())),
                preferred_element_type=jnp.float32,
            )
        core = scalars[0] ^ j
        for piece in range(pieces):
            block = total[:, piece * width : (piece + 1) * width]
            if bias_ref is not None:
                block = block + bias_ref[core, piece]
            heads_ref[core, piece] = block.astype(jnp.bfloat16)


def normal_parts(values):
    center = values - jnp.mean(values, axis=-1, keepdims=True)
    spread = jnp.mean(center * center, axis=-1, keepdims=True)
    scale = lax.rsqrt(spread + epsilon)
    return center * scale, scale


def norm_back(values, gain, dn):
    normal, scale = normal_parts(values)
    e = dn * gain
    dv = scale * (
        e
        - jnp.mean(e, axis=-1, keepdims=True)
        - normal * jnp.mean(e * normal, axis=-1, keepdims=True)
    )
    return (
        dv,
        jnp.sum(dn * normal, axis=0, keepdims=True),
        jnp.sum(dn, axis=0, keepdims=True),
    )


def middle_kernel(
    scalars, heads_ref, omine_ref, otheirs_ref, resid_ref, rows_ref, qmine_ref, qtheirs_ref,
    qbias_ref, sum_ref, norm_ref, q_ref,
):
    heads_to_model(scalars, heads_ref, omine_ref, otheirs_ref, sum_ref)
    total = sum_ref[...] + resid_ref[...].astype(jnp.float32) + rows_ref[0:1]
    sum_ref[...] = total
    normal, _ = normal_parts(total)
    norm_ref[...] = (normal * rows_ref[1:2] + rows_ref[2:3]).astype(jnp.bfloat16)
    model_to_heads(scalars, norm_ref, qmine_ref, qtheirs_ref, q_ref, qbias_ref)


def later_kernel(
    scalars, heads_ref, omine_ref, otheirs_ref, resid_ref, rows_ref, sum_ref, norm_ref
):
    heads_to_model(scalars, heads_ref, omine_ref, otheirs_ref, sum_ref)
    total = sum_ref[...] + resid_ref[...] + rows_ref[0:1]
    sum_ref[...] = total
    normal, _ = normal_parts(total)
    norm_ref[...] = (normal * rows_ref[1:2] + rows_ref[2:3]).astype(jnp.bfloat16)


def finish_back(scalars, values_ref, rows_ref, dn, upper, mine_ref, theirs_ref, d_ref, low_ref, heads_ref, sums_ref):
    dv, dg, db = norm_back(values_ref[...], rows_ref[0:1], dn)
    total = upper + dv
    d_ref[...] = total
    low_total = total.astype(jnp.bfloat16)
    low_ref[...] = low_total
    sums_ref[0:1] = dg
    sums_ref[1:2] = db
    sums_ref[2:3] = jnp.sum(low_total.astype(jnp.float32), axis=0, keepdims=True)
    model_to_heads(scalars, low_ref, mine_ref, theirs_ref, heads_ref)


def later_back_kernel(scalars, *refs):
    parts, (up_ref, values_ref, rows_ref, mine_ref, theirs_ref) = refs[:-9], refs[-9:-4]
    dn = parts[0][...].reshape(up_ref.shape)
    for part in parts[1:]:
        dn = dn + part[...].reshape(up_ref.shape).astype(jnp.float32)
    upper = up_ref[...].astype(jnp.float32)
    finish_back(scalars, values_ref, rows_ref, dn, upper, mine_ref, theirs_ref, *refs[-4:])


def middle_back_kernel(
    scalars, heads_ref, qmine_ref, qtheirs_ref, upper_ref, values_ref, rows_ref, mine_ref,
    theirs_ref, d_ref, low_ref, dheads_ref, sums_ref, work,
):
    heads_to_model(scalars, heads_ref, qmine_ref, qtheirs_ref, work)
    finish_back(
        scalars, values_ref, rows_ref, work[...], upper_ref[...], mine_ref, theirs_ref,
        d_ref, low_ref, dheads_ref, sums_ref,
    )


def input_back_kernel(scalars, *refs):
    parts, (upper_ref, values_ref, rows_ref, out_ref, sums_ref) = refs[:-5], refs[-5:]
    dn = parts[0][...].reshape(upper_ref.shape)
    for part in parts[1:]:
        dn = dn + part[...].reshape(upper_ref.shape).astype(jnp.float32)
    dv, dg, db = norm_back(values_ref[...].astype(jnp.float32), rows_ref[0:1], dn)
    out_ref[...] = (upper_ref[...] + dv).astype(jnp.bfloat16)
    sums_ref[0:1] = dg
    sums_ref[1:2] = db


def square_grad_kernel(scalars, *refs):
    kinds = (len(refs) - 2) // 2
    mine_ref, theirs_ref = refs[-2:]
    size = mine_ref.shape[4]
    for kind in range(kinds):
        heads_ref, rows_ref = refs[2 * kind], refs[2 * kind + 1]
        for j, out_ref in enumerate((mine_ref, theirs_ref)):
            for piece in range(heads_ref.shape[1]):
                turned = flip(heads_ref[scalars[0] ^ j, piece])
                for m in range(out_ref.shape[0]):
                    out_ref[m, piece, kind] = jnp.dot(
                        turned,
                        rows_ref[:, near_span(scalars, m, size)],
                        preferred_element_type=jnp.float32,
                    ).astype(out_ref.dtype)


def gelu_parts(u):
    root = math.sqrt(2.0 / math.pi)
    square = u * u
    bent = jnp.tanh(root * (u + 0.044715 * (square * u)))
    half = 0.5 * (1.0 + bent)
    slope = half + 0.5 * u * (1.0 - bent * bent) * (root * (1.0 + 3.0 * 0.044715 * square))
    return u * half, slope


def units_kernel(
    scalars, mine_ref, theirs_ref, upmine_ref, uptheirs_ref, expand_ref, shrink_ref, bias_ref,
    active_ref, dhidden_ref, dmine_ref, dtheirs_ref, half_count,
):
    step = pl.program_id(0)
    expand, shrink = expand_ref[...], shrink_ref[...]
    against_last = (((1,), (1,)), ((), ()))

    def one(rows, up):
        hidden = lax.dot_general(rows, expand, against_last, preferred_element_type=jnp.float32)
        dactive = lax.dot_general(up, shrink, against_last, preferred_element_type=jnp.float32)
        active, slope = gelu_parts(hidden + bias_ref[...])
        dhidden = (dactive * slope).astype(jnp.bfloat16)
        active_ref[0, 0] = active.astype(jnp.bfloat16)
        dhidden_ref[0, 0] = dhidden
        return jnp.dot(dhidden, expand, preferred_element_type=jnp.float32)

    @pl.when(step < half_count)
    def _():
        dtheirs_ref[0] = one(theirs_ref[0], uptheirs_ref[0]).astype(jnp.bfloat16)

    @pl.when(step >= half_count)
    def _():
        dmine_ref[0] = one(mine_ref[0], upmine_ref[0])


def units_group(scalars, mine, theirs, ups, start, expand_t, shrink_w, bias):
    count, rows, model_width = mine.shape
    units = expand_t.shape[0]

    def piece_spec(own, offset=0):
        if own:
            place = lambda step, scalars: (jnp.maximum(step - count, 0) + offset, 0, 0)
        else:
            place = lambda step, scalars: (jnp.minimum(step, count - 1) + offset, 0, 0)
        return pl.BlockSpec((1, rows, model_width), place)

    def table_place(step, scalars):
        return (1 - lax.div(step, count), lax.rem(step, count), 0, 0)

    table = jax.ShapeDtypeStruct((2, count, rows, units), jnp.bfloat16)
    table_spec = pl.BlockSpec((1, 1, rows, units), table_place)
    return pl.pallas_call(
        functools.partial(units_kernel, half_count=count),
        grid_spec=pltpu.PrefetchScalarGridSpec(
            num_scalar_prefetch=1,
            grid=(2 * count,),
            in_specs=[
                piece_spec(True),
                piece_spec(False),
                piece_spec(True, start),
                piece_spec(False, start),
                whole_spec(expand_t.shape),
                whole_spec(shrink_w.shape),
                whole_spec(bias.shape),
            ],
            out_specs=[table_spec, table_spec, piece_spec(True), piece_spec(False)],
        ),
        out_shape=[
            table,
            table,
            jax.ShapeDtypeStruct(mine.shape, jnp.float32),
            jax.ShapeDtypeStruct(mine.shape, jnp.bfloat16),
        ],
        compiler_params=params(),
        cost_estimate=cost(6.5 * count),
    )(scalars, mine, theirs, *ups, expand_t, shrink_w, bias)


def unit_gradients_kernel(scalars, *refs, counts):
    dhidden_refs, active_refs = refs[0:2], refs[2:4]
    row_refs, up_refs = (refs[4:6], refs[6:8]), refs[8:10]
    out_ref, expand_sum, shrink_sum = refs[10:]
    step = pl.program_id(0)
    width = expand_sum.shape[1]

    @pl.when(step == 0)
    def _():
        expand_sum[...] = jnp.zeros_like(expand_sum)
        shrink_sum[...] = jnp.zeros_like(shrink_sum)

    def add(group, core):
        for table_ref, rows_ref, total in (
            (dhidden_refs[group], row_refs[group][core], expand_sum),
            (active_refs[group], up_refs[core], shrink_sum),
        ):
            total[...] += lax.dot_general(
                table_ref[0, 0],
                rows_ref[0],
                (((0,), (0,)), ((), ())),
                preferred_element_type=jnp.float32,
            )

    first = 0
    for group, count in enumerate(counts):
        for core in range(2):
            @pl.when((step >= first) & (step < first + count))
            def _(group=group, core=core):
                add(group, core)

            first += count

    @pl.when(step == pl.num_programs(0) - 1)
    def _():
        out_ref[:, :width] = expand_sum[...].astype(jnp.bfloat16)
        out_ref[:, width:] = shrink_sum[...].astype(jnp.bfloat16)


def unit_gradients(scalars, dhiddens, actives, rows, ups):
    counts = [table.shape[1] for table in actives]
    _, _, tokens, units = actives[0].shape
    model_width = ups[0].shape[2]
    starts = [2 * sum(counts[:i]) for i in range(len(counts))]

    def table_spec(group):
        count, start = counts[group], starts[group]

        def place(step, scalars):
            here = jnp.clip(step - start, 0, 2 * count - 1)
            return (lax.div(here, count), lax.rem(here, count), 0, 0)

        return pl.BlockSpec((1, 1, tokens, units), place)

    def row_place(group, core):
        count, start = counts[group], starts[group] + core * counts[group]
        return pl.BlockSpec(
            (1, tokens, model_width),
            lambda step, scalars: (jnp.clip(step - start, 0, count - 1), 0, 0),
        )

    def up_place(core):
        def place(step, scalars):
            here = 0
            for i in range(len(counts)):
                inside = jnp.clip(step - starts[i] - core * counts[i], 0, counts[i] - 1)
                begun = (step >= starts[i] + core * counts[i]).astype(jnp.int32)
                here = jnp.where(begun == 1, sum(counts[:i]) + inside, here)
            return (here, 0, 0)

        return pl.BlockSpec((1, tokens, model_width), place)

    return pl.pallas_call(
        functools.partial(unit_gradients_kernel, counts=counts),
        grid_spec=pltpu.PrefetchScalarGridSpec(
            num_scalar_prefetch=1,
            grid=(2 * sum(counts),),
            in_specs=[table_spec(0), table_spec(1), table_spec(0), table_spec(1)]
            + [row_place(0, 0), row_place(0, 1), row_place(1, 0), row_place(1, 1)]
            + [up_place(0), up_place(1)],
            out_specs=whole_spec((units, 2 * model_width)),
            scratch_shapes=[pltpu.VMEM((units, model_width), jnp.float32)] * 2,
        ),
        out_shape=jax.ShapeDtypeStruct((units, 2 * model_width), jnp.bfloat16),
        compiler_params=params(),
        cost_estimate=cost(12),
    )(scalars, *dhiddens, *actives, *rows[0], *rows[1], *ups)


def layer_norm(values, gain_row, shift_row):
    center = values - jnp.mean(values, axis=-1, keepdims=True)
    spread = jnp.mean(center * center, axis=-1, keepdims=True)
    return center * lax.rsqrt(spread + epsilon) * gain_row + shift_row


def inner_rows(former, latter):
    return lax.dot_general(
        former, latter, (((0,), (0,)), ((), ())), preferred_element_type=jnp.float32
    )


def against(former, latter):
    return lax.dot_general(
        former, latter, (((1,), (1,)), ((), ())), preferred_element_type=jnp.float32
    )


def product(former, latter):
    return jnp.dot(former, latter, preferred_element_type=jnp.float32)


def low(values):
    return values.astype(jnp.bfloat16)


def wide(values):
    return values.astype(jnp.float32)


def other(values, axis, shift):
    count = lax.axis_size(axis)
    return lax.ppermute(values, axis, [(i, i ^ shift) for i in range(count)])


def trade(values, axis, split, concat):
    return lax.all_to_all(values, axis, split_axis=split, concat_axis=concat, tiled=True)


def after(values, *earlier):
    return lax.optimization_barrier((values, earlier))[0]


PLANE = ("core", "dp")


def chips_gather(block, axis="dp"):
    return [block] + [other(block, axis, m) for m in range(1, lax.axis_size(axis))]


def plane_gather(block):
    mine = jnp.stack(chips_gather(block))
    return mine, other(mine, "core", 1)


def plane_reduce(mine, theirs):
    sums = mine + wide(other(low(theirs), "core", 1))
    total = sums[0]
    for m in range(1, sums.shape[0]):
        total = total + wide(other(low(sums[m]), "dp", m))
    return total


def swap_planes(values, hop=0):
    pieces, planes, cores = (lax.axis_size(axis) for axis in ("dp", "z", "core"))
    pairs = [
        (((d ^ hop) * planes + z) * cores + c, (z * planes + d) * cores + c)
        for d in range(pieces)
        for z in range(planes)
        for c in range(cores)
    ]
    return lax.ppermute(values, ("dp", "z", "core"), pairs)


def swap_in(rows):
    return trade(trade(rows, "dp", 0, 0), "z", 0, 0)


def put_blocks(blocks, axis, dimension):
    size = blocks[0].shape[dimension]
    shape = list(blocks[0].shape)
    shape[dimension] = size * len(blocks)
    whole = jnp.zeros(shape, blocks[0].dtype)
    for m, block in enumerate(blocks):
        start = [0] * len(shape)
        start[dimension] = (lax.axis_index(axis) ^ m) * size
        whole = lax.dynamic_update_slice(whole, block, start)
    return whole


def sum_all(values):
    for axis in ("core", "dp", "z"):
        shift = 1
        while shift < lax.axis_size(axis):
            values = values + other(values, axis, shift)
            shift *= 2
    return values


def document_edges(ids, memory_ids, steps):
    documents = jnp.arange(4, dtype=jnp.int32)
    starts = jnp.sum((memory_ids[None] < documents[:, None]).astype(jnp.int32), axis=1)
    ends = jnp.sum((memory_ids[None] <= documents[:, None]).astype(jnp.int32), axis=1) - 1
    match = ids[None] == documents[:, None]
    first = jnp.sum(jnp.where(match, starts[:, None], 0), axis=0)
    last = jnp.sum(jnp.where(match, ends[:, None], 0), axis=0)
    return (first.reshape(steps, 1, -1), last.reshape(steps, 1, -1))


def shards(
    inputs,
    encoder_states,
    segment_ids,
    encoder_ids,
    norm_gains,
    norm_shifts,
    attend_weights,
    attend_output,
    attend_biases,
    cross_query,
    cross_memory,
    cross_output,
    cross_biases,
    expand_weight,
    expand_bias,
    shrink_weight,
    shrink_bias,
    output_cotangent,
):
    pieces, planes, cores = lax.axis_size("dp"), lax.axis_size("z"), lax.axis_size("core")
    piece, plane, core = lax.axis_index("dp"), lax.axis_index("z"), lax.axis_index("core")
    members = pieces * cores
    member = core * pieces + piece
    row_count, model_width = inputs.shape[1:]
    memory_rows = encoder_states.shape[1]
    pack_rows, pack_memory = segment_ids.shape[1], encoder_ids.shape[1]
    heads = HEADS // members
    head_size = model_width // HEADS
    width = heads * head_size
    steps = planes * cores
    unit_count = expand_weight.shape[1]
    block_units = unit_count // pieces
    block_rows = model_width // pieces

    all_ids = swap_planes(jnp.concatenate([segment_ids[0], encoder_ids[0]]))
    pack_ids, memory_ids = all_ids[:pack_rows], all_ids[pack_rows:]
    raw = swap_in(inputs[0])

    def columns_of(weight, count):
        weight = weight.reshape(pieces, heads, count, head_size, block_rows)
        return weight.transpose(2, 1, 3, 0, 4).reshape(count * width, model_width)

    near_w = jnp.concatenate(
        [attend_weights.T, cross_memory.T, attend_output, cross_query.T, cross_output]
    )
    near_w = lax.all_gather(near_w, "z", axis=0, tiled=False)
    heads_w = near_w[:, : 5 * width].reshape(planes * 5 * width, block_rows)
    upstream = swap_in(after(output_cotangent[0], raw))
    heads_w = trade(after(heads_w, upstream), "dp", 0, 0).reshape(pieces, 5 * width, block_rows)
    squares = near_w[:, 5 * width :].reshape(planes, 3, width, block_rows)
    unit_w = jnp.stack([expand_weight.T, shrink_weight], axis=1)
    unit_parts = []
    for m in range(pieces):
        part = lax.dynamic_slice_in_dim(unit_w, (piece ^ m) * block_units, block_units, 0)
        unit_parts.append(part if m == 0 else other(part, "dp", m))
    unit_w = put_blocks(unit_parts, "dp", 2).reshape(block_units, 2 * model_width)
    states = swap_planes(after(encoder_states[0], raw))
    whole_units = lax.all_gather(after(unit_w, states), "z", axis=0, tiled=True)
    expand_t, shrink_w = whole_units[:, :model_width], whole_units[:, model_width:]
    attend_w = columns_of(heads_w[:, : 3 * width], 3)
    cross_kv = columns_of(heads_w[:, 3 * width :], 2)

    own = jnp.stack([core, piece]).astype(jnp.int32)
    key_block = min(256, pack_rows)
    self_first, _ = document_edges(pack_ids, pack_ids, steps)
    self_last = jnp.arange(pack_rows, dtype=jnp.int32).reshape(steps, 1, -1)
    self_scalars = jnp.concatenate(
        [own, self_first[:, 0, 0] // key_block, self_last[:, 0, -1] // key_block]
    )
    cross_first, cross_last = document_edges(pack_ids, memory_ids, steps)
    key_block = min(256, pack_memory)
    cross_scalars = jnp.concatenate(
        [own, cross_first[:, 0, 0] // key_block, cross_last[:, 0, -1] // key_block]
    )

    gain_rows, shift_rows = wide(norm_gains), wide(norm_shifts)
    bias_self, bias_cross = wide(attend_biases), wide(cross_biases)

    def of_heads(row):
        return lax.dynamic_slice_in_dim(row, (piece * cores + core) * width, width, 0)

    def place_heads(row):
        return lax.dynamic_update_slice(
            jnp.zeros((model_width,), jnp.float32), row, ((piece * cores + core) * width,)
        )

    zero_heads = jnp.zeros((width,), jnp.float32)
    packed_bias = jnp.concatenate([of_heads(bias_self[0]), zero_heads, of_heads(bias_self[1])])
    memory_bias = jnp.concatenate([zero_heads, of_heads(bias_cross[1])])
    query_bias = bias_cross[0].reshape(pieces, cores, 1, width).transpose(1, 0, 2, 3)
    token_shape = (cores, pieces, row_count, width)
    part_shape = (cores, pieces, planes, row_count // planes, width)
    flat_shape = (row_count, model_width)
    flat_float = jax.ShapeDtypeStruct(flat_shape, jnp.float32)
    flat_low = jax.ShapeDtypeStruct(flat_shape, jnp.bfloat16)
    head_low = jax.ShapeDtypeStruct(token_shape, jnp.bfloat16)
    three_rows = jax.ShapeDtypeStruct((3, model_width), jnp.float32)

    def exchange(values):
        return trade(values.reshape(pieces * cores * row_count, width), PLANE, 0, 0).reshape(
            token_shape
        )

    low_one = low(layer_norm(wide(raw), gain_rows[0], shift_rows[0]))
    mine = jnp.stack(chips_gather(after(low_one, unit_w)))
    squares = after(squares, heads_w, mine)
    ones = (mine, other(mine, "core", 1))
    square_parts = chips_gather(squares)
    query1, key1, value1, context1, kept1, lse1 = self_forward(
        self_scalars, *ones, planes, attend_w, packed_bias[None], self_first, self_last
    )
    context1, square_parts = after((context1, square_parts))
    squares = jnp.stack(square_parts)
    squares = (squares, other(squares, "core", 1))
    mixed1 = exchange(context1)
    all_states = jnp.stack(chips_gather(after(states, mixed1)))
    all_states = (all_states, other(all_states, "core", 1))
    middle, low_two, query2 = single(
        middle_kernel,
        [flat_float, flat_low, head_low],
        [None, kind_spec(squares[0], 0), kind_spec(squares[1], 0), None, None]
        + [kind_spec(squares[0], 1), kind_spec(squares[1], 1), None],
        [],
        own, mixed1, *squares, raw,
        jnp.stack([bias_self[2], gain_rows[1], shift_rows[1]]),
        *squares, query_bias,
    )

    query2 = exchange(query2)
    query2 = query2.reshape(part_shape)
    key2, value2, context2, kept2, lse2 = cross_forward(
        cross_scalars, query2, *all_states, cross_kv, memory_bias[None],
        cross_first, cross_last,
    )
    ups = chips_gather(after(upstream, query2))
    context2, ups = after((context2, ups))
    ups = jnp.stack(ups)
    all_ups = (ups, other(ups, "core", 1))
    context2 = after(context2, whole_units)
    mixed2 = exchange(context2)
    later, low_three = single(
        later_kernel,
        [flat_float, flat_low],
        [None, kind_spec(squares[0], 2), kind_spec(squares[1], 2), None, None],
        [],
        own, mixed2, *squares, middle,
        jnp.stack([bias_cross[2], gain_rows[2], shift_rows[2]]),
    )

    bias_units = wide(expand_bias).reshape(planes, cores, pieces, block_units)
    bias_units = lax.dynamic_slice(
        bias_units, (0, core, piece, 0), (planes, 1, 1, block_units)
    ).reshape(1, unit_count)
    groups = [list(range(pieces - 1)), [pieces - 1]]
    pieces3 = chips_gather(low_three)
    threes, actives, d_hiddens, parts3, leaving = [], [], [], [], []
    for group in groups:
        mine = jnp.stack([pieces3[m] for m in group])
        if d_hiddens:
            mine = after(mine, d_hiddens[-1])
        theirs = other(mine, "core", 1)
        active, d_hidden, d_mine, d_theirs = units_group(
            own, mine, theirs, all_ups, group[0], expand_t, shrink_w, bias_units
        )
        d_sum = d_mine + wide(other(d_theirs, "core", 1))
        for i, m in enumerate(group):
            leaving.append(d_sum[i] if m == 0 else low(d_sum[i]))
            parts3.append(leaving[-1] if m == 0 else other(leaving[-1], "dp", m))
        threes.append((mine, theirs))
        actives.append(active)
        d_hiddens.append(d_hidden)
    actives, d_hiddens = after((actives, d_hiddens), leaving)

    unit_grads = unit_gradients(own, d_hiddens, actives, threes, all_ups)
    unit_grads, parts3 = after((unit_grads, parts3))
    unit_grads = lax.psum_scatter(unit_grads, "z", scatter_dimension=0, tiled=True)
    unit_sums = sum(jnp.sum(wide(d), axis=(0, 1, 2)) for d in d_hiddens)
    d_later, low_later, d_context2, sums3 = single(
        later_back_kernel,
        [flat_float, flat_low, head_low, three_rows],
        [None] * (pieces + 3) + [kind_spec(squares[0], 2), kind_spec(squares[1], 2)],
        [],
        own, *parts3, upstream, later, gain_rows[2:3], *squares,
    )

    actives = after(actives, low_later)
    outs = [
        jnp.concatenate(
            [
                product(active[j].reshape(-1, unit_count), shrink_w).reshape(
                    len(group), row_count, model_width
                )
                for group, active in zip(groups, actives)
            ]
        )
        for j in range(cores)
    ]
    outs = outs[0] + wide(other(low(outs[1]), "core", 1))

    d_context2 = exchange(d_context2)
    leaving = after([low(out) for out in outs[1:]], d_context2)
    out_parts = [other(out, "dp", m + 1) for m, out in enumerate(leaving)]
    d_query2, d_memory, d_memory_t = attend_back(
        cross_scalars, query2, key2, value2, d_context2.reshape(part_shape), kept2, lse2,
        cross_first, cross_last, False,
    )
    d_mixed2 = exchange(after(d_query2, out_parts))
    layer_rows = low(later + outs[0] + sum(wide(part) for part in out_parts) + wide(shrink_bias))
    d_middle, low_middle, d_context1, sums2 = single(
        middle_back_kernel,
        [flat_float, flat_low, head_low, three_rows],
        [None, kind_spec(squares[0], 1), kind_spec(squares[1], 1), None, None, None]
        + [kind_spec(squares[0], 0), kind_spec(squares[1], 0)],
        [pltpu.VMEM(flat_shape, jnp.float32)],
        own, d_mixed2, *squares, d_later, middle, gain_rows[1:2], *squares,
    )
    d_context1, unit_grads = after((exchange(d_context1), unit_grads))
    layer_rows = after(layer_rows, unit_grads)
    layer_first = trade(layer_rows, "z", 0, 0)
    unit_grads = unit_grads.reshape(block_units, 2, pieces, block_rows).transpose(2, 0, 1, 3)
    unit_grads = trade(unit_grads.reshape(unit_count, 2, block_rows), "dp", 0, 0)
    d_states = [
        product(part.reshape(-1, 2 * width), cross_kv).reshape(pieces, memory_rows, model_width)
        for part in after(d_memory, d_context1)
    ]
    d_states = d_states[0] + wide(other(low(d_states[1]), "core", 1))
    leaving = [low(d_states[m]) for m in range(1, pieces)]
    state_parts = [other(part, "dp", m + 1) for m, part in enumerate(leaving)]

    d_query1, d_query1_t, d_memory1, d_memory1_t = attend_back(
        self_scalars, query1.reshape(part_shape), key1, value1, d_context1.reshape(part_shape), kept1, lse1,
        self_first, self_last, True,
    )
    kinds = 3
    square_shape = (pieces, planes, kinds, width, block_rows)
    square_mine, square_theirs = single(
        square_grad_kernel,
        [
            jax.ShapeDtypeStruct(square_shape, jnp.bfloat16),
            jax.ShapeDtypeStruct(square_shape, jnp.bfloat16),
        ],
        [None] * 6,
        [],
        own, mixed1, after(low_middle, d_context1), d_mixed2, low_two, mixed2, low_later,
    )
    square_theirs = other(square_theirs, "core", 1)
    square_sums = [wide(square_mine[m]) + wide(square_theirs[m]) for m in range(pieces)]
    square_parts = [other(low(square_sums[m]), "dp", m) for m in range(1, pieces)]
    d_query1, d_query1_t, d_memory1, d_memory1_t, square_parts, state_parts = after(
        (d_query1, d_query1_t, d_memory1, d_memory1_t, square_parts, state_parts),
        layer_first,
        unit_grads,
    )
    layer_output = trade(layer_first, "dp", 0, 0)[None]
    encoder_rows = low(d_states[0] + sum(wide(part) for part in state_parts))
    encoder_gradient = swap_planes(after(encoder_rows, layer_first))[None]
    square_sum = square_sums[0] + sum(wide(part) for part in square_parts)
    d_ones = [
        (
            product(d_query1[j].reshape(-1, width), attend_w[:width])
            + product(d_memory1[j].reshape(-1, 2 * width), attend_w[width:])
        ).reshape(pieces, row_count, model_width)
        for j in range(cores)
    ]
    d_sum = d_ones[0] + wide(other(low(d_ones[1]), "core", 1))
    leaving = [low(d_sum[m]) for m in range(1, pieces)]
    parts1 = [d_sum[0]] + [other(part, "dp", m + 1) for m, part in enumerate(leaving)]
    parts1, encoder_gradient = after((parts1, encoder_gradient))
    input_gradient, sums1 = single(
        input_back_kernel,
        [flat_low, jax.ShapeDtypeStruct((2, model_width), jnp.float32)],
        [None] * (pieces + 3),
        [],
        own, *parts1, d_middle, raw, gain_rows[0:1],
    )
    input_gradient = trade(trade(input_gradient, "z", 0, 0), "dp", 0, 0)[None]

    def turned_grad(columns, rows):
        half = columns.shape[1] // cores
        return low(
            sum(
                product(columns[:, j * half : (j + 1) * half], rows[j].reshape(half, model_width))
                for j in range(cores)
            )
        )

    def to_chips(grad):
        columns = grad.shape[0]
        split = grad.reshape(columns, pieces, block_rows).transpose(1, 0, 2)
        mine = trade(split.reshape(pieces * columns, block_rows), "dp", 0, 0)
        return mine.reshape(planes, columns, block_rows)

    cross_sum = to_chips(after(turned_grad(d_memory_t, all_states), d_query1))
    attend_sum = jnp.concatenate([turned_grad(d_query1_t, ones), turned_grad(d_memory1_t, ones)])
    attend_sum = to_chips(after(attend_sum, cross_sum))
    tail = jnp.concatenate(
        [low(square_sum).reshape(planes, 3 * width, block_rows), cross_sum, attend_sum], axis=1
    )
    tail = sum(
        wide(part if m == 0 else other(part, "z", m))
        for m, part in enumerate(
            lax.dynamic_index_in_dim(tail, plane ^ m, 0, keepdims=False) for m in range(planes)
        )
    )
    square_sum = tail[: 3 * width].reshape(3, width, block_rows)
    cross_sum, attend_sum = tail[3 * width : 5 * width], tail[5 * width :]
    unit_grads = wide(unit_grads)

    def weight_order(turned, count):
        turned = turned.reshape(count, heads, head_size, block_rows).transpose(3, 1, 0, 2)
        return turned.reshape(block_rows, count * width)

    unit_sums = lax.dynamic_update_slice(
        jnp.zeros((planes, cores, pieces, block_units), jnp.float32),
        unit_sums.reshape(planes, 1, 1, block_units),
        (0, core, piece, 0),
    ).reshape(-1)
    small = jnp.concatenate(
        [
            sums2[0],
            sums3[0],
            sums2[1],
            sums3[1],
            sums2[2],
            jnp.sum(wide(d_mixed2), axis=2).transpose(1, 0, 2).reshape(-1),
            place_heads(jnp.sum(wide(d_memory_t[width:]), axis=1)),
            sums3[2],
            jnp.sum(wide(upstream), axis=0),
            unit_sums,
        ]
    )
    last = jnp.stack(
        [
            sums1[0],
            sums1[1],
            place_heads(jnp.sum(wide(d_query1_t), axis=1)),
            place_heads(jnp.sum(wide(d_memory1_t[width:]), axis=1)),
        ]
    )
    small = sum_all(jnp.concatenate([last.reshape(-1), small]).reshape(-1, 128)).reshape(-1)
    last, small = small[: 4 * model_width].reshape(4, model_width), small[4 * model_width :]
    rows = small[: 9 * model_width].reshape(9, model_width)
    return (
        layer_output,
        input_gradient,
        encoder_gradient,
        jnp.concatenate([last[0:1], rows[0:2]]),
        jnp.concatenate([last[1:2], rows[2:4]]),
        weight_order(attend_sum, 3),
        square_sum[0],
        jnp.concatenate([last[2:4], rows[4:5]]),
        square_sum[1].T,
        weight_order(cross_sum, 2),
        square_sum[2],
        rows[5:8],
        unit_grads[:, 0].T,
        small[9 * model_width :],
        unit_grads[:, 1],
        rows[8],
    )


def solution(mesh):
    pieces, sequence = mesh.devices.shape
    planes = Mesh(mesh.devices.reshape(pieces, sequence // 2, 2), ("dp", "z", "core"))
    seq = ("z", "core")
    in_specs = (
        P("dp", seq, None),
        P("dp", seq, None),
        P("dp", None),
        P("dp", None),
        P(),
        P(),
        P("dp", seq),
        P(seq, "dp"),
        P(),
        P("dp", seq),
        P("dp", seq),
        P(seq, "dp"),
        P(),
        P("dp", seq),
        P(),
        P(seq, "dp"),
        P(),
        P("dp", seq, None),
    )
    out_specs = (
        P("dp", seq, None),
        P("dp", seq, None),
        P("dp", seq, None),
        P(),
        P(),
        P("dp", seq),
        P(seq, "dp"),
        P(),
        P("dp", seq),
        P("dp", seq),
        P(seq, "dp"),
        P(),
        P("dp", seq),
        P(),
        P(seq, "dp"),
        P(),
    )
    return jax.shard_map(
        shards, mesh=planes, in_specs=in_specs, out_specs=out_specs, check_vma=False
    )
```

time: 969 us -> 734 us (0.76)
  waiting for transfers between devices: 327 us -> 229 us
  Pallas kernels: 43.6 us -> 113 us
  matrix products: 92.1 us -> 28.5 us
  starting transfers between devices: 195 us -> 136 us
  blocking collectives: 80.1 us -> 36.2 us
  other arithmetic: 69.6 us -> 42.1 us
  local copies, waits for them, and re-layouts: 135 us -> 120 us
    all_to_all x31 -> x15, waiting for transfers between devices: 144 us -> 56.3 us  [trade(): lax.all_to_all(values, axis, split_axis=split, concat_axis=concat, tiled=...]
    all_to_all x31 -> x15, starting transfers between devices: 151 us -> 68.1 us  [trade(): lax.all_to_all(values, axis, split_axis=split, concat_axis=concat, tiled=...]
    pallas_call x4 -> x13, Pallas kernels: 43.6 us -> 113 us  [the longest x2 26.9 us: units_group(): pl.pallas_call(functools.partial(units_kernel, half_count=count), grid_sp...]
    dot_general x20 -> x0, matrix products: 67.1 us -> none  [the longest x13 34.6 us: against(): lax.dot_general(former, latter, (((1,), (1,)), ((), ())), preferred_eleme...]
    all_gather x3 -> x0, blocking collectives: 53.3 us -> none  [the longest x2 33.8 us: fetch_heads(): whole = lax.all_gather(weight, 'z', axis=0, tiled=True)]
    reduce_sum x18 -> x7, other arithmetic: 23.7 us -> 1.38 us  [the longest x2 0.79 us: shards(): unit_sums = sum((jnp.sum(wide(d), axis=(0, 1, 2)) for d in d_hiddens))]
    unnamed x226 -> x247, local copies, waits for them, and re-layouts: 43.8 us -> 63.1 us
    ppermute x1 -> x3, waiting for transfers between devices: 0.01 us -> 15.9 us  [swap_planes(): return lax.ppermute(values, ('dp', 'z', 'core'), pairs)]
  transfers between devices with their start and end apart: 100 -> 74, of which waited for: 37 -> 33; matrix products, arithmetic and copies ran while one was open for 27% -> 19% of each run, Pallas kernels for 3% -> 15%
where the time goes in v2:
time: 734 us; the launch traced here: 721 us
  waiting for transfers between devices  229 us (31%)
  starting transfers between devices  136 us (19%)
  local copies, waits for them, and re-layouts  120 us (16%)
  Pallas kernels  113 us (15%)
  other arithmetic  42.1 us (6%)
  blocking collectives  36.2 us (5%)
  matrix products  28.5 us (4%)
  between operations  15.8 us (2%)
    ppermute x53, waiting for transfers between devices, other(): return lax.ppermute(values, axis, [(i, i ^ shift) for i in range(count)])  157 us
    all_to_all x15, starting transfers between devices, trade(): lax.all_to_all(values, axis, split_axis=split, concat_axis=concat, tiled=...  68.1 us
    unnamed x247, local copies, waits for them, and re-layouts  63.1 us
    all_to_all x15, waiting for transfers between devices, trade(): lax.all_to_all(values, axis, split_axis=split, concat_axis=concat, tiled=...  56.3 us
    ppermute x53, starting transfers between devices, other(): return lax.ppermute(values, axis, [(i, i ^ shift) for i in range(count)])  51.6 us
    all_to_all x3, blocking collectives, trade(): lax.all_to_all(values, axis, split_axis=split, concat_axis=concat, tiled=...  36.2 us
    dot_general x16, matrix products, product(): return jnp.dot(former, latter, preferred_element_type=jnp.float32)  28.5 us
    pallas_call x2, Pallas kernels, units_group(): pl.pallas_call(functools.partial(units_kernel, half_count=count), grid_sp...  26.9 us
  transfers between devices with their start and end apart: 74, of which 33 were waited for; matrix products, arithmetic and copies ran while one was open for 19% of the time, Pallas kernels for 15%

profile of v2, /device:TPU:8, one launch (start us, length us, event | category | flops | bytes accessed | tf_op | source)
XLA Modules:
  0.0 720.7 jit_solution(5096411282396653229)
XLA Ops:
  19.9 10.6 %all-to-all-done = bf16[4,64,1024]{2,1,0:T(8,128)(2,1)} async-done(((bf16[4,64,1024]{2,1,0:T(8,128)(2,1)}), bf16[4,64,1024]{2,1,0:T(8,128)(2,1)}, u32[]{:S(2)}, u32[]{:S(2)}) %all-to-all-start) | async-done | bytes 524320 | tf_op jit(solution)/shard_map/all_to_all | solution.py:823
  38.2 23.5 %all-to-all-done.1 = bf16[4,64,1024]{2,1,0:T(8,128)(2,1)S(1)} async-done(((bf16[4,64,1024]{2,1,0:T(8,128)(2,1)}), bf16[4,64,1024]{2,1,0:T(8,128)(2,1)S(1)}, u32[]{:S(2)}, u32[]{:S(2)}) %all-to-all-start.1) | async-done | bytes 524320 | tf_op jit(solution)/shard_map/all_to_all | solution.py:823
  70.3 7.2 %collective-permute-done.4 = bf16[256,1024]{1,0:T(8,128)(2,1)S(1)} collective-permute-done((bf16[256,1024]{1,0:T(8,128)(2,1)S(1)}, bf16[256,1024]{1,0:T(8,128)(2,1)S(1)}, u32[]{:S(2)}, u32[]{:S(2)}) %collective-permute-start.4) | collective-permute-done | bytes 524320 | tf_op jit(solution)/shard_map/ppermute | solution.py:819
  77.6 11.8 %collective-permute-done.5 = bf16[256,1024]{1,0:T(8,128)(2,1)S(1)} collective-permute-done((bf16[256,1024]{1,0:T(8,128)(2,1)S(1)}, bf16[256,1024]{1,0:T(8,128)(2,1)S(1)}, u32[]{:S(2)}, u32[]{:S(2)}) %collective-permute-start.5) | collective-permute-done | bytes 524320 | tf_op jit(solution)/shard_map/ppermute | solution.py:819
  127.1 15.9 %collective-permute-done.12 = bf16[128,1024]{1,0:T(8,128)(2,1)S(1)} collective-permute-done((bf16[128,1024]{1,0:T(8,128)(2,1)}, bf16[128,1024]{1,0:T(8,128)(2,1)S(1)}, u32[]{:S(2)}, u32[]{:S(2)}) %collective-permute-start.12) | collective-permute-done | bytes 262176 | tf_op jit(solution)/shard_map/ppermute | solution.py:858
  153.6 14.5 %shard_map.297 = (bf16[2,4,256,128]{3,2,1,0:T(8,128)(2,1)S(1)}, bf16[2,4,256,128]{3,2,1,0:T(8,128)(2,1)S(1)}, bf16[2,4,256,128]{3,2,1,0:T(8,128)(2,1)S(1)}, bf16...) custom-call(s32[18]{0:T(128)S(1)} %pad_add_fusion.4.scalars, ...), custom_call_target="tpu_custom_call" | custom-call | flops 17600000000 | bytes 1048576 | tf_op jit(solution)/shard_map/pallas_call | solution.py:335
  169.6 11.4 %collective-permute-done.8 = bf16[4,3,128,256]{3,2,1,0:T(8,128)(2,1)S(1)} collective-permute-done((bf16[4,3,128,256]{3,2,1,0:T(8,128)(2,1)}, bf16[4,3,128,256]{3,2,1,0:T(8,128)(2,1)S(1)}, u32[]{:S(2)}, u32[]{:S(2)}) %collective-permute-start.8) | collective-permute-done | bytes 786464 | tf_op jit(solution)/shard_map/ppermute | solution.py:819
  184.5 11.8 %all_to_all.147 = bf16[8,256,128]{2,1,0:T(8,128)(2,1)S(1)} all-to-all(bf16[8,256,128]{2,1,0:T(8,128)(2,1)S(1)} %bitcast.308), channel_id=1, replica_groups=mesh['dp'=4,'z'=4,'core'=2] {'core','dp'}, dimensions={0} | all-to-all | bytes 1048576 | tf_op jit(solution)/shard_map/all_to_all | solution.py:823
  235.5 12.3 %shard_map.299 = (bf16[2,4,128,128]{3,2,1,0:T(8,128)(2,1)S(1)}, bf16[2,4,128,128]{3,2,1,0:T(8,128)(2,1)S(1)}, bf16[2,4,4,64,128]{4,3,2,1,0:T(8,128)(2,1)S(1)}, f...) custom-call(s32[18]{0:T(128)S(1)} %pad_add_fusion.2.scalars, bf16[2,4,4,64,128]{4,3,2,1,0:T(8,128)(2,1)} %bitcast.40.q_ref, ...), custom_call_target="tpu_custom_call" | custom-call | flops 12099999744 | bytes 1048576 | tf_op jit(solution)/shard_map/pallas_call | solution.py:371
  262.7 9.2 %all-to-all-done.7 = bf16[8,256,128]{2,1,0:T(8,128)(2,1)} async-done(((bf16[8,256,128]{2,1,0:T(8,128)(2,1)}), bf16[8,256,128]{2,1,0:T(8,128)(2,1)}, u32[]{:S(2)}, u32[]{:S(2)}) %all-to-all-start.7) | async-done | bytes 524320 | tf_op jit(solution)/shard_map/all_to_all | solution.py:823
  282.9 10.9 %collective-permute-done.20 = bf16[256,1024]{1,0:T(8,128)(2,1)S(1)} collective-permute-done((bf16[256,1024]{1,0:T(8,128)(2,1)S(1)}, bf16[256,1024]{1,0:T(8,128)(2,1)S(1)}, u32[]{:S(2)}, u32[]{:S(2)}) %collective-permute-start.20) | collective-permute-done | bytes 524320 | tf_op jit(solution)/shard_map/ppermute | solution.py:819
  299.6 19.8 %shard_map.301 = (bf16[2,3,256,1024]{3,2,1,0:T(8,128)(2,1)S(1)}, bf16[2,3,256,1024]{3,2,1,0:T(8,128)(2,1)}, f32[3,256,1024]{2,1,0:T(8,128)}, bf16[3,256,1024]{2,1,0:T(8,128)(2,1)S(1)}) custom-call(s32[2]{0:T(128)S(1)} %pad_add_fusion.1.scalars, bf16[3,256,1024]{2,1,0:T(8,128)(2,1)} %pad_maximum_fusion.5.mine_ref.refs_4_, ...), custom_call_target="tpu_custom_call" | custom-call | flops 21450000384 | bytes 1048576 | tf_op jit(solution)/shard_map/pallas_call | solution.py:671
  321.3 7.1 shard_map.302
  339.8 16.5 %shard_map.303 = bf16[1024,2048]{1,0:T(8,128)(2,1)} custom-call(s32[2]{0:T(128)S(1)} %pad_add_fusion.1.scalars, bf16[2,3,256,1024]{3,2,1,0:T(8,128)(2,1)S(1)} %copy-done.6, bf16[2,1,256,1024]{3,2,1,0:T(8,128)(2,1)S(1)} %get-tuple-element.154.refs_1_, bf16[2,3,256,1024]{3,2,1,0:T(8,128)(2,1)S(1)} %get-tuple-element.160.refs_2_, ...), custom_call_target="tpu_custom_call" | custom-call | flops 13200000000 | bytes 1048576 | tf_op jit(solution)/shard_map/pallas_call | solution.py:770
  397.0 11.0 %shard_map.305 = (bf16[2,4,4,64,128]{4,3,2,1,0:T(8,128)(2,1)S(1)}, bf16[2,4,128,256]{3,2,1,0:T(8,128)(2,1)S(1)}, bf16[256,1024]{1,0:T(8,128)(2,1)S(1)}) custom-call(s32[18]{0:T(128)S(1)} %pad_add_fusion.2.scalars, bf16[2,4,4,64,128]{4,3,2,1,0:T(8,128)(2,1)} %bitcast.40.q_ref, bf16[2,4,128,128]{3,2,1,0:T(8,128)(2,1)S(1)} %get-tuple-element.165.k_ref, ...), custom_call_target="tpu_custom_call" | custom-call | flops 13200000000 | bytes 1048576 | tf_op jit(solution)/shard_map/pallas_call | solution.py:409
  409.6 8.9 %collective-permute-done.33 = bf16[256,1024]{1,0:T(8,128)(2,1)} collective-permute-done((bf16[256,1024]{1,0:T(8,128)(2,1)}, bf16[256,1024]{1,0:T(8,128)(2,1)}, u32[]{:S(2)}, u32[]{:S(2)}) %collective-permute-start.33) | collective-permute-done | bytes 524320 | tf_op jit(solution)/shard_map/ppermute | solution.py:819
  418.5 11.9 %all_to_all.148 = bf16[8,256,128]{2,1,0:T(8,128)(2,1)S(1)} all-to-all(bf16[8,256,128]{2,1,0:T(8,128)(2,1)S(1)} %bitcast.310), channel_id=1, replica_groups=mesh['dp'=4,'z'=4,'core'=2] {'core','dp'}, dimensions={0} | all-to-all | bytes 1048576 | tf_op jit(solution)/shard_map/all_to_all | solution.py:823
  434.9 12.5 %all_to_all.149 = bf16[8,256,128]{2,1,0:T(8,128)(2,1)} all-to-all(bf16[8,256,128]{2,1,0:T(8,128)(2,1)S(1)} %bitcast.312), channel_id=1, replica_groups=mesh['dp'=4,'z'=4,'core'=2] {'core','dp'}, dimensions={0} | all-to-all | bytes 1048576 | tf_op jit(solution)/shard_map/all_to_all | solution.py:823
  517.2 11.6 %shard_map.307 = (bf16[2,4,4,64,128]{4,3,2,1,0:T(8,128)(2,1)S(1)}, bf16[128,2048]{1,0:T(8,128)(2,1)S(1)}, bf16[2,4,256,256]{3,2,1,0:T(8,128)(2,1)S(1)}, bf16[256,2048]{1,0:T(8,128)(2,1)S(1)}) custom-call(s32[18]{0:T(128)S(1)} %pad_add_fusion.4.scalars, bf16[2,4,4,64,128]{4,3,2,1,0:T(8,128)(2,1)S(1)} %bitcast.331, bf16[2,4,256,128]{3,2,1,0:T(8,128)(2,1)S(1)} %copy-done.68, ...), custom_call_target="tpu_custom_call" | custom-call | flops 13200000000 | bytes 1048576 | tf_op jit(solution)/shard_map/pallas_call | solution.py:409
  532.5 17.0 %collective-permute-done.38 = bf16[4,3,128,256]{3,2,1,0:T(8,128)(2,1)} collective-permute-done((bf16[4,3,128,256]{3,2,1,0:T(8,128)(2,1)}, bf16[4,3,128,256]{3,2,1,0:T(8,128)(2,1)}, u32[]{:S(2)}, u32[]{:S(2)}) %collective-permute-start.38) | collective-permute-done | bytes 786464 | tf_op jit(solution)/shard_map/ppermute | solution.py:819
  599.6 17.5 %collective-permute-done.45.refs_2_ = bf16[256,1024]{1,0:T(8,128)(2,1)S(1)} collective-permute-done((bf16[256,1024]{1,0:T(8,128)(2,1)}, bf16[256,1024]{1,0:T(8,128)(2,1)S(1)}, u32[]{:S(2)}, u32[]{:S(2)}) %collective-permute-start.45) | collective-permute-done | bytes 524320 | tf_op jit(solution)/shard_map/ppermute | solution.py:819
  653.7 13.9 %collective-permute-done.54 = bf16[1024,256]{1,0:T(8,128)(2,1)} collective-permute-done((bf16[1024,256]{1,0:T(8,128)(2,1)}, bf16[1024,256]{1,0:T(8,128)(2,1)}, u32[]{:S(2)}, u32[]{:S(2)}) %collective-permute-start.54) | collective-permute-done | bytes 524320 | tf_op jit(solution)/shard_map/ppermute | solution.py:819
  667.6 10.2 %collective-permute-done.55 = bf16[1024,256]{1,0:T(8,128)(2,1)} collective-permute-done((bf16[1024,256]{1,0:T(8,128)(2,1)}, bf16[1024,256]{1,0:T(8,128)(2,1)}, u32[]{:S(2)}, u32[]{:S(2)}) %collective-permute-start.55) | collective-permute-done | bytes 524320 | tf_op jit(solution)/shard_map/ppermute | solution.py:819
  689.4 7.7 %collective-permute-done.52 = f32[168,128]{1,0:T(8,128)S(1)} collective-permute-done((f32[168,128]{1,0:T(8,128)S(1)}, f32[168,128]{1,0:T(8,128)S(1)}, u32[]{:S(2)}, u32[]{:S(2)}) %collective-permute-start.52) | collective-permute-done | bytes 86048 | tf_op jit(solution)/shard_map/ppermute | solution.py:819
  (540 shorter events, 400.3 us)
Async XLA Ops:
  17.6 86.5 %all-gather.6.cloned.1.call-start = ((), (), s32[]{:S(2)}) async-start(), calls=%async_computation.21 | async-start | bytes 2621440 | tf_op jit(solution)/shard_map/all_gather | solution.py:942
  30.5 31.3 %all-to-all-start.1 = ((bf16[4,64,1024]{2,1,0:T(8,128)(2,1)}), bf16[4,64,1024]{2,1,0:T(8,128)(2,1)S(1)}, u32[]{:S(2)}, u32[]{:S(2)}) async-start(bf16[4,64,1024]{2,1,0:T(8,128)(2,1)} %all-to-all-done), calls=%async_computation.1 | async-start | bytes 1048576 | tf_op jit(solution)/shard_map/all_to_all | solution.py:823
  66.2 31.4 %all-to-all-start.2 = ((bf16[4,64,1024]{2,1,0:T(8,128)(2,1)}), bf16[4,64,1024]{2,1,0:T(8,128)(2,1)}, u32[]{:S(2)}, u32[]{:S(2)}) async-start(bf16[4,64,1024]{2,1,0:T(8,128)(2,1)} %bitcast.23), calls=%async_computation.2 | async-start | bytes 1048576 | tf_op jit(solution)/shard_map/all_to_all | solution.py:823
  92.0 61.5 %collective-permute-start.7 = (bf16[4,256,1024]{2,1,0:T(8,128)(2,1)S(1)}, bf16[4,256,1024]{2,1,0:T(8,128)(2,1)}, u32[]{:S(2)}, u32[]{:S(2)}) collective-permute-start(bf16[4,256,1024]{2,1,0:T(8,128)(2,1)S(1)} %pad_maximum_fusion.1.mine_ref), channel_id=1, source_target_pairs={{0,1},{1,0},{2,3},{3,2},{4,5},{5,4},{6,7},{7,6},{8,9},{9,8},{10,11... | collective-permute-start | bytes 6291464 | tf_op jit(solution)/shard_map/ppermute | solution.py:819
  115.4 32.6 %all-to-all-start.4 = ((bf16[4,640,256]{2,1,0:T(8,128)(2,1)}), bf16[4,640,256]{2,1,0:T(8,128)(2,1)}, u32[]{:S(2)}, u32[]{:S(2)}) async-start(bf16[4,640,256]{2,1,0:T(8,128)(2,1)} %copy.124), calls=%async_computation.4 | async-start | bytes 2621440 | tf_op jit(solution)/shard_map/all_to_all | solution.py:823
  119.7 138.8 %all-gather.4.cloned.1.call-start = ((), (), s32[]{:S(2)}) async-start(), calls=%async_computation.19 | async-start | bytes 5242880 | tf_op jit(solution)/shard_map/all_gather | solution.py:954
  148.0 32.9 %collective-permute-start.8 = (bf16[4,3,128,256]{3,2,1,0:T(8,128)(2,1)}, bf16[4,3,128,256]{3,2,1,0:T(8,128)(2,1)S(1)}, u32[]{:S(2)}, u32[]{:S(2)}) collective-permute-start(bf16[4,3,128,256]{3,2,1,0:T(8,128)(2,1)} %bitcast.345), channel_id=1, source_target_pairs={{0,8},{8,0},{16,24},{24,16},{1,9},{9,1},{17,25},{25,17},{2,10},{10... | collective-permute-start | bytes 2359304 | tf_op jit(solution)/shard_map/ppermute | solution.py:819
  148.0 35.9 %collective-permute-start.9 = (bf16[4,3,128,256]{3,2,1,0:T(8,128)(2,1)}, bf16[4,3,128,256]{3,2,1,0:T(8,128)(2,1)S(1)}, u32[]{:S(2)}, u32[]{:S(2)}) collective-permute-start(bf16[4,3,128,256]{3,2,1,0:T(8,128)(2,1)} %bitcast.346), channel_id=1, source_target_pairs={{0,16},{8,24},{16,0},{24,8},{1,17},{9,25},{17,1},{25,9},{2,18},{10... | collective-permute-start | bytes 2359304 | tf_op jit(solution)/shard_map/ppermute | solution.py:819
  184.3 28.2 %collective-permute-start.11 = (bf16[4,4,3,128,256]{4,3,2,1,0:T(8,128)(2,1)S(1)}, bf16[4,4,3,128,256]{4,3,2,1,0:T(8,128)(2,1)S(1)}, u32[]{:S(2)}, u32[]{:S(2)}) collective-permute-start(bf16[4,4,3,128,256]{4,3,2,1,0:T(8,128)(2,1)S(1)} %pad_maximum_fusion.omine_ref.qmine_ref.refs_7_.mine_ref), channel_id=1, source_target_pairs={{0,1},{1,0},{2,3},{3,2},{4,5},{5,4},{6,7},{7,6},{8,9},{9,8},{10,11... | collective-permute-start | bytes 9437192 | tf_op jit(solution)/shard_map/ppermute | solution.py:819
  262.6 184.8 %reduce-scatter.2.cloned.1.call-start = ((), (), s32[]{:S(2)}) async-start(), calls=%async_computation.20 | async-start | bytes 5242880 | tf_op jit(solution)/shard_map/reduce_scatter | solution.py:1072
  459.5 37.5 %collective-permute-start.35 = (bf16[4,4,3,128,256]{4,3,2,1,0:T(8,128)(2,1)}, bf16[4,4,3,128,256]{4,3,2,1,0:T(8,128)(2,1)}, u32[]{:S(2)}, u32[]{:S(2)}) collective-permute-start(bf16[4,4,3,128,256]{4,3,2,1,0:T(8,128)(2,1)} %get-tuple-element.191), channel_id=1, source_target_pairs={{0,1},{1,0},{2,3},{3,2},{4,5},{5,4},{6,7},{7,6},{8,9},{9,8},{10,11... | collective-permute-start | bytes 9437192 | tf_op jit(solution)/shard_map/ppermute | solution.py:819
  495.5 36.1 %collective-permute-start.41 = (bf16[128,1024]{1,0:T(8,128)(2,1)}, bf16[128,1024]{1,0:T(8,128)(2,1)}, u32[]{:S(2)}, u32[]{:S(2)}) collective-permute-start(bf16[128,1024]{1,0:T(8,128)(2,1)} %get-tuple-element.333), channel_id=1, source_target_pairs={{0,16},{8,24},{16,0},{24,8},{1,17},{9,25},{17,1},{25,9},{2,18},{10... | collective-permute-start | bytes 786440 | tf_op jit(solution)/shard_map/ppermute | solution.py:819
  497.0 34.6 %collective-permute-start.42 = (bf16[128,1024]{1,0:T(8,128)(2,1)}, bf16[128,1024]{1,0:T(8,128)(2,1)}, u32[]{:S(2)}, u32[]{:S(2)}) collective-permute-start(bf16[128,1024]{1,0:T(8,128)(2,1)} %get-tuple-element.332), channel_id=1, source_target_pairs={{0,24},{8,16},{16,8},{24,0},{1,25},{9,17},{17,9},{25,1},{2,26},{10... | collective-permute-start | bytes 786440 | tf_op jit(solution)/shard_map/ppermute | solution.py:819
  500.6 32.0 %collective-permute-start.36 = (bf16[4,3,128,256]{3,2,1,0:T(8,128)(2,1)}, bf16[4,3,128,256]{3,2,1,0:T(8,128)(2,1)}, u32[]{:S(2)}, u32[]{:S(2)}) collective-permute-start(bf16[4,3,128,256]{3,2,1,0:T(8,128)(2,1)} %get-tuple-element.311), channel_id=1, source_target_pairs={{0,8},{8,0},{16,24},{24,16},{1,9},{9,1},{17,25},{25,17},{2,10},{10... | collective-permute-start | bytes 2359304 | tf_op jit(solution)/shard_map/ppermute | solution.py:819
  502.5 30.0 %collective-permute-start.37 = (bf16[4,3,128,256]{3,2,1,0:T(8,128)(2,1)}, bf16[4,3,128,256]{3,2,1,0:T(8,128)(2,1)}, u32[]{:S(2)}, u32[]{:S(2)}) collective-permute-start(bf16[4,3,128,256]{3,2,1,0:T(8,128)(2,1)} %get-tuple-element.310), channel_id=1, source_target_pairs={{0,16},{8,24},{16,0},{24,8},{1,17},{9,25},{17,1},{25,9},{2,18},{10... | collective-permute-start | bytes 2359304 | tf_op jit(solution)/shard_map/ppermute | solution.py:819
  504.4 27.2 %all-to-all-start.11 = ((bf16[4,64,1024]{2,1,0:T(8,128)(2,1)}), bf16[4,64,1024]{2,1,0:T(8,128)(2,1)}, u32[]{:S(2)}, u32[]{:S(2)}) async-start(bf16[4,64,1024]{2,1,0:T(8,128)(2,1)} %bitcast.82), calls=%async_computation.12 | async-start | bytes 1048576 | tf_op jit(solution)/shard_map/all_to_all | solution.py:823
  510.9 38.7 %collective-permute-start.38 = (bf16[4,3,128,256]{3,2,1,0:T(8,128)(2,1)}, bf16[4,3,128,256]{3,2,1,0:T(8,128)(2,1)}, u32[]{:S(2)}, u32[]{:S(2)}) collective-permute-start(bf16[4,3,128,256]{3,2,1,0:T(8,128)(2,1)} %get-tuple-element.309), channel_id=1, source_target_pairs={{0,24},{8,16},{16,8},{24,0},{1,25},{9,17},{17,9},{25,1},{2,26},{10... | collective-permute-start | bytes 2359304 | tf_op jit(solution)/shard_map/ppermute | solution.py:819
  551.6 43.3 %collective-permute-start.47 = (bf16[128,1024]{1,0:T(8,128)(2,1)}, bf16[128,1024]{1,0:T(8,128)(2,1)}, u32[]{:S(2)}, u32[]{:S(2)}) collective-permute-start(bf16[128,1024]{1,0:T(8,128)(2,1)} %fusion.29), channel_id=1, source_target_pairs={{0,0},{1,1},{2,8},{3,9},{4,16},{5,17},{6,24},{7,25},{8,2},{9,3},{1... | collective-permute-start | bytes 786440 | tf_op jit(solution)/shard_map/ppermute | solution.py:858
  586.7 30.5 %collective-permute-start.45 = (bf16[256,1024]{1,0:T(8,128)(2,1)}, bf16[256,1024]{1,0:T(8,128)(2,1)S(1)}, u32[]{:S(2)}, u32[]{:S(2)}) collective-permute-start(bf16[256,1024]{1,0:T(8,128)(2,1)} %get-tuple-element.318), channel_id=1, source_target_pairs={{0,16},{8,24},{16,0},{24,8},{1,17},{9,25},{17,1},{25,9},{2,18},{10... | collective-permute-start | bytes 1572872 | tf_op jit(solution)/shard_map/ppermute | solution.py:819
  588.1 29.0 %collective-permute-start.46 = (bf16[256,1024]{1,0:T(8,128)(2,1)}, bf16[256,1024]{1,0:T(8,128)(2,1)S(1)}, u32[]{:S(2)}, u32[]{:S(2)}) collective-permute-start(bf16[256,1024]{1,0:T(8,128)(2,1)} %get-tuple-element.317), channel_id=1, source_target_pairs={{0,24},{8,16},{16,8},{24,0},{1,25},{9,17},{17,9},{25,1},{2,26},{10... | collective-permute-start | bytes 1572872 | tf_op jit(solution)/shard_map/ppermute | solution.py:819
  589.2 31.2 %all-to-all-start.17 = ((bf16[4,384,256]{2,1,0:T(8,128)(2,1)}), bf16[4,384,256]{2,1,0:T(8,128)(2,1)}, u32[]{:S(2)}, u32[]{:S(2)}) async-start(bf16[4,384,256]{2,1,0:T(8,128)(2,1)} %bitcast.348), calls=%async_computation.18 | async-start | bytes 1572864 | tf_op jit(solution)/shard_map/all_to_all | solution.py:823
  631.2 36.5 %collective-permute-start.54 = (bf16[1024,256]{1,0:T(8,128)(2,1)}, bf16[1024,256]{1,0:T(8,128)(2,1)}, u32[]{:S(2)}, u32[]{:S(2)}) collective-permute-start(bf16[1024,256]{1,0:T(8,128)(2,1)} %get-tuple-element.316), channel_id=1, source_target_pairs={{0,4},{2,6},{4,0},{6,2},{1,5},{3,7},{5,1},{7,3},{8,12},{10,14},{12... | collective-permute-start | bytes 1572872 | tf_op jit(solution)/shard_map/ppermute | solution.py:819
  632.4 45.4 %collective-permute-start.55 = (bf16[1024,256]{1,0:T(8,128)(2,1)}, bf16[1024,256]{1,0:T(8,128)(2,1)}, u32[]{:S(2)}, u32[]{:S(2)}) collective-permute-start(bf16[1024,256]{1,0:T(8,128)(2,1)} %get-tuple-element.315), channel_id=1, source_target_pairs={{0,6},{2,4},{4,2},{6,0},{1,7},{3,5},{5,3},{7,1},{8,14},{10,12},{12... | collective-permute-start | bytes 1572872 | tf_op jit(solution)/shard_map/ppermute | solution.py:819
  645.3 38.3 %collective-permute-start.51 = (f32[168,128]{1,0:T(8,128)S(1)}, f32[168,128]{1,0:T(8,128)S(1)}, u32[]{:S(2)}, u32[]{:S(2)}) collective-permute-start(f32[168,128]{1,0:T(8,128)S(1)} %add.259), channel_id=1, source_target_pairs={{0,2},{2,0},{4,6},{6,4},{1,3},{3,1},{5,7},{7,5},{8,10},{10,8},{12,... | collective-permute-start | bytes 258056 | tf_op jit(solution)/shard_map/ppermute | solution.py:819
  (158 other events, 1565.9 us)
Sparse Core Ops, SparseCore 0:
  20.6 55.0 all-gather.5
  143.1 78.0 all-gather.3
  358.3 77.3 reduce-scatter.1

commit v3 on v2

--- a/solution.py
+++ b/solution.py
@@ -319,8 +319,8 @@
     )
 
 
-def params():
-    return pltpu.CompilerParams(vmem_limit_bytes=36 * 2**20)
+def params(mebibytes=56):
+    return pltpu.CompilerParams(vmem_limit_bytes=mebibytes * 2**20)
 
 
 def self_forward(scalars, mine, theirs, planes, weight, bias, first, last):
@@ -628,7 +628,7 @@
 
 def units_kernel(
     scalars, mine_ref, theirs_ref, upmine_ref, uptheirs_ref, expand_ref, shrink_ref, bias_ref,
-    active_ref, dhidden_ref, dmine_ref, dtheirs_ref, half_count,
+    active_ref, dhidden_ref, dmine_ref, dtheirs_ref, outmine_ref, outtheirs_ref, half_count,
 ):
     step = pl.program_id(0)
     expand, shrink = expand_ref[...], shrink_ref[...]
@@ -639,17 +639,25 @@
         dactive = lax.dot_general(up, shrink, against_last, preferred_element_type=jnp.float32)
         active, slope = gelu_parts(hidden + bias_ref[...])
         dhidden = (dactive * slope).astype(jnp.bfloat16)
-        active_ref[0, 0] = active.astype(jnp.bfloat16)
+        active = active.astype(jnp.bfloat16)
+        active_ref[0, 0] = active
         dhidden_ref[0, 0] = dhidden
-        return jnp.dot(dhidden, expand, preferred_element_type=jnp.float32)
+        return (
+            jnp.dot(dhidden, expand, preferred_element_type=jnp.float32),
+            jnp.dot(active, shrink, preferred_element_type=jnp.float32),
+        )
 
     @pl.when(step < half_count)
     def _():
-        dtheirs_ref[0] = one(theirs_ref[0], uptheirs_ref[0]).astype(jnp.bfloat16)
+        dthree, out = one(theirs_ref[0], uptheirs_ref[0])
+        dtheirs_ref[0] = dthree.astype(jnp.bfloat16)
+        outtheirs_ref[0] = out.astype(jnp.bfloat16)
 
     @pl.when(step >= half_count)
     def _():
-        dmine_ref[0] = one(mine_ref[0], upmine_ref[0])
+        dthree, out = one(mine_ref[0], upmine_ref[0])
+        dmine_ref[0] = dthree
+        outmine_ref[0] = out
 
 
 def units_group(scalars, mine, theirs, ups, start, expand_t, shrink_w, bias):
@@ -682,15 +690,19 @@
                 whole_spec(shrink_w.shape),
                 whole_spec(bias.shape),
             ],
-            out_specs=[table_spec, table_spec, piece_spec(True), piece_spec(False)],
+            out_specs=[table_spec, table_spec] + [piece_spec(True), piece_spec(False)] * 2,
         ),
         out_shape=[
             table,
             table,
             jax.ShapeDtypeStruct(mine.shape, jnp.float32),
             jax.ShapeDtypeStruct(mine.shape, jnp.bfloat16),
+        ]
+        + [
+            jax.ShapeDtypeStruct(mine.shape, jnp.float32),
+            jax.ShapeDtypeStruct(mine.shape, jnp.bfloat16),
         ],
-        compiler_params=params(),
+        compiler_params=params(32),
         cost_estimate=cost(6.5 * count),
     )(scalars, mine, theirs, *ups, expand_t, shrink_w, bias)
 
@@ -856,10 +868,6 @@
         for c in range(cores)
     ]
     return lax.ppermute(values, ("dp", "z", "core"), pairs)
-
-
-def swap_in(rows):
-    return trade(trade(rows, "dp", 0, 0), "z", 0, 0)
 
 
 def put_blocks(blocks, axis, dimension):
@@ -930,20 +938,20 @@
 
     all_ids = swap_planes(jnp.concatenate([segment_ids[0], encoder_ids[0]]))
     pack_ids, memory_ids = all_ids[:pack_rows], all_ids[pack_rows:]
-    raw = swap_in(inputs[0])
+    attend_at = lax.all_gather(attend_weights.T, "z", axis=0, tiled=True)
+    raw = trade(after(trade(inputs[0], "dp", 0, 0), attend_at), "z", 0, 0)
 
     def columns_of(weight, count):
         weight = weight.reshape(pieces, heads, count, head_size, block_rows)
         return weight.transpose(2, 1, 3, 0, 4).reshape(count * width, model_width)
 
-    near_w = jnp.concatenate(
-        [attend_weights.T, cross_memory.T, attend_output, cross_query.T, cross_output]
-    )
-    near_w = lax.all_gather(near_w, "z", axis=0, tiled=False)
-    heads_w = near_w[:, : 5 * width].reshape(planes * 5 * width, block_rows)
-    upstream = swap_in(after(output_cotangent[0], raw))
-    heads_w = trade(after(heads_w, upstream), "dp", 0, 0).reshape(pieces, 5 * width, block_rows)
-    squares = near_w[:, 5 * width :].reshape(planes, 3, width, block_rows)
+    near_w = jnp.concatenate([cross_memory.T, attend_output, cross_query.T, cross_output])
+    near_w = lax.all_gather(after(near_w, attend_at), "z", axis=0, tiled=True)
+    near_w = near_w.reshape(planes, 5 * width, block_rows)
+    attend_w = trade(after(attend_at, raw), "dp", 0, 0).reshape(pieces, 3 * width, block_rows)
+    upstream = trade(after(output_cotangent[0], attend_w), "dp", 0, 0)
+    squares = near_w[:, 2 * width :].reshape(planes, 3, width, block_rows)
+    cross_kv = near_w[:, : 2 * width].reshape(planes * 2 * width, block_rows)
     unit_w = jnp.stack([expand_weight.T, shrink_weight], axis=1)
     unit_parts = []
     for m in range(pieces):
@@ -951,10 +959,9 @@
         unit_parts.append(part if m == 0 else other(part, "dp", m))
     unit_w = put_blocks(unit_parts, "dp", 2).reshape(block_units, 2 * model_width)
     states = swap_planes(after(encoder_states[0], raw))
-    whole_units = lax.all_gather(after(unit_w, states), "z", axis=0, tiled=True)
+    whole_units = lax.all_gather(after(unit_w, near_w), "z", axis=0, tiled=True)
     expand_t, shrink_w = whole_units[:, :model_width], whole_units[:, model_width:]
-    attend_w = columns_of(heads_w[:, : 3 * width], 3)
-    cross_kv = columns_of(heads_w[:, 3 * width :], 2)
+    attend_w = columns_of(attend_w, 3)
 
     own = jnp.stack([core, piece]).astype(jnp.int32)
     key_block = min(256, pack_rows)
@@ -999,18 +1006,21 @@
 
     low_one = low(layer_norm(wide(raw), gain_rows[0], shift_rows[0]))
     mine = jnp.stack(chips_gather(after(low_one, unit_w)))
-    squares = after(squares, heads_w, mine)
+    mine, states = after((mine, states), attend_w, near_w)
+    squares = after(squares, mine)
+    state_parts = chips_gather(after(states, mine))
+    squares = after(squares, state_parts)
     ones = (mine, other(mine, "core", 1))
     square_parts = chips_gather(squares)
     query1, key1, value1, context1, kept1, lse1 = self_forward(
         self_scalars, *ones, planes, attend_w, packed_bias[None], self_first, self_last
     )
-    context1, square_parts = after((context1, square_parts))
+    context1, square_parts = after((context1, square_parts), upstream)
     squares = jnp.stack(square_parts)
     squares = (squares, other(squares, "core", 1))
     mixed1 = exchange(context1)
-    all_states = jnp.stack(chips_gather(after(states, mixed1)))
-    all_states = (all_states, other(all_states, "core", 1))
+    cross_kv = trade(after(cross_kv, mixed1), "dp", 0, 0).reshape(pieces, 2 * width, block_rows)
+    cross_kv = columns_of(cross_kv, 2)
     middle, low_two, query2 = single(
         middle_kernel,
         [flat_float, flat_low, head_low],
@@ -1022,15 +1032,17 @@
         *squares, query_bias,
     )
 
+    all_states = jnp.stack(state_parts)
+    all_states = (all_states, other(after(all_states, mixed1), "core", 1))
     query2 = exchange(query2)
     query2 = query2.reshape(part_shape)
     key2, value2, context2, kept2, lse2 = cross_forward(
         cross_scalars, query2, *all_states, cross_kv, memory_bias[None],
         cross_first, cross_last,
     )
-    ups = chips_gather(after(upstream, query2))
-    context2, ups = after((context2, ups))
-    ups = jnp.stack(ups)
+    upstream = trade(after(upstream, query2), "z", 0, 0)
+    context2, upstream = after((context2, upstream))
+    ups = jnp.stack(chips_gather(upstream))
     all_ups = (ups, other(ups, "core", 1))
     context2 = after(context2, whole_units)
     mixed2 = exchange(context2)
@@ -1049,13 +1061,13 @@
     ).reshape(1, unit_count)
     groups = [list(range(pieces - 1)), [pieces - 1]]
     pieces3 = chips_gather(low_three)
-    threes, actives, d_hiddens, parts3, leaving = [], [], [], [], []
+    threes, actives, d_hiddens, parts3, leaving, out_groups = [], [], [], [], [], []
     for group in groups:
         mine = jnp.stack([pieces3[m] for m in group])
         if d_hiddens:
             mine = after(mine, d_hiddens[-1])
         theirs = other(mine, "core", 1)
-        active, d_hidden, d_mine, d_theirs = units_group(
+        active, d_hidden, d_mine, d_theirs, out_mine, out_theirs = units_group(
             own, mine, theirs, all_ups, group[0], expand_t, shrink_w, bias_units
         )
         d_sum = d_mine + wide(other(d_theirs, "core", 1))
@@ -1063,6 +1075,7 @@
             leaving.append(d_sum[i] if m == 0 else low(d_sum[i]))
             parts3.append(leaving[-1] if m == 0 else other(leaving[-1], "dp", m))
         threes.append((mine, theirs))
+        out_groups.append((out_mine, out_theirs))
         actives.append(active)
         d_hiddens.append(d_hidden)
     actives, d_hiddens = after((actives, d_hiddens), leaving)
@@ -1079,20 +1092,10 @@
         own, *parts3, upstream, later, gain_rows[2:3], *squares,
     )
 
-    actives = after(actives, low_later)
-    outs = [
-        jnp.concatenate(
-            [
-                product(active[j].reshape(-1, unit_count), shrink_w).reshape(
-                    len(group), row_count, model_width
-                )
-                for group, active in zip(groups, actives)
-            ]
-        )
-        for j in range(cores)
+    out_groups = [
+        mine + wide(other(after(theirs, low_later), "core", 1)) for mine, theirs in out_groups
     ]
-    outs = outs[0] + wide(other(low(outs[1]), "core", 1))
-
+    outs = [group[i] for group in out_groups for i in range(group.shape[0])]
     d_context2 = exchange(d_context2)
     leaving = after([low(out) for out in outs[1:]], d_context2)
     out_parts = [other(out, "dp", m + 1) for m, out in enumerate(leaving)]
@@ -1111,22 +1114,53 @@
         own, d_mixed2, *squares, d_later, middle, gain_rows[1:2], *squares,
     )
     d_context1, unit_grads = after((exchange(d_context1), unit_grads))
-    layer_rows = after(layer_rows, unit_grads)
-    layer_first = trade(layer_rows, "z", 0, 0)
-    unit_grads = unit_grads.reshape(block_units, 2, pieces, block_rows).transpose(2, 0, 1, 3)
-    unit_grads = trade(unit_grads.reshape(unit_count, 2, block_rows), "dp", 0, 0)
-    d_states = [
-        product(part.reshape(-1, 2 * width), cross_kv).reshape(pieces, memory_rows, model_width)
-        for part in after(d_memory, d_context1)
-    ]
-    d_states = d_states[0] + wide(other(low(d_states[1]), "core", 1))
-    leaving = [low(d_states[m]) for m in range(1, pieces)]
-    state_parts = [other(part, "dp", m + 1) for m, part in enumerate(leaving)]
-
+
+    def turned_grad(columns, rows):
+        half = columns.shape[1] // cores
+        return low(
+            sum(
+                product(columns[:, j * half : (j + 1) * half], rows[j].reshape(half, model_width))
+                for j in range(cores)
+            )
+        )
+
+    def to_chips(*grads):
+        split = [grad.reshape(-1, pieces, block_rows) for grad in grads]
+        return trade(jnp.concatenate(split).transpose(1, 0, 2), "dp", 0, 0)
+
+    unit_grads = to_chips(
+        unit_grads.reshape(2 * block_units, model_width),
+        turned_grad(after(d_memory_t, d_context1), all_states),
+    )
     d_query1, d_query1_t, d_memory1, d_memory1_t = attend_back(
         self_scalars, query1.reshape(part_shape), key1, value1, d_context1.reshape(part_shape), kept1, lse1,
         self_first, self_last, True,
     )
+    d_query1, d_query1_t, d_memory1, d_memory1_t, unit_grads = after(
+        (d_query1, d_query1_t, d_memory1, d_memory1_t, unit_grads)
+    )
+    cross_sum = unit_grads[:, 2 * block_units :]
+    unit_grads = unit_grads[:, : 2 * block_units].reshape(unit_count, 2, block_rows)
+    d_ones = [
+        (
+            product(d_query1[j].reshape(-1, width), attend_w[:width])
+            + product(d_memory1[j].reshape(-1, 2 * width), attend_w[width:])
+        ).reshape(pieces, row_count, model_width)
+        for j in range(cores)
+    ]
+    d_sum = d_ones[0] + wide(other(low(d_ones[1]), "core", 1))
+    leaving = [low(d_sum[m]) for m in range(1, pieces)]
+    parts1 = [d_sum[0]] + [other(part, "dp", m + 1) for m, part in enumerate(leaving)]
+
+    d_memory, low_middle_late, layer_rows, turned_late = after(
+        (d_memory, low_middle, layer_rows, (d_query1_t, d_memory1_t)), leaving
+    )
+    layer_first = trade(layer_rows, "z", 0, 0)
+    d_states = [
+        product(part.reshape(-1, 2 * width), cross_kv).reshape(pieces, memory_rows, model_width)
+        for part in d_memory
+    ]
+    d_states = d_states[0] + wide(other(low(d_states[1]), "core", 1))
     kinds = 3
     square_shape = (pieces, planes, kinds, width, block_rows)
     square_mine, square_theirs = single(
@@ -1137,31 +1171,22 @@
         ],
         [None] * 6,
         [],
-        own, mixed1, after(low_middle, d_context1), d_mixed2, low_two, mixed2, low_later,
-    )
+        own, mixed1, low_middle_late, d_mixed2, low_two, mixed2, low_later,
+    )
+    attend_sum = [turned_grad(turned, ones) for turned in turned_late]
+    parts1, layer_first, d_states, square_mine, square_theirs, attend_sum = after(
+        (parts1, layer_first, d_states, square_mine, square_theirs, attend_sum)
+    )
+    attend_sum = to_chips(*attend_sum)
+    state_parts = [other(low(d_states[m]), "dp", m) for m in range(1, pieces)]
+    encoder_rows = low(d_states[0] + sum(wide(part) for part in state_parts))
+    encoder_gradient = swap_planes(encoder_rows)[None]
     square_theirs = other(square_theirs, "core", 1)
     square_sums = [wide(square_mine[m]) + wide(square_theirs[m]) for m in range(pieces)]
-    square_parts = [other(low(square_sums[m]), "dp", m) for m in range(1, pieces)]
-    d_query1, d_query1_t, d_memory1, d_memory1_t, square_parts, state_parts = after(
-        (d_query1, d_query1_t, d_memory1, d_memory1_t, square_parts, state_parts),
-        layer_first,
-        unit_grads,
-    )
-    layer_output = trade(layer_first, "dp", 0, 0)[None]
-    encoder_rows = low(d_states[0] + sum(wide(part) for part in state_parts))
-    encoder_gradient = swap_planes(after(encoder_rows, layer_first))[None]
+    square_parts = [
+        other(after(low(square_sums[m]), state_parts), "dp", m) for m in range(1, pieces)
+    ]
     square_sum = square_sums[0] + sum(wide(part) for part in square_parts)
-    d_ones = [
-        (
-            product(d_query1[j].reshape(-1, width), attend_w[:width])
-            + product(d_memory1[j].reshape(-1, 2 * width), attend_w[width:])
-        ).reshape(pieces, row_count, model_width)
-        for j in range(cores)
-    ]
-    d_sum = d_ones[0] + wide(other(low(d_ones[1]), "core", 1))
-    leaving = [low(d_sum[m]) for m in range(1, pieces)]
-    parts1 = [d_sum[0]] + [other(part, "dp", m + 1) for m, part in enumerate(leaving)]
-    parts1, encoder_gradient = after((parts1, encoder_gradient))
     input_gradient, sums1 = single(
         input_back_kernel,
         [flat_low, jax.ShapeDtypeStruct((2, model_width), jnp.float32)],
@@ -1169,26 +1194,9 @@
         [],
         own, *parts1, d_middle, raw, gain_rows[0:1],
     )
-    input_gradient = trade(trade(input_gradient, "z", 0, 0), "dp", 0, 0)[None]
-
-    def turned_grad(columns, rows):
-        half = columns.shape[1] // cores
-        return low(
-            sum(
-                product(columns[:, j * half : (j + 1) * half], rows[j].reshape(half, model_width))
-                for j in range(cores)
-            )
-        )
-
-    def to_chips(grad):
-        columns = grad.shape[0]
-        split = grad.reshape(columns, pieces, block_rows).transpose(1, 0, 2)
-        mine = trade(split.reshape(pieces * columns, block_rows), "dp", 0, 0)
-        return mine.reshape(planes, columns, block_rows)
-
-    cross_sum = to_chips(after(turned_grad(d_memory_t, all_states), d_query1))
-    attend_sum = jnp.concatenate([turned_grad(d_query1_t, ones), turned_grad(d_memory1_t, ones)])
-    attend_sum = to_chips(after(attend_sum, cross_sum))
+    input_gradient = trade(trade(after(input_gradient, attend_sum), "z", 0, 0), "dp", 0, 0)[None]
+    layer_output = trade(after(layer_first, input_gradient), "dp", 0, 0)[None]
+
     tail = jnp.concatenate(
         [low(square_sum).reshape(planes, 3 * width, block_rows), cross_sum, attend_sum], axis=1
     )

time: 734 us -> 661 us (0.901)
  local copies, waits for them, and re-layouts: 120 us -> 66.5 us
  waiting for transfers between devices: 229 us -> 187 us
  Pallas kernels: 113 us -> 144 us
  blocking collectives: 36.2 us -> 18.2 us
  starting transfers between devices: 136 us -> 152 us
  matrix products: 28.5 us -> 16 us
  other arithmetic: 42.1 us -> 50.4 us
    unnamed x247 -> x193, local copies, waits for them, and re-layouts: 63.1 us -> 20.6 us
    ppermute x53 -> x54, waiting for transfers between devices: 157 us -> 121 us  [other(): return lax.ppermute(values, axis, [(i, i ^ shift) for i in range(count)])]
    all_to_all x3 -> x0, blocking collectives: 36.2 us -> none  [trade(): lax.all_to_all(values, axis, split_axis=split, concat_axis=concat, tiled=...]
    all_gather x0 -> x1, blocking collectives: none -> 18.2 us  [shards(): attend_at = lax.all_gather(attend_weights.T, 'z', axis=0, tiled=True)]
    ppermute x3, waiting for transfers between devices: 15.9 us -> 0.01 us  [swap_planes(): return lax.ppermute(values, ('dp', 'z', 'core'), pairs)]
    pallas_call x6, Pallas kernels: 20 us -> 35.7 us  [single(): pl.pallas_call(kernel, grid_spec=pltpu.PrefetchScalarGridSpec(num_scalar_...]
    ppermute x53 -> x54, starting transfers between devices: 51.6 us -> 64.8 us  [other(): return lax.ppermute(values, axis, [(i, i ^ shift) for i in range(count)])]
    dot_general x16 -> x12, matrix products: 28.5 us -> 16 us  [product(): return jnp.dot(former, latter, preferred_element_type=jnp.float32)]
  transfers between devices with their start and end apart: 74 -> 78, of which waited for: 33 -> 29; matrix products, arithmetic and copies ran while one was open for 19% -> 15% of each run, Pallas kernels for 15% -> 22%
where the time goes in v3:
time: 661 us; the launch traced here: 650 us
  waiting for transfers between devices  187 us (28%)
  starting transfers between devices  152 us (23%)
  Pallas kernels  144 us (22%)
  local copies, waits for them, and re-layouts  66.5 us (10%)
  other arithmetic  50.4 us (8%)
  blocking collectives  18.2 us (3%)
  matrix products  16 us (2%)
  between operations  15.8 us (2%)
    ppermute x54, waiting for transfers between devices, other(): return lax.ppermute(values, axis, [(i, i ^ shift) for i in range(count)])  121 us
    all_to_all x18, starting transfers between devices, trade(): lax.all_to_all(values, axis, split_axis=split, concat_axis=concat, tiled=...  75.9 us
    all_to_all x18, waiting for transfers between devices, trade(): lax.all_to_all(values, axis, split_axis=split, concat_axis=concat, tiled=...  66.4 us
    ppermute x54, starting transfers between devices, other(): return lax.ppermute(values, axis, [(i, i ^ shift) for i in range(count)])  64.8 us
    pallas_call x6, Pallas kernels, single(): pl.pallas_call(kernel, grid_spec=pltpu.PrefetchScalarGridSpec(num_scalar_...  35.7 us
    pallas_call x2, Pallas kernels, units_group(): pl.pallas_call(functools.partial(units_kernel, half_count=count), grid_sp...  29.5 us
    pallas_call x2, Pallas kernels, attend_back(): pl.pallas_call(functools.partial(backward_kernel, heads=width // head_wid...  29.2 us
    unnamed x193, local copies, waits for them, and re-layouts  20.6 us
  transfers between devices with their start and end apart: 78, of which 29 were waited for; matrix products, arithmetic and copies ran while one was open for 15% of the time, Pallas kernels for 22%

profile of v3, /device:TPU:8, one launch (start us, length us, event | category | flops | bytes accessed | tf_op | source)
XLA Modules:
  0.0 650.4 jit_solution(834208391456715143)
XLA Ops:
  17.6 18.2 %all_gather.9 = bf16[1536,256]{0,1:T(8,128)(2,1)S(1)} all-gather(bf16[384,256]{0,1:T(8,128)(2,1)S(1)} %bitcast.352), channel_id=1, replica_groups=mesh['dp'=4,'z'=4,'core'=2] {'z'}, dimensions={0}, use_global_device_ids=true | all-gather | bytes 983040 | tf_op jit(solution)/shard_map/all_gather | solution.py:941
  49.0 12.1 %all-to-all-done.1 = bf16[4,64,1024]{2,1,0:T(8,128)(2,1)S(1)} async-done(((bf16[4,64,1024]{2,1,0:T(8,128)(2,1)}), bf16[4,64,1024]{2,1,0:T(8,128)(2,1)S(1)}, u32[]{:S(2)}, u32[]{:S(2)}) %all-to-all-start.1) | async-done | bytes 524320 | tf_op jit(solution)/shard_map/all_to_all | solution.py:835
  81.5 10.9 %all-to-all-done.2 = bf16[4,384,256]{2,1,0:T(8,128)(2,1)S(1)} async-done(((bf16[4,384,256]{2,1,0:T(8,128)(2,1)}), bf16[4,384,256]{2,1,0:T(8,128)(2,1)S(1)}, u32[]{:S(2)}, u32[]{:S(2)}) %all-to-all-start.2) | async-done | bytes 786464 | tf_op jit(solution)/shard_map/all_to_all | solution.py:835
  113.4 6.8 %collective-permute-done.9 = bf16[128,1024]{1,0:T(8,128)(2,1)S(1)} collective-permute-done((bf16[128,1024]{1,0:T(8,128)(2,1)}, bf16[128,1024]{1,0:T(8,128)(2,1)S(1)}, u32[]{:S(2)}, u32[]{:S(2)}) %collective-permute-start.9) | collective-permute-done | bytes 262176 | tf_op jit(solution)/shard_map/ppermute | solution.py:831
  129.4 17.2 %shard_map.297 = (bf16[2,4,256,128]{3,2,1,0:T(8,128)(2,1)}, bf16[2,4,256,128]{3,2,1,0:T(8,128)(2,1)}, bf16[2,4,256,128]{3,2,1,0:T(8,128)(2,1)}, bf16[2,4,4,64,12...) custom-call(s32[18]{0:T(128)} %pad_add_fusion.1.scalars, bf16[4,256,1024]{2,1,0:T(8,128)(2,1)} %copy-done.14, ...), custom_call_target="tpu_custom_call" | custom-call | flops 17600000000 | bytes 1048576 | tf_op jit(solution)/shard_map/pallas_call | solution.py:335
  146.7 16.7 %collective-permute-done.13 = bf16[4,3,128,256]{3,2,1,0:T(8,128)(2,1)} collective-permute-done((bf16[4,3,128,256]{3,2,1,0:T(8,128)(2,1)}, bf16[4,3,128,256]{3,2,1,0:T(8,128)(2,1)}, u32[]{:S(2)}, u32[]{:S(2)}) %collective-permute-start.13) | collective-permute-done | bytes 786464 | tf_op jit(solution)/shard_map/ppermute | solution.py:831
  206.9 6.8 %all-to-all-start.7 = ((bf16[4,64,1024]{2,1,0:T(8,128)(2,1)}), bf16[4,64,1024]{2,1,0:T(8,128)(2,1)S(1)}, u32[]{:S(2)}, u32[]{:S(2)}) async-start(bf16[4,64,1024]{2,1,0:T(8,128)(2,1)} %bitcast.54), calls=%async_computation.7 | async-start | bytes 1048576 | tf_op jit(solution)/shard_map/all_to_all | solution.py:835
  214.7 14.5 %shard_map.299 = (bf16[2,4,128,128]{3,2,1,0:T(8,128)(2,1)}, bf16[2,4,128,128]{3,2,1,0:T(8,128)(2,1)}, bf16[2,4,4,64,128]{4,3,2,1,0:T(8,128)(2,1)}, f32[8,128,256]{2,1,0:T(8,128)}, f32[8,1,512]{2,1,0:T(1,128)}) custom-call(s32[18]{0:T(128)} %pad_add_fusion.4.scalars, bf16[2,4,4,64,128]{4,3,2,1,0:T(8,128)(2,1)} %bitcast.332, bf16[4,128,1024]{2,1,0:T(8,128)(2,1)} %copy-done.27, ...), custom_call_target="tpu_custom_call" | custom-call | flops 12099999744 | bytes 1048576 | tf_op jit(solution)/shard_map/pallas_call | solution.py:371
  253.2 12.2 %collective-permute-done.22 = bf16[256,1024]{1,0:T(8,128)(2,1)S(1)} collective-permute-done((bf16[256,1024]{1,0:T(8,128)(2,1)S(1)}, bf16[256,1024]{1,0:T(8,128)(2,1)S(1)}, u32[]{:S(2)}, u32[]{:S(2)}) %collective-permute-start.22) | collective-permute-done | bytes 524320 | tf_op jit(solution)/shard_map/ppermute | solution.py:831
  268.0 7.3 %collective-permute-done.17 = bf16[256,1024]{1,0:T(8,128)(2,1)S(1)} collective-permute-done((bf16[256,1024]{1,0:T(8,128)(2,1)}, bf16[256,1024]{1,0:T(8,128)(2,1)S(1)}, u32[]{:S(2)}, u32[]{:S(2)}) %collective-permute-start.17) | collective-permute-done | bytes 524320 | tf_op jit(solution)/shard_map/ppermute | solution.py:831
  280.9 21.5 %shard_map.301 = (bf16[2,3,256,1024]{3,2,1,0:T(8,128)(2,1)S(1)}, bf16[2,3,256,1024]{3,2,1,0:T(8,128)(2,1)S(1)}, f32[3,256,1024]{2,1,0:T(8,128)}, bf16[3,256,1024...) custom-call(s32[2]{0:T(128)S(1)} %copy-done.11, ...), custom_call_target="tpu_custom_call" | custom-call | flops 21450000384 | bytes 1048576 | tf_op jit(solution)/shard_map/pallas_call | solution.py:679
  306.1 8.0 %shard_map.302 = (bf16[2,1,256,1024]{3,2,1,0:T(8,128)(2,1)S(1)}, bf16[2,1,256,1024]{3,2,1,0:T(8,128)(2,1)S(1)}, f32[1,256,1024]{2,1,0:T(8,128)S(1)}, bf16[1,256,...) custom-call(s32[2]{0:T(128)S(1)} %copy-done.11, ...), custom_call_target="tpu_custom_call" | custom-call | flops 7150000128 | bytes 1048576 | tf_op jit(solution)/shard_map/pallas_call | solution.py:679
  321.7 17.9 %shard_map.303 = bf16[1024,2048]{1,0:T(8,128)(2,1)} custom-call(s32[2]{0:T(128)} %pad_add_fusion.3.scalars, bf16[2,3,256,1024]{3,2,1,0:T(8,128)(2,1)} %copy-done, bf16[2,1,256,1024]{3,2,1,0:T(8,128)(2,1)} %copy-done.3, bf16[2,3,256,1024]{3,2,1,0:T(8,128)(2,1)} %copy-done.12, bf16[2,1,256,1024]{3,2,1,0:T(8,128)(2,1)} %copy-done.13, ...), custom_call_target="tpu_custom_call" | custom-call | flops 13200000000 | bytes 1048576 | tf_op jit(solution)/shard_map/pallas_call | solution.py:782
  364.3 13.5 %shard_map.305 = (bf16[2,4,4,64,128]{4,3,2,1,0:T(8,128)(2,1)}, bf16[2,4,128,256]{3,2,1,0:T(8,128)(2,1)}, bf16[256,1024]{1,0:T(8,128)(2,1)}) custom-call(s32[18]{0:T(128)} %pad_add_fusion.4.scalars, bf16[2,4,4,64,128]{4,3,2,1,0:T(8,128)(2,1)} %bitcast.333, bf16[2,4,128,128]{3,2,1,0:T(8,128)(2,1)} %get-tuple-element.151.k_ref, ...), custom_call_target="tpu_custom_call" | custom-call | flops 13200000000 | bytes 1048576 | tf_op jit(solution)/shard_map/pallas_call | solution.py:409
  377.8 10.0 %collective-permute-done.34 = bf16[256,1024]{1,0:T(8,128)(2,1)S(1)} collective-permute-done((bf16[256,1024]{1,0:T(8,128)(2,1)}, bf16[256,1024]{1,0:T(8,128)(2,1)S(1)}, u32[]{:S(2)}, u32[]{:S(2)}) %collective-permute-start.34) | collective-permute-done | bytes 524320 | tf_op jit(solution)/shard_map/ppermute | solution.py:831
  402.3 7.1 %shard_map.306 = (f32[256,1024]{1,0:T(8,128)}, bf16[256,1024]{1,0:T(8,128)(2,1)}, bf16[2,4,256,128]{3,2,1,0:T(8,128)(2,1)}, f32[3,1024]{1,0:T(4,128)}) custom-call(s32[2]{0:T(128)} %pad_add_fusion.3.scalars, bf16[2,4,256,128]{3,2,1,0:T(8,128)(2,1)} %bitcast.303, bf16[4,4,3,128,256]{4,3,2,1,0:T(8,128)(2,1)} %pad_maximum_fusion.omine_ref.qmine_ref.refs_7_.mine_ref, ...), custom_call_target="tpu_custom_call" | custom-call | flops 4400000000 | bytes 1048576 | tf_op jit(solution)/shard_map/pallas_call | solution.py:451
  414.4 8.5 %all-to-all-done.11 = bf16[8,256,128]{2,1,0:T(8,128)(2,1)} async-done(((bf16[8,256,128]{2,1,0:T(8,128)(2,1)}), bf16[8,256,128]{2,1,0:T(8,128)(2,1)}, u32[]{:S(2)}, u32[]{:S(2)}) %all-to-all-start.11) | async-done | bytes 524320 | tf_op jit(solution)/shard_map/all_to_all | solution.py:835
  432.3 15.7 %shard_map.307 = (bf16[2,4,4,64,128]{4,3,2,1,0:T(8,128)(2,1)}, bf16[128,2048]{1,0:T(8,128)(2,1)}, bf16[2,4,256,256]{3,2,1,0:T(8,128)(2,1)}, bf16[256,2048]{1,0:T(8,128)(2,1)}) custom-call(s32[18]{0:T(128)} %pad_add_fusion.1.scalars, bf16[2,4,4,64,128]{4,3,2,1,0:T(8,128)(2,1)} %bitcast.386, bf16[2,4,256,128]{3,2,1,0:T(8,128)(2,1)} %get-tuple-element.136.k_ref, ...), custom_call_target="tpu_custom_call" | custom-call | flops 13200000000 | bytes 1048576 | tf_op jit(solution)/shard_map/pallas_call | solution.py:409
  487.9 7.0 %shard_map.308 = (bf16[4,4,3,128,256]{4,3,2,1,0:T(8,128)(2,1)}, bf16[4,4,3,128,256]{4,3,2,1,0:T(8,128)(2,1)}) custom-call(s32[2]{0:T(128)} %pad_add_fusion.3.scalars, bf16[2,4,256,128]{3,2,1,0:T(8,128)(2,1)} %bitcast.329, bf16[256,1024]{1,0:T(8,128)(2,1)} %get-tuple-element.215.refs_1_, bf16[2,4,256,128]{3,2,1,0:T(8,128)(2,1)} %bitcast.304, ...), custom_call_target="tpu_custom_call" | custom-call | flops 4400000000 | bytes 1048576 | tf_op jit(solution)/shard_map/pallas_call | solution.py:451
  564.9 8.6 %collective-permute-done.51 = bf16[4,3,128,256]{3,2,1,0:T(8,128)(2,1)} collective-permute-done((bf16[4,3,128,256]{3,2,1,0:T(8,128)(2,1)}, bf16[4,3,128,256]{3,2,1,0:T(8,128)(2,1)}, u32[]{:S(2)}, u32[]{:S(2)}) %collective-permute-start.51) | collective-permute-done | bytes 786464 | tf_op jit(solution)/shard_map/ppermute | solution.py:831
  573.5 7.4 %collective-permute-done.53 = bf16[4,3,128,256]{3,2,1,0:T(8,128)(2,1)} collective-permute-done((bf16[4,3,128,256]{3,2,1,0:T(8,128)(2,1)}, bf16[4,3,128,256]{3,2,1,0:T(8,128)(2,1)}, u32[]{:S(2)}, u32[]{:S(2)}) %collective-permute-start.53) | collective-permute-done | bytes 786464 | tf_op jit(solution)/shard_map/ppermute | solution.py:831
  585.0 8.5 %collective-permute-start.54 = (bf16[1024,256]{1,0:T(8,128)(2,1)}, bf16[1024,256]{1,0:T(8,128)(2,1)}, u32[]{:S(2)}, u32[]{:S(2)}) collective-permute-start(bf16[1024,256]{1,0:T(8,128)(2,1)} %get-tuple-element.324), channel_id=1, source_target_pairs={{0,2},{2,0},{4,6},{6,4},{1,3},{3,1},{5,7},{7,5},{8,10},{10,8},{12,... | collective-permute-start | bytes 1572872 | tf_op jit(solution)/shard_map/ppermute | solution.py:831
  607.6 20.6 %collective-permute-done.55 = bf16[1024,256]{1,0:T(8,128)(2,1)} collective-permute-done((bf16[1024,256]{1,0:T(8,128)(2,1)}, bf16[1024,256]{1,0:T(8,128)(2,1)}, u32[]{:S(2)}, u32[]{:S(2)}) %collective-permute-start.55) | collective-permute-done | bytes 524320 | tf_op jit(solution)/shard_map/ppermute | solution.py:831
  628.2 8.1 %collective-permute-done.56 = bf16[1024,256]{1,0:T(8,128)(2,1)} collective-permute-done((bf16[1024,256]{1,0:T(8,128)(2,1)}, bf16[1024,256]{1,0:T(8,128)(2,1)}, u32[]{:S(2)}, u32[]{:S(2)}) %collective-permute-start.56) | collective-permute-done | bytes 524320 | tf_op jit(solution)/shard_map/ppermute | solution.py:831
  (496 shorter events, 349.2 us)
Async XLA Ops:
  9.8 33.9 %collective-permute-start.1 = (bf16[256,2,256]{2,0,1:T(8,128)(2,1)S(1)}, bf16[256,2,256]{2,0,1:T(8,128)(2,1)}, u32[]{:S(2)}, u32[]{:S(2)}) collective-permute-start(bf16[256,2,256]{2,0,1:T(8,128)(2,1)S(1)} %get-tuple-element.344), channel_id=1, source_target_pairs={{0,8},{8,0},{16,24},{24,16},{1,9},{9,1},{17,25},{25,17},{2,10},{10... | collective-permute-start | bytes 786440 | tf_op jit(solution)/shard_map/ppermute | solution.py:831
  11.4 33.7 %collective-permute-start.2 = (bf16[256,2,256]{2,0,1:T(8,128)(2,1)S(1)}, bf16[256,2,256]{2,0,1:T(8,128)(2,1)}, u32[]{:S(2)}, u32[]{:S(2)}) collective-permute-start(bf16[256,2,256]{2,0,1:T(8,128)(2,1)S(1)} %get-tuple-element.345), channel_id=1, source_target_pairs={{0,16},{8,24},{16,0},{24,8},{1,17},{9,25},{17,1},{25,9},{2,18},{10... | collective-permute-start | bytes 786440 | tf_op jit(solution)/shard_map/ppermute | solution.py:831
  12.9 33.5 %collective-permute-start.3 = (bf16[256,2,256]{2,0,1:T(8,128)(2,1)S(1)}, bf16[256,2,256]{2,0,1:T(8,128)(2,1)}, u32[]{:S(2)}, u32[]{:S(2)}) collective-permute-start(bf16[256,2,256]{2,0,1:T(8,128)(2,1)S(1)} %get-tuple-element.342), channel_id=1, source_target_pairs={{0,24},{8,16},{16,8},{24,0},{1,25},{9,17},{17,9},{25,1},{2,26},{10... | collective-permute-start | bytes 786440 | tf_op jit(solution)/shard_map/ppermute | solution.py:831
  17.5 76.6 %all-gather.3.cloned.1.call-start = ((), (), s32[]{:S(2)}) async-start(), calls=%async_computation.19 | async-start | bytes 1638400 | tf_op jit(solution)/shard_map/all_gather | solution.py:949
  97.8 31.7 %collective-permute-start.8 = (bf16[4,256,1024]{2,1,0:T(8,128)(2,1)S(1)}, bf16[4,256,1024]{2,1,0:T(8,128)(2,1)}, u32[]{:S(2)}, u32[]{:S(2)}) collective-permute-start(bf16[4,256,1024]{2,1,0:T(8,128)(2,1)S(1)} %pad_maximum_fusion.1.mine_ref), channel_id=1, source_target_pairs={{0,1},{1,0},{2,3},{3,2},{4,5},{5,4},{6,7},{7,6},{8,9},{9,8},{10,11... | collective-permute-start | bytes 6291464 | tf_op jit(solution)/shard_map/ppermute | solution.py:831
  101.0 45.6 %all-to-all-start.3 = ((bf16[4,64,1024]{2,1,0:T(8,128)(2,1)}), bf16[4,64,1024]{2,1,0:T(8,128)(2,1)}, u32[]{:S(2)}, u32[]{:S(2)}) async-start(bf16[4,64,1024]{2,1,0:T(8,128)(2,1)} %bitcast.32), calls=%async_computation.3 | async-start | bytes 1048576 | tf_op jit(solution)/shard_map/all_to_all | solution.py:835
  105.2 124.0 %all-gather.5.cloned.1.call-start = ((), (), s32[]{:S(2)}) async-start(), calls=%async_computation.20 | async-start | bytes 5242880 | tf_op jit(solution)/shard_map/all_gather | solution.py:962
  127.5 35.9 %collective-permute-start.13 = (bf16[4,3,128,256]{3,2,1,0:T(8,128)(2,1)}, bf16[4,3,128,256]{3,2,1,0:T(8,128)(2,1)}, u32[]{:S(2)}, u32[]{:S(2)}) collective-permute-start(bf16[4,3,128,256]{3,2,1,0:T(8,128)(2,1)} %bitcast.294), channel_id=1, source_target_pairs={{0,16},{8,24},{16,0},{24,8},{1,17},{9,25},{17,1},{25,9},{2,18},{10... | collective-permute-start | bytes 2359304 | tf_op jit(solution)/shard_map/ppermute | solution.py:831
  127.5 35.9 %collective-permute-start.14 = (bf16[4,3,128,256]{3,2,1,0:T(8,128)(2,1)}, bf16[4,3,128,256]{3,2,1,0:T(8,128)(2,1)}, u32[]{:S(2)}, u32[]{:S(2)}) collective-permute-start(bf16[4,3,128,256]{3,2,1,0:T(8,128)(2,1)} %bitcast.295), channel_id=1, source_target_pairs={{0,24},{8,16},{16,8},{24,0},{1,25},{9,17},{17,9},{25,1},{2,26},{10... | collective-permute-start | bytes 2359304 | tf_op jit(solution)/shard_map/ppermute | solution.py:831
  180.0 33.7 %collective-permute-start.16 = (bf16[4,128,1024]{2,1,0:T(8,128)(2,1)S(1)}, bf16[4,128,1024]{2,1,0:T(8,128)(2,1)S(1)}, u32[]{:S(2)}, u32[]{:S(2)}) collective-permute-start(bf16[4,128,1024]{2,1,0:T(8,128)(2,1)S(1)} %pad_maximum_fusion.5.mine_ref), channel_id=1, source_target_pairs={{0,1},{1,0},{2,3},{3,2},{4,5},{5,4},{6,7},{7,6},{8,9},{9,8},{10,11... | collective-permute-start | bytes 3145736 | tf_op jit(solution)/shard_map/ppermute | solution.py:831
  232.7 190.2 %reduce-scatter.2.cloned.1.call-start = ((), (), s32[]{:S(2)}) async-start(), calls=%async_computation.21 | async-start | bytes 5242880 | tf_op jit(solution)/shard_map/reduce_scatter | solution.py:1085
  236.1 29.3 %collective-permute-start.22 = (bf16[256,1024]{1,0:T(8,128)(2,1)S(1)}, bf16[256,1024]{1,0:T(8,128)(2,1)S(1)}, u32[]{:S(2)}, u32[]{:S(2)}) collective-permute-start(bf16[256,1024]{1,0:T(8,128)(2,1)S(1)} %bitcast.285), channel_id=1, source_target_pairs={{0,24},{8,16},{16,8},{24,0},{1,25},{9,17},{17,9},{25,1},{2,26},{10... | collective-permute-start | bytes 1572872 | tf_op jit(solution)/shard_map/ppermute | solution.py:831
  247.5 27.7 %collective-permute-start.17 = (bf16[256,1024]{1,0:T(8,128)(2,1)}, bf16[256,1024]{1,0:T(8,128)(2,1)S(1)}, u32[]{:S(2)}, u32[]{:S(2)}) collective-permute-start(bf16[256,1024]{1,0:T(8,128)(2,1)} %get-tuple-element.159), channel_id=1, source_target_pairs={{0,8},{8,0},{16,24},{24,16},{1,9},{9,1},{17,25},{25,17},{2,10},{10... | collective-permute-start | bytes 1572872 | tf_op jit(solution)/shard_map/ppermute | solution.py:831
  471.0 28.4 %collective-permute-start.37 = (bf16[256,1024]{1,0:T(8,128)(2,1)}, bf16[256,1024]{1,0:T(8,128)(2,1)}, u32[]{:S(2)}, u32[]{:S(2)}) collective-permute-start(bf16[256,1024]{1,0:T(8,128)(2,1)} %get-tuple-element.329), channel_id=1, source_target_pairs={{0,8},{8,0},{16,24},{24,16},{1,9},{9,1},{17,25},{25,17},{2,10},{10... | collective-permute-start | bytes 1572872 | tf_op jit(solution)/shard_map/ppermute | solution.py:831
  472.5 27.0 %collective-permute-start.38 = (bf16[256,1024]{1,0:T(8,128)(2,1)}, bf16[256,1024]{1,0:T(8,128)(2,1)}, u32[]{:S(2)}, u32[]{:S(2)}) collective-permute-start(bf16[256,1024]{1,0:T(8,128)(2,1)} %get-tuple-element.328), channel_id=1, source_target_pairs={{0,16},{8,24},{16,0},{24,8},{1,17},{9,25},{17,1},{25,9},{2,18},{10... | collective-permute-start | bytes 1572872 | tf_op jit(solution)/shard_map/ppermute | solution.py:831
  499.8 37.2 %collective-permute-start.50 = (bf16[4,4,3,128,256]{4,3,2,1,0:T(8,128)(2,1)}, bf16[4,4,3,128,256]{4,3,2,1,0:T(8,128)(2,1)}, u32[]{:S(2)}, u32[]{:S(2)}) collective-permute-start(bf16[4,4,3,128,256]{4,3,2,1,0:T(8,128)(2,1)} %get-tuple-element.237), channel_id=1, source_target_pairs={{0,1},{1,0},{2,3},{3,2},{4,5},{5,4},{6,7},{7,6},{8,9},{9,8},{10,11... | collective-permute-start | bytes 9437192 | tf_op jit(solution)/shard_map/ppermute | solution.py:831
  532.8 27.7 %all-to-all-start.15 = ((bf16[4,64,1024]{2,1,0:T(8,128)(2,1)}), bf16[4,64,1024]{2,1,0:T(8,128)(2,1)}, u32[]{:S(2)}, u32[]{:S(2)}) async-start(bf16[4,64,1024]{2,1,0:T(8,128)(2,1)} %bitcast.103), calls=%async_computation.16 | async-start | bytes 1048576 | tf_op jit(solution)/shard_map/all_to_all | solution.py:835
  541.4 32.1 %collective-permute-start.51 = (bf16[4,3,128,256]{3,2,1,0:T(8,128)(2,1)}, bf16[4,3,128,256]{3,2,1,0:T(8,128)(2,1)}, u32[]{:S(2)}, u32[]{:S(2)}) collective-permute-start(bf16[4,3,128,256]{3,2,1,0:T(8,128)(2,1)} %get-tuple-element.238), channel_id=1, source_target_pairs={{0,8},{8,0},{16,24},{24,16},{1,9},{9,1},{17,25},{25,17},{2,10},{10... | collective-permute-start | bytes 2359304 | tf_op jit(solution)/shard_map/ppermute | solution.py:831
  542.0 31.5 %collective-permute-start.52 = (bf16[4,3,128,256]{3,2,1,0:T(8,128)(2,1)}, bf16[4,3,128,256]{3,2,1,0:T(8,128)(2,1)}, u32[]{:S(2)}, u32[]{:S(2)}) collective-permute-start(bf16[4,3,128,256]{3,2,1,0:T(8,128)(2,1)} %get-tuple-element.239), channel_id=1, source_target_pairs={{0,16},{8,24},{16,0},{24,8},{1,17},{9,25},{17,1},{25,9},{2,18},{10... | collective-permute-start | bytes 2359304 | tf_op jit(solution)/shard_map/ppermute | solution.py:831
  542.6 38.3 %collective-permute-start.53 = (bf16[4,3,128,256]{3,2,1,0:T(8,128)(2,1)}, bf16[4,3,128,256]{3,2,1,0:T(8,128)(2,1)}, u32[]{:S(2)}, u32[]{:S(2)}) collective-permute-start(bf16[4,3,128,256]{3,2,1,0:T(8,128)(2,1)} %get-tuple-element.240), channel_id=1, source_target_pairs={{0,24},{8,16},{16,8},{24,0},{1,25},{9,17},{17,9},{25,1},{2,26},{10... | collective-permute-start | bytes 2359304 | tf_op jit(solution)/shard_map/ppermute | solution.py:831
  557.4 46.1 %collective-permute-start.44 = (bf16[128,1024]{1,0:T(8,128)(2,1)}, bf16[128,1024]{1,0:T(8,128)(2,1)S(1)}, u32[]{:S(2)}, u32[]{:S(2)}) collective-permute-start(bf16[128,1024]{1,0:T(8,128)(2,1)} %fusion.17), channel_id=1, source_target_pairs={{0,0},{1,1},{2,8},{3,9},{4,16},{5,17},{6,24},{7,25},{8,2},{9,3},{1... | collective-permute-start | bytes 786440 | tf_op jit(solution)/shard_map/ppermute | solution.py:870
  560.5 37.0 %all-to-all-start.16 = ((bf16[4,64,1024]{2,1,0:T(8,128)(2,1)}), bf16[4,64,1024]{2,1,0:T(8,128)(2,1)S(1)}, u32[]{:S(2)}, u32[]{:S(2)}) async-start(bf16[4,64,1024]{2,1,0:T(8,128)(2,1)} %all-to-all-done.15), calls=%async_computation.17 | async-start | bytes 1048576 | tf_op jit(solution)/shard_map/all_to_all | solution.py:835
  593.4 34.8 %collective-permute-start.55 = (bf16[1024,256]{1,0:T(8,128)(2,1)}, bf16[1024,256]{1,0:T(8,128)(2,1)}, u32[]{:S(2)}, u32[]{:S(2)}) collective-permute-start(bf16[1024,256]{1,0:T(8,128)(2,1)} %get-tuple-element.326), channel_id=1, source_target_pairs={{0,4},{2,6},{4,0},{6,2},{1,5},{3,7},{5,1},{7,3},{8,12},{10,14},{12... | collective-permute-start | bytes 1572872 | tf_op jit(solution)/shard_map/ppermute | solution.py:831
  596.3 40.0 %collective-permute-start.56 = (bf16[1024,256]{1,0:T(8,128)(2,1)}, bf16[1024,256]{1,0:T(8,128)(2,1)}, u32[]{:S(2)}, u32[]{:S(2)}) collective-permute-start(bf16[1024,256]{1,0:T(8,128)(2,1)} %get-tuple-element.325), channel_id=1, source_target_pairs={{0,6},{2,4},{4,2},{6,0},{1,7},{3,5},{5,3},{7,1},{8,14},{10,12},{12... | collective-permute-start | bytes 1572872 | tf_op jit(solution)/shard_map/ppermute | solution.py:831
  (140 other events, 2167.9 us)
Sparse Core Ops, SparseCore 0:
  37.0 40.2 all-gather.2
  113.5 81.7 all-gather.4
  342.8 77.3 reduce-scatter.1

commit v4 on v3

--- a/solution.py
+++ b/solution.py
@@ -188,6 +188,7 @@
     *rest, heads, key_block, planes, near,
 ):
     if near:
+        weight_ref, dmine_ref, dtheirs_ref, *rest = rest
         dq_ref, dqt_ref, dkv_ref, dkvt_ref, keys, values, flipped, dkeys, dvalues = rest
     else:
         dq_ref, dkv_ref, dkvt_ref, keys, values, flipped, dkeys, dvalues = rest
@@ -272,8 +273,20 @@
                     dkv_ref[slot[0], slot[1], first : first + part, column : column + width] = (
                         total[here, :].astype(jnp.bfloat16)
                     )
-        for j in range(cores):
+        for j in reversed(range(cores)):
             for m in range(pieces):
+                if near:
+                    rows_grad = jnp.dot(
+                        dq_ref[j, m].reshape(key_rows, width),
+                        weight_ref[:width],
+                        preferred_element_type=jnp.float32,
+                    ) + jnp.dot(
+                        dkv_ref[j, m], weight_ref[width:], preferred_element_type=jnp.float32
+                    )
+                    if j == 0:
+                        dmine_ref[m] = rows_grad
+                    else:
+                        dtheirs_ref[m] = rows_grad.astype(jnp.bfloat16)
                 place = (j * pieces + m) * key_rows
                 dkvt_ref[:, place : place + key_rows] = flip(dkv_ref[j, m])
                 if near:
@@ -394,7 +407,8 @@
     )(scalars, queries, mine, theirs, weight, bias, first, last)
 
 
-def attend_back(scalars, queries, key_rows, values, grad, kept, lse, first, last, near):
+def attend_back(scalars, queries, key_rows, values, grad, kept, lse, first, last, weight=None):
+    near = weight is not None
     cores, pieces, planes, rows, width = queries.shape
     steps = cores * planes
     key_shape = key_rows.shape
@@ -402,8 +416,14 @@
     key_block = min(256, key_count)
     dq_shape = jax.ShapeDtypeStruct(queries.shape, jnp.bfloat16)
     if near:
-        dq_shapes = [dq_shape, jax.ShapeDtypeStruct((width, key_count), jnp.bfloat16)]
-        dq_specs = [whole_spec(queries.shape), whole_spec((width, key_count))]
+        row_shape = (pieces, planes * rows, weight.shape[1])
+        dq_shapes = [
+            jax.ShapeDtypeStruct(row_shape, jnp.float32),
+            jax.ShapeDtypeStruct(row_shape, jnp.bfloat16),
+            dq_shape,
+            jax.ShapeDtypeStruct((width, key_count), jnp.bfloat16),
+        ]
+        dq_specs = [whole_spec(shape.shape) for shape in dq_shapes]
     else:
         dq_shapes, dq_specs = [dq_shape], [member_spec(queries.shape, False)]
     return pl.pallas_call(
@@ -426,7 +446,8 @@
                 step_spec(lse.shape),
                 step_spec(first.shape),
                 step_spec(last.shape),
-            ],
+            ]
+            + ([whole_spec(weight.shape)] if near else []),
             out_specs=dq_specs
             + [whole_spec(key_shape[:3] + (2 * width,)), whole_spec((2 * width, key_count))],
             scratch_shapes=[
@@ -444,7 +465,10 @@
         ],
         compiler_params=params(),
         cost_estimate=cost(12),
-    )(scalars, queries, key_rows, values, grad, kept, lse, first, last)
+    )(
+        scalars, queries, key_rows, values, grad, kept, lse, first, last,
+        *([weight] if near else []),
+    )
 
 
 def single(kernel, out_shape, in_specs, scratch, *args):
@@ -1008,6 +1032,7 @@
     mine = jnp.stack(chips_gather(after(low_one, unit_w)))
     mine, states = after((mine, states), attend_w, near_w)
     squares = after(squares, mine)
+    upstream = trade(upstream, "z", 0, 0)
     state_parts = chips_gather(after(states, mine))
     squares = after(squares, state_parts)
     ones = (mine, other(mine, "core", 1))
@@ -1040,9 +1065,9 @@
         cross_scalars, query2, *all_states, cross_kv, memory_bias[None],
         cross_first, cross_last,
     )
-    upstream = trade(after(upstream, query2), "z", 0, 0)
-    context2, upstream = after((context2, upstream))
-    ups = jnp.stack(chips_gather(upstream))
+    ups = chips_gather(after(upstream, query2))
+    context2, ups = after((context2, ups))
+    ups = jnp.stack(ups)
     all_ups = (ups, other(ups, "core", 1))
     context2 = after(context2, whole_units)
     mixed2 = exchange(context2)
@@ -1101,7 +1126,7 @@
     out_parts = [other(out, "dp", m + 1) for m, out in enumerate(leaving)]
     d_query2, d_memory, d_memory_t = attend_back(
         cross_scalars, query2, key2, value2, d_context2.reshape(part_shape), kept2, lse2,
-        cross_first, cross_last, False,
+        cross_first, cross_last,
     )
     d_mixed2 = exchange(after(d_query2, out_parts))
     layer_rows = low(later + outs[0] + sum(wide(part) for part in out_parts) + wide(shrink_bias))
@@ -1132,23 +1157,17 @@
         unit_grads.reshape(2 * block_units, model_width),
         turned_grad(after(d_memory_t, d_context1), all_states),
     )
-    d_query1, d_query1_t, d_memory1, d_memory1_t = attend_back(
+    d_mine, d_theirs, d_query1, d_query1_t, d_memory1, d_memory1_t = attend_back(
         self_scalars, query1.reshape(part_shape), key1, value1, d_context1.reshape(part_shape), kept1, lse1,
-        self_first, self_last, True,
-    )
-    d_query1, d_query1_t, d_memory1, d_memory1_t, unit_grads = after(
-        (d_query1, d_query1_t, d_memory1, d_memory1_t, unit_grads)
+        self_first, self_last, attend_w,
+    )
+    d_mine, d_theirs, d_query1_t, d_memory1_t, unit_grads = after(
+        (d_mine, d_theirs, d_query1_t, d_memory1_t, unit_grads)
     )
     cross_sum = unit_grads[:, 2 * block_units :]
     unit_grads = unit_grads[:, : 2 * block_units].reshape(unit_count, 2, block_rows)
-    d_ones = [
-        (
-            product(d_query1[j].reshape(-1, width), attend_w[:width])
-            + product(d_memory1[j].reshape(-1, 2 * width), attend_w[width:])
-        ).reshape(pieces, row_count, model_width)
-        for j in range(cores)
-    ]
-    d_sum = d_ones[0] + wide(other(low(d_ones[1]), "core", 1))
+    d_theirs = other(d_theirs, "core", 1)
+    d_sum = [d_mine[m] + wide(d_theirs[m]) for m in range(pieces)]
     leaving = [low(d_sum[m]) for m in range(1, pieces)]
     parts1 = [d_sum[0]] + [other(part, "dp", m + 1) for m, part in enumerate(leaving)]
 

time: 661 us -> 648 us (0.980)
  waiting for transfers between devices: 187 us -> 170 us
  blocking collectives: 18.2 us -> 32 us
  local copies, waits for them, and re-layouts: 66.5 us -> 58.3 us
  other arithmetic: 50.4 us -> 57.2 us
    ppermute x54, waiting for transfers between devices: 121 us -> 106 us  [other(): return lax.ppermute(values, axis, [(i, i ^ shift) for i in range(count)])]
    all_to_all x0 -> x1, blocking collectives: none -> 13.7 us  [trade(): lax.all_to_all(values, axis, split_axis=split, concat_axis=concat, tiled=...]
    dot_general x12 -> x8, matrix products: 16 us -> 9.83 us  [product(): return jnp.dot(former, latter, preferred_element_type=jnp.float32)]
    convert_element_type x7 -> x8, other arithmetic: 13.6 us -> 17.6 us  [low(): return values.astype(jnp.bfloat16)]
    all_to_all x18 -> x17, waiting for transfers between devices: 66.4 us -> 62.8 us  [trade(): lax.all_to_all(values, axis, split_axis=split, concat_axis=concat, tiled=...]
    unnamed x193 -> x169, local copies, waits for them, and re-layouts: 20.6 us -> 18.8 us
    all_to_all x18 -> x17, starting transfers between devices: 75.9 us -> 76.4 us  [trade(): lax.all_to_all(values, axis, split_axis=split, concat_axis=concat, tiled=...]
  transfers between devices with their start and end apart: 78 -> 77, of which waited for: 29 -> 26; matrix products, arithmetic and copies ran while one was open for 15% -> 16% of each run, Pallas kernels for 22% -> 22%
where the time goes in v4:
time: 648 us; the launch traced here: 638 us
  waiting for transfers between devices  170 us (26%)
  starting transfers between devices  150 us (23%)
  Pallas kernels  145 us (22%)
  local copies, waits for them, and re-layouts  58.3 us (9%)
  other arithmetic  57.2 us (9%)
  blocking collectives  32 us (5%)
  between operations  15.9 us (2%)
  matrix products  9.83 us (2%)
    ppermute x54, waiting for transfers between devices, other(): return lax.ppermute(values, axis, [(i, i ^ shift) for i in range(count)])  106 us
    all_to_all x17, starting transfers between devices, trade(): lax.all_to_all(values, axis, split_axis=split, concat_axis=concat, tiled=...  76.4 us
    all_to_all x17, waiting for transfers between devices, trade(): lax.all_to_all(values, axis, split_axis=split, concat_axis=concat, tiled=...  62.8 us
    ppermute x54, starting transfers between devices, other(): return lax.ppermute(values, axis, [(i, i ^ shift) for i in range(count)])  61.9 us
    pallas_call x6, Pallas kernels, single(): pl.pallas_call(kernel, grid_spec=pltpu.PrefetchScalarGridSpec(num_scalar_...  35.6 us
    pallas_call x2, Pallas kernels, attend_back(): pl.pallas_call(functools.partial(backward_kernel, heads=width // head_wid...  32 us
    pallas_call x2, Pallas kernels, units_group(): pl.pallas_call(functools.partial(units_kernel, half_count=count), grid_sp...  29.6 us
    unnamed x169, local copies, waits for them, and re-layouts  18.8 us
  transfers between devices with their start and end apart: 77, of which 26 were waited for; matrix products, arithmetic and copies ran while one was open for 16% of the time, Pallas kernels for 22%

profile of v4, /device:TPU:8, one launch (start us, length us, event | category | flops | bytes accessed | tf_op | source)
XLA Modules:
  0.0 638.2 jit_solution(10954648944168067361)
XLA Ops:
  17.6 18.2 %all_gather.9 = bf16[1536,256]{0,1:T(8,128)(2,1)S(1)} all-gather(bf16[384,256]{0,1:T(8,128)(2,1)S(1)} %bitcast.309), channel_id=1, replica_groups=mesh['dp'=4,'z'=4,'core'=2] {'z'}, dimensions={0}, use_global_device_ids=true | all-gather | bytes 983040 | tf_op jit(solution)/shard_map/all_gather | solution.py:965
  49.0 12.2 %all-to-all-done.1 = bf16[4,64,1024]{2,1,0:T(8,128)(2,1)S(1)} async-done(((bf16[4,64,1024]{2,1,0:T(8,128)(2,1)}), bf16[4,64,1024]{2,1,0:T(8,128)(2,1)S(1)}, u32[]{:S(2)}, u32[]{:S(2)}) %all-to-all-start.1) | async-done | bytes 524320 | tf_op jit(solution)/shard_map/all_to_all | solution.py:859
  81.7 10.8 %all-to-all-done.2 = bf16[4,384,256]{2,1,0:T(8,128)(2,1)S(1)} async-done(((bf16[4,384,256]{2,1,0:T(8,128)(2,1)}), bf16[4,384,256]{2,1,0:T(8,128)(2,1)S(1)}, u32[]{:S(2)}, u32[]{:S(2)}) %all-to-all-start.2) | async-done | bytes 786464 | tf_op jit(solution)/shard_map/all_to_all | solution.py:859
  113.9 7.9 %all-to-all-start.4 = ((bf16[4,64,1024]{2,1,0:T(8,128)(2,1)}), bf16[4,64,1024]{2,1,0:T(8,128)(2,1)}, u32[]{:S(2)}, u32[]{:S(2)}) async-start(bf16[4,64,1024]{2,1,0:T(8,128)(2,1)} %all-to-all-done.3), calls=%async_computation.4 | async-start | bytes 1048576 | tf_op jit(solution)/shard_map/all_to_all | solution.py:859
  129.0 16.9 %shard_map.297 = (bf16[2,4,256,128]{3,2,1,0:T(8,128)(2,1)}, bf16[2,4,256,128]{3,2,1,0:T(8,128)(2,1)}, bf16[2,4,256,128]{3,2,1,0:T(8,128)(2,1)}, bf16[2,4,4,64,12...) custom-call(s32[18]{0:T(128)} %pad_add_fusion.1.scalars, bf16[4,256,1024]{2,1,0:T(8,128)(2,1)} %copy-done.13, ...), custom_call_target="tpu_custom_call" | custom-call | flops 17600000000 | bytes 1048576 | tf_op jit(solution)/shard_map/pallas_call | solution.py:348
  146.3 16.4 %collective-permute-done.13 = bf16[4,3,128,256]{3,2,1,0:T(8,128)(2,1)} collective-permute-done((bf16[4,3,128,256]{3,2,1,0:T(8,128)(2,1)}, bf16[4,3,128,256]{3,2,1,0:T(8,128)(2,1)}, u32[]{:S(2)}, u32[]{:S(2)}) %collective-permute-start.13) | collective-permute-done | bytes 786464 | tf_op jit(solution)/shard_map/ppermute | solution.py:855
  209.7 13.6 %shard_map.299 = (bf16[2,4,128,128]{3,2,1,0:T(8,128)(2,1)}, bf16[2,4,128,128]{3,2,1,0:T(8,128)(2,1)}, bf16[2,4,4,64,128]{4,3,2,1,0:T(8,128)(2,1)}, f32[8,128,256]{2,1,0:T(8,128)}, f32[8,1,512]{2,1,0:T(1,128)}) custom-call(s32[18]{0:T(128)} %pad_add_fusion.4.scalars, bf16[2,4,4,64,128]{4,3,2,1,0:T(8,128)(2,1)} %bitcast.292, bf16[4,128,1024]{2,1,0:T(8,128)(2,1)} %copy-done.20, ...), custom_call_target="tpu_custom_call" | custom-call | flops 12099999744 | bytes 1048576 | tf_op jit(solution)/shard_map/pallas_call | solution.py:384
  223.3 9.0 %collective-permute-done.18 = bf16[256,1024]{1,0:T(8,128)(2,1)S(1)} collective-permute-done((bf16[256,1024]{1,0:T(8,128)(2,1)}, bf16[256,1024]{1,0:T(8,128)(2,1)S(1)}, u32[]{:S(2)}, u32[]{:S(2)}) %collective-permute-start.18) | collective-permute-done | bytes 524320 | tf_op jit(solution)/shard_map/ppermute | solution.py:855
  236.5 8.5 %all-to-all-done.8 = bf16[8,256,128]{2,1,0:T(8,128)(2,1)S(1)} async-done(((bf16[8,256,128]{2,1,0:T(8,128)(2,1)}), bf16[8,256,128]{2,1,0:T(8,128)(2,1)S(1)}, u32[]{:S(2)}, u32[]{:S(2)}) %all-to-all-start.8) | async-done | bytes 524320 | tf_op jit(solution)/shard_map/all_to_all | solution.py:859
  254.1 10.8 %collective-permute-done.20 = bf16[256,1024]{1,0:T(8,128)(2,1)S(1)} collective-permute-done((bf16[256,1024]{1,0:T(8,128)(2,1)}, bf16[256,1024]{1,0:T(8,128)(2,1)S(1)}, u32[]{:S(2)}, u32[]{:S(2)}) %collective-permute-start.20) | collective-permute-done | bytes 524320 | tf_op jit(solution)/shard_map/ppermute | solution.py:855
  270.5 21.6 %shard_map.301 = (bf16[2,3,256,1024]{3,2,1,0:T(8,128)(2,1)S(1)}, bf16[2,3,256,1024]{3,2,1,0:T(8,128)(2,1)S(1)}, f32[3,256,1024]{2,1,0:T(8,128)}, bf16[3,256,1024...) custom-call(s32[2]{0:T(128)S(1)} %copy-done.10, ...), custom_call_target="tpu_custom_call" | custom-call | flops 21450000384 | bytes 1048576 | tf_op jit(solution)/shard_map/pallas_call | solution.py:703
  296.9 8.0 %shard_map.302 = (bf16[2,1,256,1024]{3,2,1,0:T(8,128)(2,1)S(1)}, bf16[2,1,256,1024]{3,2,1,0:T(8,128)(2,1)S(1)}, f32[1,256,1024]{2,1,0:T(8,128)S(1)}, bf16[1,256,...) custom-call(s32[2]{0:T(128)S(1)} %copy-done.10, ...), custom_call_target="tpu_custom_call" | custom-call | flops 7150000128 | bytes 1048576 | tf_op jit(solution)/shard_map/pallas_call | solution.py:703
  312.5 17.7 %shard_map.303 = bf16[1024,2048]{1,0:T(8,128)(2,1)} custom-call(s32[2]{0:T(128)} %pad_add_fusion.3.scalars, bf16[2,3,256,1024]{3,2,1,0:T(8,128)(2,1)} %copy-done, bf16[2,1,256,1024]{3,2,1,0:T(8,128)(2,1)} %copy-done.3, bf16[2,3,256,1024]{3,2,1,0:T(8,128)(2,1)} %copy-done.11, bf16[2,1,256,1024]{3,2,1,0:T(8,128)(2,1)} %copy-done.12, ...), custom_call_target="tpu_custom_call" | custom-call | flops 13200000000 | bytes 1048576 | tf_op jit(solution)/shard_map/pallas_call | solution.py:806
  354.4 12.4 %shard_map.305 = (bf16[2,4,4,64,128]{4,3,2,1,0:T(8,128)(2,1)}, bf16[2,4,128,256]{3,2,1,0:T(8,128)(2,1)}, bf16[256,1024]{1,0:T(8,128)(2,1)}) custom-call(s32[18]{0:T(128)} %pad_add_fusion.4.scalars, bf16[2,4,4,64,128]{4,3,2,1,0:T(8,128)(2,1)} %bitcast.293, bf16[2,4,128,128]{3,2,1,0:T(8,128)(2,1)} %get-tuple-element.154.k_ref, ...), custom_call_target="tpu_custom_call" | custom-call | flops 13200000000 | bytes 1048576 | tf_op jit(solution)/shard_map/pallas_call | solution.py:429
  366.8 10.9 %collective-permute-done.34 = bf16[256,1024]{1,0:T(8,128)(2,1)S(1)} collective-permute-done((bf16[256,1024]{1,0:T(8,128)(2,1)S(1)}, bf16[256,1024]{1,0:T(8,128)(2,1)S(1)}, u32[]{:S(2)}, u32[]{:S(2)}) %collective-permute-start.34) | collective-permute-done | bytes 524320 | tf_op jit(solution)/shard_map/ppermute | solution.py:855
  377.7 13.7 %all_to_all.158 = bf16[8,256,128]{2,1,0:T(8,128)(2,1)} all-to-all(bf16[8,256,128]{2,1,0:T(8,128)(2,1)} %bitcast.300), channel_id=1, replica_groups=mesh['dp'=4,'z'=4,'core'=2] {'core','dp'}, dimensions={0} | all-to-all | bytes 1048576 | tf_op jit(solution)/shard_map/all_to_all | solution.py:859
  391.5 6.9 %shard_map.306 = (f32[256,1024]{1,0:T(8,128)}, bf16[256,1024]{1,0:T(8,128)(2,1)}, bf16[2,4,256,128]{3,2,1,0:T(8,128)(2,1)}, f32[3,1024]{1,0:T(4,128)}) custom-call(s32[2]{0:T(128)} %pad_add_fusion.3.scalars, bf16[2,4,256,128]{3,2,1,0:T(8,128)(2,1)} %bitcast.267, bf16[4,4,3,128,256]{4,3,2,1,0:T(8,128)(2,1)} %pad_maximum_fusion.omine_ref.qmine_ref.refs_7_.mine_ref, ...), custom_call_target="tpu_custom_call" | custom-call | flops 4400000000 | bytes 1048576 | tf_op jit(solution)/shard_map/pallas_call | solution.py:475
  402.1 9.1 %all-to-all-done.11 = bf16[8,256,128]{2,1,0:T(8,128)(2,1)S(1)} async-done(((bf16[8,256,128]{2,1,0:T(8,128)(2,1)}), bf16[8,256,128]{2,1,0:T(8,128)(2,1)S(1)}, u32[]{:S(2)}, u32[]{:S(2)}) %all-to-all-start.11) | async-done | bytes 524320 | tf_op jit(solution)/shard_map/all_to_all | solution.py:859
  421.9 19.6 %shard_map.307 = (f32[4,256,1024]{2,1,0:T(8,128)}, bf16[4,256,1024]{2,1,0:T(8,128)(2,1)}, bf16[2,4,4,64,128]{4,3,2,1,0:T(8,128)(2,1)}, bf16[128,2048]{1,0:T(8,12...) custom-call(s32[18]{0:T(128)} %pad_add_fusion.1.scalars, bf16[2,4,4,64,128]{4,3,2,1,0:T(8,128)(2,1)} %bitcast.342, ...), custom_call_target="tpu_custom_call" | custom-call | flops 13200000000 | bytes 1048576 | tf_op jit(solution)/shard_map/pallas_call | solution.py:429
  462.6 6.9 %all-to-all-start.13 = ((bf16[4,64,1024]{2,1,0:T(8,128)(2,1)}), bf16[4,64,1024]{2,1,0:T(8,128)(2,1)}, u32[]{:S(2)}, u32[]{:S(2)}) async-start(bf16[4,64,1024]{2,1,0:T(8,128)(2,1)} %bitcast.87), calls=%async_computation.14 | async-start | bytes 1048576 | tf_op jit(solution)/shard_map/all_to_all | solution.py:859
  472.7 7.2 %shard_map.308 = (bf16[4,4,3,128,256]{4,3,2,1,0:T(8,128)(2,1)}, bf16[4,4,3,128,256]{4,3,2,1,0:T(8,128)(2,1)}) custom-call(s32[2]{0:T(128)} %pad_add_fusion.3.scalars, bf16[2,4,256,128]{3,2,1,0:T(8,128)(2,1)} %bitcast.289, bf16[256,1024]{1,0:T(8,128)(2,1)} %get-tuple-element.221.refs_1_, bf16[2,4,256,128]{3,2,1,0:T(8,128)(2,1)} %bitcast.268, ...), custom_call_target="tpu_custom_call" | custom-call | flops 4400000000 | bytes 1048576 | tf_op jit(solution)/shard_map/pallas_call | solution.py:475
  560.3 7.9 %collective-permute-done.53 = bf16[4,3,128,256]{3,2,1,0:T(8,128)(2,1)} collective-permute-done((bf16[4,3,128,256]{3,2,1,0:T(8,128)(2,1)}, bf16[4,3,128,256]{3,2,1,0:T(8,128)(2,1)}, u32[]{:S(2)}, u32[]{:S(2)}) %collective-permute-start.53) | collective-permute-done | bytes 786464 | tf_op jit(solution)/shard_map/ppermute | solution.py:855
  594.8 20.9 %collective-permute-done.55 = bf16[1024,256]{1,0:T(8,128)(2,1)} collective-permute-done((bf16[1024,256]{1,0:T(8,128)(2,1)}, bf16[1024,256]{1,0:T(8,128)(2,1)}, u32[]{:S(2)}, u32[]{:S(2)}) %collective-permute-start.55) | collective-permute-done | bytes 524320 | tf_op jit(solution)/shard_map/ppermute | solution.py:855
  615.7 8.3 %collective-permute-done.56 = bf16[1024,256]{1,0:T(8,128)(2,1)} collective-permute-done((bf16[1024,256]{1,0:T(8,128)(2,1)}, bf16[1024,256]{1,0:T(8,128)(2,1)}, u32[]{:S(2)}, u32[]{:S(2)}) %collective-permute-start.56) | collective-permute-done | bytes 524320 | tf_op jit(solution)/shard_map/ppermute | solution.py:855
  (456 shorter events, 326.9 us)
Async XLA Ops:
  9.8 33.9 %collective-permute-start.1 = (bf16[256,2,256]{2,0,1:T(8,128)(2,1)S(1)}, bf16[256,2,256]{2,0,1:T(8,128)(2,1)}, u32[]{:S(2)}, u32[]{:S(2)}) collective-permute-start(bf16[256,2,256]{2,0,1:T(8,128)(2,1)S(1)} %get-tuple-element.347), channel_id=1, source_target_pairs={{0,8},{8,0},{16,24},{24,16},{1,9},{9,1},{17,25},{25,17},{2,10},{10... | collective-permute-start | bytes 786440 | tf_op jit(solution)/shard_map/ppermute | solution.py:855
  11.4 33.7 %collective-permute-start.2 = (bf16[256,2,256]{2,0,1:T(8,128)(2,1)S(1)}, bf16[256,2,256]{2,0,1:T(8,128)(2,1)}, u32[]{:S(2)}, u32[]{:S(2)}) collective-permute-start(bf16[256,2,256]{2,0,1:T(8,128)(2,1)S(1)} %get-tuple-element.348), channel_id=1, source_target_pairs={{0,16},{8,24},{16,0},{24,8},{1,17},{9,25},{17,1},{25,9},{2,18},{10... | collective-permute-start | bytes 786440 | tf_op jit(solution)/shard_map/ppermute | solution.py:855
  12.9 33.5 %collective-permute-start.3 = (bf16[256,2,256]{2,0,1:T(8,128)(2,1)S(1)}, bf16[256,2,256]{2,0,1:T(8,128)(2,1)}, u32[]{:S(2)}, u32[]{:S(2)}) collective-permute-start(bf16[256,2,256]{2,0,1:T(8,128)(2,1)S(1)} %get-tuple-element.345), channel_id=1, source_target_pairs={{0,24},{8,16},{16,8},{24,0},{1,25},{9,17},{17,9},{25,1},{2,26},{10... | collective-permute-start | bytes 786440 | tf_op jit(solution)/shard_map/ppermute | solution.py:855
  17.5 76.7 %all-gather.3.cloned.1.call-start = ((), (), s32[]{:S(2)}) async-start(), calls=%async_computation.19 | async-start | bytes 1638400 | tf_op jit(solution)/shard_map/all_gather | solution.py:973
  71.7 25.2 %collective-permute-start.7 = (bf16[128,1024]{1,0:T(8,128)(2,1)}, bf16[128,1024]{1,0:T(8,128)(2,1)}, u32[]{:S(2)}, u32[]{:S(2)}) collective-permute-start(bf16[128,1024]{1,0:T(8,128)(2,1)} %bitcast.19), channel_id=1, source_target_pairs={{0,0},{1,1},{2,8},{3,9},{4,16},{5,17},{6,24},{7,25},{8,2},{9,3},{1... | collective-permute-start | bytes 786440 | tf_op jit(solution)/shard_map/ppermute | solution.py:894
  96.9 32.0 %collective-permute-start.8 = (bf16[4,256,1024]{2,1,0:T(8,128)(2,1)S(1)}, bf16[4,256,1024]{2,1,0:T(8,128)(2,1)}, u32[]{:S(2)}, u32[]{:S(2)}) collective-permute-start(bf16[4,256,1024]{2,1,0:T(8,128)(2,1)S(1)} %pad_maximum_fusion.1.mine_ref), channel_id=1, source_target_pairs={{0,1},{1,0},{2,3},{3,2},{4,5},{5,4},{6,7},{7,6},{8,9},{9,8},{10,11... | collective-permute-start | bytes 6291464 | tf_op jit(solution)/shard_map/ppermute | solution.py:855
  113.9 32.0 %all-to-all-start.4 = ((bf16[4,64,1024]{2,1,0:T(8,128)(2,1)}), bf16[4,64,1024]{2,1,0:T(8,128)(2,1)}, u32[]{:S(2)}, u32[]{:S(2)}) async-start(bf16[4,64,1024]{2,1,0:T(8,128)(2,1)} %all-to-all-done.3), calls=%async_computation.4 | async-start | bytes 1048576 | tf_op jit(solution)/shard_map/all_to_all | solution.py:859
  121.8 110.5 %all-gather.5.cloned.1.call-start = ((), (), s32[]{:S(2)}) async-start(), calls=%async_computation.20 | async-start | bytes 5242880 | tf_op jit(solution)/shard_map/all_gather | solution.py:986
  126.9 35.8 %collective-permute-start.13 = (bf16[4,3,128,256]{3,2,1,0:T(8,128)(2,1)}, bf16[4,3,128,256]{3,2,1,0:T(8,128)(2,1)}, u32[]{:S(2)}, u32[]{:S(2)}) collective-permute-start(bf16[4,3,128,256]{3,2,1,0:T(8,128)(2,1)} %bitcast.260), channel_id=1, source_target_pairs={{0,16},{8,24},{16,0},{24,8},{1,17},{9,25},{17,1},{25,9},{2,18},{10... | collective-permute-start | bytes 2359304 | tf_op jit(solution)/shard_map/ppermute | solution.py:855
  127.0 35.7 %collective-permute-start.14 = (bf16[4,3,128,256]{3,2,1,0:T(8,128)(2,1)}, bf16[4,3,128,256]{3,2,1,0:T(8,128)(2,1)}, u32[]{:S(2)}, u32[]{:S(2)}) collective-permute-start(bf16[4,3,128,256]{3,2,1,0:T(8,128)(2,1)} %bitcast.261), channel_id=1, source_target_pairs={{0,24},{8,16},{16,8},{24,0},{1,25},{9,17},{17,9},{25,1},{2,26},{10... | collective-permute-start | bytes 2359304 | tf_op jit(solution)/shard_map/ppermute | solution.py:855
  179.1 30.6 %collective-permute-start.16 = (bf16[4,128,1024]{2,1,0:T(8,128)(2,1)S(1)}, bf16[4,128,1024]{2,1,0:T(8,128)(2,1)}, u32[]{:S(2)}, u32[]{:S(2)}) collective-permute-start(bf16[4,128,1024]{2,1,0:T(8,128)(2,1)S(1)} %pad_maximum_fusion.5.mine_ref), channel_id=1, source_target_pairs={{0,1},{1,0},{2,3},{3,2},{4,5},{5,4},{6,7},{7,6},{8,9},{9,8},{10,11... | collective-permute-start | bytes 3145736 | tf_op jit(solution)/shard_map/ppermute | solution.py:855
  235.8 176.7 %reduce-scatter.2.cloned.1.call-start = ((), (), s32[]{:S(2)}) async-start(), calls=%async_computation.21 | async-start | bytes 5242880 | tf_op jit(solution)/shard_map/reduce_scatter | solution.py:1110
  269.4 25.6 %collective-permute-start.24 = (bf16[256,1024]{1,0:T(8,128)(2,1)S(1)}, bf16[256,1024]{1,0:T(8,128)(2,1)S(1)}, u32[]{:S(2)}, u32[]{:S(2)}) collective-permute-start(bf16[256,1024]{1,0:T(8,128)(2,1)S(1)} %copy-done.39), channel_id=1, source_target_pairs={{0,24},{8,16},{16,8},{24,0},{1,25},{9,17},{17,9},{25,1},{2,26},{10... | collective-permute-start | bytes 1572872 | tf_op jit(solution)/shard_map/ppermute | solution.py:855
  458.6 26.0 %collective-permute-start.37 = (bf16[256,1024]{1,0:T(8,128)(2,1)}, bf16[256,1024]{1,0:T(8,128)(2,1)}, u32[]{:S(2)}, u32[]{:S(2)}) collective-permute-start(bf16[256,1024]{1,0:T(8,128)(2,1)} %get-tuple-element.326), channel_id=1, source_target_pairs={{0,8},{8,0},{16,24},{24,16},{1,9},{9,1},{17,25},{25,17},{2,10},{10... | collective-permute-start | bytes 1572872 | tf_op jit(solution)/shard_map/ppermute | solution.py:855
  460.6 25.6 %collective-permute-start.38 = (bf16[256,1024]{1,0:T(8,128)(2,1)}, bf16[256,1024]{1,0:T(8,128)(2,1)}, u32[]{:S(2)}, u32[]{:S(2)}) collective-permute-start(bf16[256,1024]{1,0:T(8,128)(2,1)} %get-tuple-element.325), channel_id=1, source_target_pairs={{0,16},{8,24},{16,0},{24,8},{1,17},{9,25},{17,1},{25,9},{2,18},{10... | collective-permute-start | bytes 1572872 | tf_op jit(solution)/shard_map/ppermute | solution.py:855
  486.2 37.6 %collective-permute-start.50 = (bf16[4,4,3,128,256]{4,3,2,1,0:T(8,128)(2,1)}, bf16[4,4,3,128,256]{4,3,2,1,0:T(8,128)(2,1)}, u32[]{:S(2)}, u32[]{:S(2)}) collective-permute-start(bf16[4,4,3,128,256]{4,3,2,1,0:T(8,128)(2,1)} %get-tuple-element.243), channel_id=1, source_target_pairs={{0,1},{1,0},{2,3},{3,2},{4,5},{5,4},{6,7},{7,6},{8,9},{9,8},{10,11... | collective-permute-start | bytes 9437192 | tf_op jit(solution)/shard_map/ppermute | solution.py:855
  517.9 31.6 %all-to-all-start.15 = ((bf16[4,64,1024]{2,1,0:T(8,128)(2,1)}), bf16[4,64,1024]{2,1,0:T(8,128)(2,1)}, u32[]{:S(2)}, u32[]{:S(2)}) async-start(bf16[4,64,1024]{2,1,0:T(8,128)(2,1)} %bitcast.94), calls=%async_computation.16 | async-start | bytes 1048576 | tf_op jit(solution)/shard_map/all_to_all | solution.py:859
  528.2 32.1 %collective-permute-start.51 = (bf16[4,3,128,256]{3,2,1,0:T(8,128)(2,1)}, bf16[4,3,128,256]{3,2,1,0:T(8,128)(2,1)}, u32[]{:S(2)}, u32[]{:S(2)}) collective-permute-start(bf16[4,3,128,256]{3,2,1,0:T(8,128)(2,1)} %get-tuple-element.244), channel_id=1, source_target_pairs={{0,8},{8,0},{16,24},{24,16},{1,9},{9,1},{17,25},{25,17},{2,10},{10... | collective-permute-start | bytes 2359304 | tf_op jit(solution)/shard_map/ppermute | solution.py:855
  528.8 31.5 %collective-permute-start.52 = (bf16[4,3,128,256]{3,2,1,0:T(8,128)(2,1)}, bf16[4,3,128,256]{3,2,1,0:T(8,128)(2,1)}, u32[]{:S(2)}, u32[]{:S(2)}) collective-permute-start(bf16[4,3,128,256]{3,2,1,0:T(8,128)(2,1)} %get-tuple-element.245), channel_id=1, source_target_pairs={{0,16},{8,24},{16,0},{24,8},{1,17},{9,25},{17,1},{25,9},{2,18},{10... | collective-permute-start | bytes 2359304 | tf_op jit(solution)/shard_map/ppermute | solution.py:855
  529.3 38.8 %collective-permute-start.53 = (bf16[4,3,128,256]{3,2,1,0:T(8,128)(2,1)}, bf16[4,3,128,256]{3,2,1,0:T(8,128)(2,1)}, u32[]{:S(2)}, u32[]{:S(2)}) collective-permute-start(bf16[4,3,128,256]{3,2,1,0:T(8,128)(2,1)} %get-tuple-element.246), channel_id=1, source_target_pairs={{0,24},{8,16},{16,8},{24,0},{1,25},{9,17},{17,9},{25,1},{2,26},{10... | collective-permute-start | bytes 2359304 | tf_op jit(solution)/shard_map/ppermute | solution.py:855
  546.1 44.7 %collective-permute-start.44 = (bf16[128,1024]{1,0:T(8,128)(2,1)}, bf16[128,1024]{1,0:T(8,128)(2,1)S(1)}, u32[]{:S(2)}, u32[]{:S(2)}) collective-permute-start(bf16[128,1024]{1,0:T(8,128)(2,1)} %fusion.20), channel_id=1, source_target_pairs={{0,0},{1,1},{2,8},{3,9},{4,16},{5,17},{6,24},{7,25},{8,2},{9,3},{1... | collective-permute-start | bytes 786440 | tf_op jit(solution)/shard_map/ppermute | solution.py:894
  549.5 35.2 %all-to-all-start.16 = ((bf16[4,64,1024]{2,1,0:T(8,128)(2,1)}), bf16[4,64,1024]{2,1,0:T(8,128)(2,1)S(1)}, u32[]{:S(2)}, u32[]{:S(2)}) async-start(bf16[4,64,1024]{2,1,0:T(8,128)(2,1)} %all-to-all-done.15), calls=%async_computation.17 | async-start | bytes 1048576 | tf_op jit(solution)/shard_map/all_to_all | solution.py:859
  578.7 37.0 %collective-permute-start.55 = (bf16[1024,256]{1,0:T(8,128)(2,1)}, bf16[1024,256]{1,0:T(8,128)(2,1)}, u32[]{:S(2)}, u32[]{:S(2)}) collective-permute-start(bf16[1024,256]{1,0:T(8,128)(2,1)} %get-tuple-element.334), channel_id=1, source_target_pairs={{0,4},{2,6},{4,0},{6,2},{1,5},{3,7},{5,1},{7,3},{8,12},{10,14},{12... | collective-permute-start | bytes 1572872 | tf_op jit(solution)/shard_map/ppermute | solution.py:855
  583.6 40.4 %collective-permute-start.56 = (bf16[1024,256]{1,0:T(8,128)(2,1)}, bf16[1024,256]{1,0:T(8,128)(2,1)}, u32[]{:S(2)}, u32[]{:S(2)}) collective-permute-start(bf16[1024,256]{1,0:T(8,128)(2,1)} %get-tuple-element.333), channel_id=1, source_target_pairs={{0,6},{2,4},{4,2},{6,0},{1,7},{3,5},{5,3},{7,1},{8,14},{10,12},{12... | collective-permute-start | bytes 1572872 | tf_op jit(solution)/shard_map/ppermute | solution.py:855
  (125 other events, 2098.2 us)
Sparse Core Ops, SparseCore 0:
  37.0 40.2 all-gather.2
  125.5 78.0 all-gather.4
  333.8 78.5 reduce-scatter.1

commit v5 on v4

--- a/solution.py
+++ b/solution.py
@@ -1197,14 +1197,14 @@
         (parts1, layer_first, d_states, square_mine, square_theirs, attend_sum)
     )
     attend_sum = to_chips(*attend_sum)
-    state_parts = [other(low(d_states[m]), "dp", m) for m in range(1, pieces)]
+    square_theirs = other(square_theirs, "core", 1)
+    square_sums = [wide(square_mine[m]) + wide(square_theirs[m]) for m in range(pieces)]
+    square_parts = [other(low(square_sums[m]), "dp", m) for m in range(1, pieces)]
+    state_parts = [
+        other(after(low(d_states[m]), square_parts), "dp", m) for m in range(1, pieces)
+    ]
     encoder_rows = low(d_states[0] + sum(wide(part) for part in state_parts))
     encoder_gradient = swap_planes(encoder_rows)[None]
-    square_theirs = other(square_theirs, "core", 1)
-    square_sums = [wide(square_mine[m]) + wide(square_theirs[m]) for m in range(pieces)]
-    square_parts = [
-        other(after(low(square_sums[m]), state_parts), "dp", m) for m in range(1, pieces)
-    ]
     square_sum = square_sums[0] + sum(wide(part) for part in square_parts)
     input_gradient, sums1 = single(
         input_back_kernel,

time: 648 us -> 667 us (1.029)
  waiting for transfers between devices: 170 us -> 188 us
  starting transfers between devices: 150 us -> 138 us
  Pallas kernels: 145 us -> 155 us
    all_to_all x17, waiting for transfers between devices: 62.8 us -> 88.3 us  [trade(): lax.all_to_all(values, axis, split_axis=split, concat_axis=concat, tiled=...]
    ppermute x54, starting transfers between devices: 61.9 us -> 51.8 us  [other(): return lax.ppermute(values, axis, [(i, i ^ shift) for i in range(count)])]
    ppermute x54, waiting for transfers between devices: 106 us -> 98.7 us  [other(): return lax.ppermute(values, axis, [(i, i ^ shift) for i in range(count)])]
  transfers between devices with their start and end apart: 77 -> 77, of which waited for: 26 -> 27; matrix products, arithmetic and copies ran while one was open for 16% -> 16% of each run, Pallas kernels for 22% -> 23%
where the time goes in v5:
time: 667 us; the launch traced here: 657 us
  waiting for transfers between devices  188 us (28%)
  Pallas kernels  155 us (23%)
  starting transfers between devices  138 us (21%)
  local copies, waits for them, and re-layouts  61 us (9%)
  other arithmetic  56 us (8%)
  blocking collectives  32 us (5%)
  between operations  16 us (2%)
  matrix products  10.7 us (2%)
    ppermute x54, waiting for transfers between devices, other(): return lax.ppermute(values, axis, [(i, i ^ shift) for i in range(count)])  98.7 us
    all_to_all x17, waiting for transfers between devices, trade(): lax.all_to_all(values, axis, split_axis=split, concat_axis=concat, tiled=...  88.3 us
    all_to_all x17, starting transfers between devices, trade(): lax.all_to_all(values, axis, split_axis=split, concat_axis=concat, tiled=...  74.3 us
    ppermute x54, starting transfers between devices, other(): return lax.ppermute(values, axis, [(i, i ^ shift) for i in range(count)])  51.8 us
    pallas_call x2, Pallas kernels, attend_back(): pl.pallas_call(functools.partial(backward_kernel, heads=width // head_wid...  36.9 us
    pallas_call x6, Pallas kernels, single(): pl.pallas_call(kernel, grid_spec=pltpu.PrefetchScalarGridSpec(num_scalar_...  35.3 us
    pallas_call x2, Pallas kernels, units_group(): pl.pallas_call(functools.partial(units_kernel, half_count=count), grid_sp...  29.7 us
    unnamed x169, local copies, waits for them, and re-layouts  20.7 us
  transfers between devices with their start and end apart: 77, of which 27 were waited for; matrix products, arithmetic and copies ran while one was open for 16% of the time, Pallas kernels for 23%

profile of v5, /device:TPU:8, one launch (start us, length us, event | category | flops | bytes accessed | tf_op | source)
XLA Modules:
  0.0 656.8 jit_solution(3812593364220279028)
XLA Ops:
  17.6 18.2 %all_gather.9 = bf16[1536,256]{0,1:T(8,128)(2,1)S(1)} all-gather(bf16[384,256]{0,1:T(8,128)(2,1)S(1)} %bitcast.311), channel_id=1, replica_groups=mesh['dp'=4,'z'=4,'core'=2] {'z'}, dimensions={0}, use_global_device_ids=true | all-gather | bytes 983040 | tf_op jit(solution)/shard_map/all_gather | solution.py:965
  49.0 12.2 %all-to-all-done.1 = bf16[4,64,1024]{2,1,0:T(8,128)(2,1)S(1)} async-done(((bf16[4,64,1024]{2,1,0:T(8,128)(2,1)}), bf16[4,64,1024]{2,1,0:T(8,128)(2,1)S(1)}, u32[]{:S(2)}, u32[]{:S(2)}) %all-to-all-start.1) | async-done | bytes 524320 | tf_op jit(solution)/shard_map/all_to_all | solution.py:859
  81.7 10.8 %all-to-all-done.2 = bf16[4,384,256]{2,1,0:T(8,128)(2,1)S(1)} async-done(((bf16[4,384,256]{2,1,0:T(8,128)(2,1)}), bf16[4,384,256]{2,1,0:T(8,128)(2,1)S(1)}, u32[]{:S(2)}, u32[]{:S(2)}) %all-to-all-start.2) | async-done | bytes 786464 | tf_op jit(solution)/shard_map/all_to_all | solution.py:859
  113.9 7.9 %all-to-all-start.4 = ((bf16[4,64,1024]{2,1,0:T(8,128)(2,1)}), bf16[4,64,1024]{2,1,0:T(8,128)(2,1)}, u32[]{:S(2)}, u32[]{:S(2)}) async-start(bf16[4,64,1024]{2,1,0:T(8,128)(2,1)} %all-to-all-done.3), calls=%async_computation.4 | async-start | bytes 1048576 | tf_op jit(solution)/shard_map/all_to_all | solution.py:859
  129.0 19.2 %shard_map.297 = (bf16[2,4,256,128]{3,2,1,0:T(8,128)(2,1)}, bf16[2,4,256,128]{3,2,1,0:T(8,128)(2,1)}, bf16[2,4,256,128]{3,2,1,0:T(8,128)(2,1)}, bf16[2,4,4,64,12...) custom-call(s32[18]{0:T(128)} %pad_add_fusion.1.scalars, bf16[4,256,1024]{2,1,0:T(8,128)(2,1)} %copy-done.13, ...), custom_call_target="tpu_custom_call" | custom-call | flops 17600000000 | bytes 1048576 | tf_op jit(solution)/shard_map/pallas_call | solution.py:348
  148.2 14.5 %collective-permute-done.13 = bf16[4,3,128,256]{3,2,1,0:T(8,128)(2,1)} collective-permute-done((bf16[4,3,128,256]{3,2,1,0:T(8,128)(2,1)}, bf16[4,3,128,256]{3,2,1,0:T(8,128)(2,1)}, u32[]{:S(2)}, u32[]{:S(2)}) %collective-permute-start.13) | collective-permute-done | bytes 786464 | tf_op jit(solution)/shard_map/ppermute | solution.py:855
  199.8 6.4 all-to-all-done.6
  209.7 16.3 %shard_map.299 = (bf16[2,4,128,128]{3,2,1,0:T(8,128)(2,1)}, bf16[2,4,128,128]{3,2,1,0:T(8,128)(2,1)}, bf16[2,4,4,64,128]{4,3,2,1,0:T(8,128)(2,1)}, f32[8,128,256]{2,1,0:T(8,128)}, f32[8,1,512]{2,1,0:T(1,128)}) custom-call(s32[18]{0:T(128)} %pad_add_fusion.4.scalars, bf16[2,4,4,64,128]{4,3,2,1,0:T(8,128)(2,1)} %bitcast.292, bf16[4,128,1024]{2,1,0:T(8,128)(2,1)} %copy-done.21, ...), custom_call_target="tpu_custom_call" | custom-call | flops 12099999744 | bytes 1048576 | tf_op jit(solution)/shard_map/pallas_call | solution.py:384
  226.0 6.3 collective-permute-done.18
  236.5 8.5 %all-to-all-done.8 = bf16[8,256,128]{2,1,0:T(8,128)(2,1)S(1)} async-done(((bf16[8,256,128]{2,1,0:T(8,128)(2,1)}), bf16[8,256,128]{2,1,0:T(8,128)(2,1)S(1)}, u32[]{:S(2)}, u32[]{:S(2)}) %all-to-all-start.8) | async-done | bytes 524320 | tf_op jit(solution)/shard_map/all_to_all | solution.py:859
  254.1 10.8 %collective-permute-done.20 = bf16[256,1024]{1,0:T(8,128)(2,1)S(1)} collective-permute-done((bf16[256,1024]{1,0:T(8,128)(2,1)}, bf16[256,1024]{1,0:T(8,128)(2,1)S(1)}, u32[]{:S(2)}, u32[]{:S(2)}) %collective-permute-start.20) | collective-permute-done | bytes 524320 | tf_op jit(solution)/shard_map/ppermute | solution.py:855
  270.6 21.6 %shard_map.301 = (bf16[2,3,256,1024]{3,2,1,0:T(8,128)(2,1)S(1)}, bf16[2,3,256,1024]{3,2,1,0:T(8,128)(2,1)S(1)}, f32[3,256,1024]{2,1,0:T(8,128)}, bf16[3,256,1024...) custom-call(s32[2]{0:T(128)S(1)} %copy-done.10, ...), custom_call_target="tpu_custom_call" | custom-call | flops 21450000384 | bytes 1048576 | tf_op jit(solution)/shard_map/pallas_call | solution.py:703
  297.0 8.0 %shard_map.302 = (bf16[2,1,256,1024]{3,2,1,0:T(8,128)(2,1)S(1)}, bf16[2,1,256,1024]{3,2,1,0:T(8,128)(2,1)S(1)}, f32[1,256,1024]{2,1,0:T(8,128)S(1)}, bf16[1,256,...) custom-call(s32[2]{0:T(128)S(1)} %copy-done.10, ...), custom_call_target="tpu_custom_call" | custom-call | flops 7150000128 | bytes 1048576 | tf_op jit(solution)/shard_map/pallas_call | solution.py:703
  312.6 17.7 %shard_map.303 = bf16[1024,2048]{1,0:T(8,128)(2,1)} custom-call(s32[2]{0:T(128)} %pad_add_fusion.3.scalars, bf16[2,3,256,1024]{3,2,1,0:T(8,128)(2,1)} %copy-done, bf16[2,1,256,1024]{3,2,1,0:T(8,128)(2,1)} %copy-done.3, bf16[2,3,256,1024]{3,2,1,0:T(8,128)(2,1)} %copy-done.11, bf16[2,1,256,1024]{3,2,1,0:T(8,128)(2,1)} %copy-done.12, ...), custom_call_target="tpu_custom_call" | custom-call | flops 13200000000 | bytes 1048576 | tf_op jit(solution)/shard_map/pallas_call | solution.py:806
  354.5 15.2 %shard_map.305 = (bf16[2,4,4,64,128]{4,3,2,1,0:T(8,128)(2,1)}, bf16[2,4,128,256]{3,2,1,0:T(8,128)(2,1)}, bf16[256,1024]{1,0:T(8,128)(2,1)}) custom-call(s32[18]{0:T(128)} %pad_add_fusion.4.scalars, bf16[2,4,4,64,128]{4,3,2,1,0:T(8,128)(2,1)} %bitcast.293, bf16[2,4,128,128]{3,2,1,0:T(8,128)(2,1)} %get-tuple-element.154.k_ref, ...), custom_call_target="tpu_custom_call" | custom-call | flops 13200000000 | bytes 1048576 | tf_op jit(solution)/shard_map/pallas_call | solution.py:429
  369.7 8.1 %collective-permute-done.34 = bf16[256,1024]{1,0:T(8,128)(2,1)S(1)} collective-permute-done((bf16[256,1024]{1,0:T(8,128)(2,1)S(1)}, bf16[256,1024]{1,0:T(8,128)(2,1)S(1)}, u32[]{:S(2)}, u32[]{:S(2)}) %collective-permute-start.34) | collective-permute-done | bytes 524320 | tf_op jit(solution)/shard_map/ppermute | solution.py:855
  377.8 13.7 %all_to_all.158 = bf16[8,256,128]{2,1,0:T(8,128)(2,1)} all-to-all(bf16[8,256,128]{2,1,0:T(8,128)(2,1)} %bitcast.300), channel_id=1, replica_groups=mesh['dp'=4,'z'=4,'core'=2] {'core','dp'}, dimensions={0} | all-to-all | bytes 1048576 | tf_op jit(solution)/shard_map/all_to_all | solution.py:859
  391.5 6.9 %shard_map.306 = (f32[256,1024]{1,0:T(8,128)}, bf16[256,1024]{1,0:T(8,128)(2,1)}, bf16[2,4,256,128]{3,2,1,0:T(8,128)(2,1)}, f32[3,1024]{1,0:T(4,128)}) custom-call(s32[2]{0:T(128)} %pad_add_fusion.3.scalars, bf16[2,4,256,128]{3,2,1,0:T(8,128)(2,1)} %bitcast.267, bf16[4,4,3,128,256]{4,3,2,1,0:T(8,128)(2,1)} %pad_maximum_fusion.omine_ref.qmine_ref.refs_7_.mine_ref, ...), custom_call_target="tpu_custom_call" | custom-call | flops 4400000000 | bytes 1048576 | tf_op jit(solution)/shard_map/pallas_call | solution.py:475
  404.5 6.7 %all-to-all-done.11 = bf16[8,256,128]{2,1,0:T(8,128)(2,1)S(1)} async-done(((bf16[8,256,128]{2,1,0:T(8,128)(2,1)}), bf16[8,256,128]{2,1,0:T(8,128)(2,1)S(1)}, u32[]{:S(2)}, u32[]{:S(2)}) %all-to-all-start.11) | async-done | bytes 524320 | tf_op jit(solution)/shard_map/all_to_all | solution.py:859
  422.0 21.7 %shard_map.307 = (f32[4,256,1024]{2,1,0:T(8,128)}, bf16[4,256,1024]{2,1,0:T(8,128)(2,1)}, bf16[2,4,4,64,128]{4,3,2,1,0:T(8,128)(2,1)}, bf16[128,2048]{1,0:T(8,12...) custom-call(s32[18]{0:T(128)} %pad_add_fusion.1.scalars, bf16[2,4,4,64,128]{4,3,2,1,0:T(8,128)(2,1)} %bitcast.344, ...), custom_call_target="tpu_custom_call" | custom-call | flops 13200000000 | bytes 1048576 | tf_op jit(solution)/shard_map/pallas_call | solution.py:429
  470.2 7.0 %shard_map.308 = (bf16[4,4,3,128,256]{4,3,2,1,0:T(8,128)(2,1)}, bf16[4,4,3,128,256]{4,3,2,1,0:T(8,128)(2,1)}) custom-call(s32[2]{0:T(128)} %pad_add_fusion.3.scalars, bf16[2,4,256,128]{3,2,1,0:T(8,128)(2,1)} %bitcast.289, bf16[256,1024]{1,0:T(8,128)(2,1)} %get-tuple-element.221.refs_1_, bf16[2,4,256,128]{3,2,1,0:T(8,128)(2,1)} %bitcast.268, ...), custom_call_target="tpu_custom_call" | custom-call | flops 4400000000 | bytes 1048576 | tf_op jit(solution)/shard_map/pallas_call | solution.py:475
  546.5 30.1 %all-to-all-done.16 = bf16[4,64,1024]{2,1,0:T(8,128)(2,1)S(1)} async-done(((bf16[4,64,1024]{2,1,0:T(8,128)(2,1)}), bf16[4,64,1024]{2,1,0:T(8,128)(2,1)S(1)}, u32[]{:S(2)}, u32[]{:S(2)}) %all-to-all-start.16) | async-done | bytes 524320 | tf_op jit(solution)/shard_map/all_to_all | solution.py:859
  610.0 16.9 %collective-permute-done.55 = bf16[1024,256]{1,0:T(8,128)(2,1)} collective-permute-done((bf16[1024,256]{1,0:T(8,128)(2,1)}, bf16[1024,256]{1,0:T(8,128)(2,1)}, u32[]{:S(2)}, u32[]{:S(2)}) %collective-permute-start.55) | collective-permute-done | bytes 524320 | tf_op jit(solution)/shard_map/ppermute | solution.py:855
  626.8 15.6 %collective-permute-done.56 = bf16[1024,256]{1,0:T(8,128)(2,1)} collective-permute-done((bf16[1024,256]{1,0:T(8,128)(2,1)}, bf16[1024,256]{1,0:T(8,128)(2,1)}, u32[]{:S(2)}, u32[]{:S(2)}) %collective-permute-start.56) | collective-permute-done | bytes 524320 | tf_op jit(solution)/shard_map/ppermute | solution.py:855
  (456 shorter events, 320.5 us)
Async XLA Ops:
  9.8 33.9 %collective-permute-start.1 = (bf16[256,2,256]{2,0,1:T(8,128)(2,1)S(1)}, bf16[256,2,256]{2,0,1:T(8,128)(2,1)}, u32[]{:S(2)}, u32[]{:S(2)}) collective-permute-start(bf16[256,2,256]{2,0,1:T(8,128)(2,1)S(1)} %get-tuple-element.347), channel_id=1, source_target_pairs={{0,8},{8,0},{16,24},{24,16},{1,9},{9,1},{17,25},{25,17},{2,10},{10... | collective-permute-start | bytes 786440 | tf_op jit(solution)/shard_map/ppermute | solution.py:855
  11.4 33.7 %collective-permute-start.2 = (bf16[256,2,256]{2,0,1:T(8,128)(2,1)S(1)}, bf16[256,2,256]{2,0,1:T(8,128)(2,1)}, u32[]{:S(2)}, u32[]{:S(2)}) collective-permute-start(bf16[256,2,256]{2,0,1:T(8,128)(2,1)S(1)} %get-tuple-element.348), channel_id=1, source_target_pairs={{0,16},{8,24},{16,0},{24,8},{1,17},{9,25},{17,1},{25,9},{2,18},{10... | collective-permute-start | bytes 786440 | tf_op jit(solution)/shard_map/ppermute | solution.py:855
  12.9 33.5 %collective-permute-start.3 = (bf16[256,2,256]{2,0,1:T(8,128)(2,1)S(1)}, bf16[256,2,256]{2,0,1:T(8,128)(2,1)}, u32[]{:S(2)}, u32[]{:S(2)}) collective-permute-start(bf16[256,2,256]{2,0,1:T(8,128)(2,1)S(1)} %get-tuple-element.345), channel_id=1, source_target_pairs={{0,24},{8,16},{16,8},{24,0},{1,25},{9,17},{17,9},{25,1},{2,26},{10... | collective-permute-start | bytes 786440 | tf_op jit(solution)/shard_map/ppermute | solution.py:855
  17.5 76.7 %all-gather.3.cloned.1.call-start = ((), (), s32[]{:S(2)}) async-start(), calls=%async_computation.19 | async-start | bytes 1638400 | tf_op jit(solution)/shard_map/all_gather | solution.py:973
  71.7 25.2 %collective-permute-start.7 = (bf16[128,1024]{1,0:T(8,128)(2,1)}, bf16[128,1024]{1,0:T(8,128)(2,1)}, u32[]{:S(2)}, u32[]{:S(2)}) collective-permute-start(bf16[128,1024]{1,0:T(8,128)(2,1)} %bitcast.19), channel_id=1, source_target_pairs={{0,0},{1,1},{2,8},{3,9},{4,16},{5,17},{6,24},{7,25},{8,2},{9,3},{1... | collective-permute-start | bytes 786440 | tf_op jit(solution)/shard_map/ppermute | solution.py:894
  96.9 32.0 %collective-permute-start.8 = (bf16[4,256,1024]{2,1,0:T(8,128)(2,1)S(1)}, bf16[4,256,1024]{2,1,0:T(8,128)(2,1)}, u32[]{:S(2)}, u32[]{:S(2)}) collective-permute-start(bf16[4,256,1024]{2,1,0:T(8,128)(2,1)S(1)} %pad_maximum_fusion.1.mine_ref), channel_id=1, source_target_pairs={{0,1},{1,0},{2,3},{3,2},{4,5},{5,4},{6,7},{7,6},{8,9},{9,8},{10,11... | collective-permute-start | bytes 6291464 | tf_op jit(solution)/shard_map/ppermute | solution.py:855
  113.9 34.3 %all-to-all-start.4 = ((bf16[4,64,1024]{2,1,0:T(8,128)(2,1)}), bf16[4,64,1024]{2,1,0:T(8,128)(2,1)}, u32[]{:S(2)}, u32[]{:S(2)}) async-start(bf16[4,64,1024]{2,1,0:T(8,128)(2,1)} %all-to-all-done.3), calls=%async_computation.4 | async-start | bytes 1048576 | tf_op jit(solution)/shard_map/all_to_all | solution.py:859
  121.8 110.6 %all-gather.5.cloned.1.call-start = ((), (), s32[]{:S(2)}) async-start(), calls=%async_computation.20 | async-start | bytes 5242880 | tf_op jit(solution)/shard_map/all_gather | solution.py:986
  126.9 35.8 %collective-permute-start.13 = (bf16[4,3,128,256]{3,2,1,0:T(8,128)(2,1)}, bf16[4,3,128,256]{3,2,1,0:T(8,128)(2,1)}, u32[]{:S(2)}, u32[]{:S(2)}) collective-permute-start(bf16[4,3,128,256]{3,2,1,0:T(8,128)(2,1)} %bitcast.260), channel_id=1, source_target_pairs={{0,16},{8,24},{16,0},{24,8},{1,17},{9,25},{17,1},{25,9},{2,18},{10... | collective-permute-start | bytes 2359304 | tf_op jit(solution)/shard_map/ppermute | solution.py:855
  127.0 35.7 %collective-permute-start.14 = (bf16[4,3,128,256]{3,2,1,0:T(8,128)(2,1)}, bf16[4,3,128,256]{3,2,1,0:T(8,128)(2,1)}, u32[]{:S(2)}, u32[]{:S(2)}) collective-permute-start(bf16[4,3,128,256]{3,2,1,0:T(8,128)(2,1)} %bitcast.261), channel_id=1, source_target_pairs={{0,24},{8,16},{16,8},{24,0},{1,25},{9,17},{17,9},{25,1},{2,26},{10... | collective-permute-start | bytes 2359304 | tf_op jit(solution)/shard_map/ppermute | solution.py:855
  179.1 30.6 %collective-permute-start.16 = (bf16[4,128,1024]{2,1,0:T(8,128)(2,1)S(1)}, bf16[4,128,1024]{2,1,0:T(8,128)(2,1)}, u32[]{:S(2)}, u32[]{:S(2)}) collective-permute-start(bf16[4,128,1024]{2,1,0:T(8,128)(2,1)S(1)} %pad_maximum_fusion.5.mine_ref), channel_id=1, source_target_pairs={{0,1},{1,0},{2,3},{3,2},{4,5},{5,4},{6,7},{7,6},{8,9},{9,8},{10,11... | collective-permute-start | bytes 3145736 | tf_op jit(solution)/shard_map/ppermute | solution.py:855
  235.9 176.7 %reduce-scatter.2.cloned.1.call-start = ((), (), s32[]{:S(2)}) async-start(), calls=%async_computation.21 | async-start | bytes 5242880 | tf_op jit(solution)/shard_map/reduce_scatter | solution.py:1110
  269.5 25.6 %collective-permute-start.24 = (bf16[256,1024]{1,0:T(8,128)(2,1)S(1)}, bf16[256,1024]{1,0:T(8,128)(2,1)S(1)}, u32[]{:S(2)}, u32[]{:S(2)}) collective-permute-start(bf16[256,1024]{1,0:T(8,128)(2,1)S(1)} %copy-done.40), channel_id=1, source_target_pairs={{0,24},{8,16},{16,8},{24,0},{1,25},{9,17},{17,9},{25,1},{2,26},{10... | collective-permute-start | bytes 1572872 | tf_op jit(solution)/shard_map/ppermute | solution.py:855
  417.6 26.1 %all-to-all-start.12 = ((bf16[4,768,256]{2,1,0:T(8,128)(2,1)}), bf16[4,768,256]{2,1,0:T(8,128)(2,1)}, u32[]{:S(2)}, u32[]{:S(2)}) async-start(bf16[4,768,256]{2,1,0:T(8,128)(2,1)} %maximum_bitcast_fusion), calls=%async_computation.13 | async-start | bytes 3145728 | tf_op jit(solution)/shard_map/all_to_all | solution.py:859
  458.9 25.6 %collective-permute-start.38 = (bf16[256,1024]{1,0:T(8,128)(2,1)}, bf16[256,1024]{1,0:T(8,128)(2,1)}, u32[]{:S(2)}, u32[]{:S(2)}) collective-permute-start(bf16[256,1024]{1,0:T(8,128)(2,1)} %get-tuple-element.325), channel_id=1, source_target_pairs={{0,16},{8,24},{16,0},{24,8},{1,17},{9,25},{17,1},{25,9},{2,18},{10... | collective-permute-start | bytes 1572872 | tf_op jit(solution)/shard_map/ppermute | solution.py:855
  484.5 46.1 %collective-permute-start.41 = (bf16[4,4,3,128,256]{4,3,2,1,0:T(8,128)(2,1)}, bf16[4,4,3,128,256]{4,3,2,1,0:T(8,128)(2,1)}, u32[]{:S(2)}, u32[]{:S(2)}) collective-permute-start(bf16[4,4,3,128,256]{4,3,2,1,0:T(8,128)(2,1)} %get-tuple-element.240), channel_id=1, source_target_pairs={{0,1},{1,0},{2,3},{3,2},{4,5},{5,4},{6,7},{7,6},{8,9},{9,8},{10,11... | collective-permute-start | bytes 9437192 | tf_op jit(solution)/shard_map/ppermute | solution.py:855
  493.8 30.9 %all-to-all-start.14 = ((bf16[4,384,256]{2,1,0:T(8,128)(2,1)}), bf16[4,384,256]{2,1,0:T(8,128)(2,1)}, u32[]{:S(2)}, u32[]{:S(2)}) async-start(bf16[4,384,256]{2,1,0:T(8,128)(2,1)} %maximum_bitcast_fusion.1), calls=%async_computation.15 | async-start | bytes 1572864 | tf_op jit(solution)/shard_map/all_to_all | solution.py:859
  534.9 45.5 %collective-permute-start.42 = (bf16[4,3,128,256]{3,2,1,0:T(8,128)(2,1)}, bf16[4,3,128,256]{3,2,1,0:T(8,128)(2,1)}, u32[]{:S(2)}, u32[]{:S(2)}) collective-permute-start(bf16[4,3,128,256]{3,2,1,0:T(8,128)(2,1)} %get-tuple-element.323), channel_id=1, source_target_pairs={{0,8},{8,0},{16,24},{24,16},{1,9},{9,1},{17,25},{25,17},{2,10},{10... | collective-permute-start | bytes 2359304 | tf_op jit(solution)/shard_map/ppermute | solution.py:855
  536.4 44.0 %collective-permute-start.43 = (bf16[4,3,128,256]{3,2,1,0:T(8,128)(2,1)}, bf16[4,3,128,256]{3,2,1,0:T(8,128)(2,1)}, u32[]{:S(2)}, u32[]{:S(2)}) collective-permute-start(bf16[4,3,128,256]{3,2,1,0:T(8,128)(2,1)} %get-tuple-element.322), channel_id=1, source_target_pairs={{0,16},{8,24},{16,0},{24,8},{1,17},{9,25},{17,1},{25,9},{2,18},{10... | collective-permute-start | bytes 2359304 | tf_op jit(solution)/shard_map/ppermute | solution.py:855
  536.9 43.5 %collective-permute-start.44 = (bf16[4,3,128,256]{3,2,1,0:T(8,128)(2,1)}, bf16[4,3,128,256]{3,2,1,0:T(8,128)(2,1)}, u32[]{:S(2)}, u32[]{:S(2)}) collective-permute-start(bf16[4,3,128,256]{3,2,1,0:T(8,128)(2,1)} %get-tuple-element.321), channel_id=1, source_target_pairs={{0,24},{8,16},{16,8},{24,0},{1,25},{9,17},{17,9},{25,1},{2,26},{10... | collective-permute-start | bytes 2359304 | tf_op jit(solution)/shard_map/ppermute | solution.py:855
  541.2 35.4 %all-to-all-start.16 = ((bf16[4,64,1024]{2,1,0:T(8,128)(2,1)}), bf16[4,64,1024]{2,1,0:T(8,128)(2,1)S(1)}, u32[]{:S(2)}, u32[]{:S(2)}) async-start(bf16[4,64,1024]{2,1,0:T(8,128)(2,1)} %all-to-all-done.15), calls=%async_computation.17 | async-start | bytes 1048576 | tf_op jit(solution)/shard_map/all_to_all | solution.py:859
  589.3 37.5 %collective-permute-start.55 = (bf16[1024,256]{1,0:T(8,128)(2,1)}, bf16[1024,256]{1,0:T(8,128)(2,1)}, u32[]{:S(2)}, u32[]{:S(2)}) collective-permute-start(bf16[1024,256]{1,0:T(8,128)(2,1)} %get-tuple-element.334), channel_id=1, source_target_pairs={{0,4},{2,6},{4,0},{6,2},{1,5},{3,7},{5,1},{7,3},{8,12},{10,14},{12... | collective-permute-start | bytes 1572872 | tf_op jit(solution)/shard_map/ppermute | solution.py:855
  591.9 50.5 %collective-permute-start.56 = (bf16[1024,256]{1,0:T(8,128)(2,1)}, bf16[1024,256]{1,0:T(8,128)(2,1)}, u32[]{:S(2)}, u32[]{:S(2)}) collective-permute-start(bf16[1024,256]{1,0:T(8,128)(2,1)} %get-tuple-element.333), channel_id=1, source_target_pairs={{0,6},{2,4},{4,2},{6,0},{1,7},{3,5},{5,3},{7,1},{8,14},{10,12},{12... | collective-permute-start | bytes 1572872 | tf_op jit(solution)/shard_map/ppermute | solution.py:855
  603.9 43.6 %collective-permute-start.48 = (bf16[128,1024]{1,0:T(8,128)(2,1)}, bf16[128,1024]{1,0:T(8,128)(2,1)S(1)}, u32[]{:S(2)}, u32[]{:S(2)}) collective-permute-start(bf16[128,1024]{1,0:T(8,128)(2,1)} %fusion.20), channel_id=1, source_target_pairs={{0,0},{1,1},{2,8},{3,9},{4,16},{5,17},{6,24},{7,25},{8,2},{9,3},{1... | collective-permute-start | bytes 786440 | tf_op jit(solution)/shard_map/ppermute | solution.py:894
  (125 other events, 2060.4 us)
Sparse Core Ops, SparseCore 0:
  37.0 40.2 all-gather.2
  125.5 78.0 all-gather.4
  333.9 78.5 reduce-scatter.1
